TPU v7x, 512 devices: a whole 4x4x16 slice. The times are simulated.
512 devices in a mesh: slab: 128 (over z, y, core), col: 4 (over x).
Axes of the slice: x: 4, y: 4, z: 16, core: 2. Of those that a mesh axis runs over, the one named last changes fastest.
Arguments:
- stiff_tiles: float32 [4096, 3, 128, 128], P('slab'), as said below
- tile_mask: int32 [4096, 2], P('slab'), may hold values from 0 to 1, as said below
- edge_star: float32 [524288], P('slab'), may hold values from 0.5 to 2
- start_modes: float32 [16, 524288], P(None, 'slab'), may hold values from -6 to 6
- start_directions: float32 [16, 524288], P(None, 'slab'), may hold values from -6 to 6
Outputs:
- mode_block: float32 [16, 524288], P(None, 'slab')
- directions: float32 [16, 524288], P(None, 'slab')
- ritz: float32 [16, 16], replicated
Inputs may be any that keep to these rules, and one draw needn't show every extreme that they name: The assembled operator is symmetric and positive definite: stiff_tiles[b, 0] is the transpose of stiff_tiles[b - 1, 2] and stiff_tiles[b, 1] is symmetric. tile_mask[b, 0] equals tile_mask[b - 1, 1] for b of 1 and more.
All inputs are finite; a program needn't handle non-finite values.
Results may differ from a plain program's by a relative error of at most 0.0003.
Values sent between devices are 32-bit elements; how exact they have to be, the bound alone decides.
No kernel may reach another device: no remote copies, remote signals or barrier semaphores. Data moves between devices by JAX's collectives and lax.ppermute only.
A program may use at most 64 MiB of HBM per device.

v0:
```python
import jax
import jax.numpy as jnp
from jax import lax
from jax.experimental import pallas as pl
from jax.experimental.pallas import tpu as pltpu
from jax.sharding import Mesh
from jax.sharding import PartitionSpec as P

SLAB = ("z", "y", "core")
TILE = 128
STEP_BLOCKS = 4


def slab_sum(rows):
    parts = lax.axis_size(("y", "core"))
    shared = rows.reshape(parts, -1, 128)
    own = lax.all_to_all(shared, ("y", "core"), 0, 0, tiled=True).sum(0)
    copies = jnp.broadcast_to(own[None], (lax.axis_size("z"),) + own.shape)
    own = lax.all_to_all(copies, "z", 0, 0, tiled=True).sum(0)
    copies = jnp.broadcast_to(own[None], (parts,) + own.shape)
    return lax.all_to_all(copies, ("y", "core"), 0, 0, tiled=True).reshape(rows.shape)


def from_left(edge):
    count = lax.axis_size(SLAB)
    return lax.ppermute(edge, SLAB, [(i, i + 1) for i in range(count - 1)])


def from_right(edge):
    count = lax.axis_size(SLAB)
    return lax.ppermute(edge, SLAB, [(i + 1, i) for i in range(count - 1)])


def with_halo(block):
    low = from_left(block[:, -TILE:])
    high = from_right(block[:, :TILE])
    return jnp.concatenate([low, block, high], axis=1)


def split(values):
    high = values.astype(jnp.bfloat16)
    low = (values - high.astype(jnp.float32)).astype(jnp.bfloat16)
    return high, low


def band_kernel(mask_ref, tiles_ref, ext_ref, out_ref):
    step = pl.program_id(0)
    count = ext_ref.shape[0]
    start = pl.multiple_of(step * STEP_BLOCKS * TILE, TILE)
    window = ext_ref[:, pl.ds(start, (STEP_BLOCKS + 2) * TILE)]
    left = jnp.concatenate(split(window), axis=0)
    for k in range(STEP_BLOCKS):
        block = step * STEP_BLOCKS + k
        weight_low = mask_ref[block, 0].astype(jnp.float32)
        weight_high = mask_ref[block, 1].astype(jnp.float32)
        row = jnp.concatenate(
            [tiles_ref[k, 0] * weight_low, tiles_ref[k, 1], tiles_ref[k, 2] * weight_high], axis=1
        )
        right = jnp.concatenate(split(row), axis=0)
        term = lax.dot_general(
            left[:, k * TILE : (k + 3) * TILE],
            right,
            (((1,), (1,)), ((), ())),
            preferred_element_type=jnp.float32,
        )
        term = term[:, :TILE] + term[:, TILE:]
        out_ref[:, k * TILE : (k + 1) * TILE] = term[:count] + term[count:]


def band(extended, tile_set, coupling):
    count, width = extended.shape
    width -= 2 * TILE
    return pl.pallas_call(
        band_kernel,
        grid=(width // (STEP_BLOCKS * TILE),),
        in_specs=[
            pl.BlockSpec(memory_space=pltpu.SMEM),
            pl.BlockSpec((STEP_BLOCKS, 3, TILE, TILE), lambda i: (i, 0, 0, 0)),
            pl.BlockSpec((count, width + 2 * TILE), lambda i: (0, 0)),
        ],
        out_specs=pl.BlockSpec((count, STEP_BLOCKS * TILE), lambda i: (0, i)),
        out_shape=jax.ShapeDtypeStruct((count, width), jnp.float32),
        compiler_params=pltpu.CompilerParams(vmem_limit_bytes=32 * 1024 * 1024),
        name="band",
    )(coupling, tile_set, extended)


def gram(left, right):
    return lax.dot_general(
        left,
        right,
        (((1,), (1,)), ((), ())),
        precision=lax.Precision.HIGHEST,
        preferred_element_type=jnp.float32,
    )


def product(left, right):
    return jnp.dot(left, right, precision=lax.Precision.HIGHEST, preferred_element_type=jnp.float32)


def symmetric(matrix):
    return 0.5 * (matrix + matrix.T)


def congruence(coeffs, matrix):
    return symmetric(product(coeffs, gram(matrix, coeffs)))


def rayleigh_ritz(gram_stiff, gram_mass, total_rows, mode_count):
    shifted = gram_stiff + 1.0 * gram_mass
    factor = jnp.linalg.cholesky(shifted)
    coeffs = jax.scipy.linalg.cho_solve((factor, True), gram_mass[:, :mode_count])
    normalizer = product(coeffs.T, product(gram_mass, coeffs)) / total_rows
    chol_factor = jnp.linalg.cholesky(normalizer)
    rotation = jax.scipy.linalg.solve_triangular(chol_factor, coeffs.T, lower=True)
    ritz_matrix = product(rotation, product(gram_stiff, rotation.T)) / total_rows
    return (rotation, ritz_matrix)


def first_coefficients(gram_stiff, gram_mass, total_rows, m):
    eye = jnp.eye(m, dtype=jnp.float32)
    none = jnp.zeros((m, m), jnp.float32)
    chol_factor = jnp.linalg.cholesky(gram_mass[:m, :m] / total_rows)
    start = jax.scipy.linalg.solve_triangular(chol_factor, eye, lower=True)
    ritz_matrix = product(start, product(gram_stiff[:m, :m], start.T)) / total_rows
    basis = jnp.concatenate(
        [
            jnp.concatenate([start, none, none, none], axis=1),
            jnp.concatenate([none, start, -product(ritz_matrix, start), none], axis=1),
            jnp.concatenate([none, none, none, eye], axis=1),
        ]
    )
    rotation, ritz_matrix = rayleigh_ritz(
        congruence(basis, gram_stiff), congruence(basis, gram_mass), total_rows, m
    )
    modes = product(rotation, basis)
    directions = product(rotation[:, m:], basis[m:])
    return jnp.concatenate([modes, directions]), ritz_matrix


def last_coefficients(gram_stiff, gram_mass, ritz_matrix, total_rows, m):
    none = jnp.zeros((m, m), jnp.float32)
    rotation, next_ritz = rayleigh_ritz(
        gram_stiff[: 3 * m, : 3 * m], gram_mass[: 3 * m, : 3 * m], total_rows, m
    )
    of_x, of_r, of_p = rotation[:, :m], rotation[:, m : 2 * m], rotation[:, 2 * m :]
    pulled = product(next_ritz, rotation)
    zeros5 = jnp.zeros((m, 5 * m), jnp.float32)
    basis = jnp.concatenate(
        [
            jnp.concatenate([rotation, zeros5], axis=1),
            jnp.concatenate(
                [
                    none,
                    of_x,
                    none,
                    of_r,
                    of_p,
                    product(of_x, ritz_matrix) - pulled[:, :m],
                    -pulled[:, m:],
                ],
                axis=1,
            ),
            jnp.concatenate([none, of_r, of_p, zeros5], axis=1),
        ]
    )
    rotation, last_ritz = rayleigh_ritz(
        congruence(basis, gram_stiff), congruence(basis, gram_mass), total_rows, m
    )
    modes = product(rotation, basis)
    directions = product(rotation[:, m:], basis[m:])
    return jnp.concatenate([modes, directions]), last_ritz


def packed(gram_stiff, gram_mass):
    size = gram_stiff.shape[0]
    low = jnp.tril(jnp.ones((size, size), bool), -1)
    both = jnp.where(low, gram_stiff, gram_mass)
    return jnp.concatenate([both, jnp.broadcast_to(jnp.diagonal(gram_stiff)[None], (8, size))])


def unpacked(rows):
    size = rows.shape[1]
    both, diagonal = rows[:size], rows[size]
    low = jnp.tril(both, -1)
    high = jnp.triu(both, 1)
    return low + low.T + jnp.diag(diagonal), high + high.T + jnp.diag(jnp.diagonal(both))


def on_device(stiff_tiles, tile_mask, edge_star, start_modes, start_directions):
    m = start_modes.shape[0]
    total_rows = edge_star.shape[0] * lax.axis_size(SLAB)
    star = edge_star[None, :]
    fields = jnp.concatenate(
        [start_modes, start_directions, start_modes * star, jnp.broadcast_to(star, (8, star.shape[1]))]
    )
    fields = with_halo(fields)
    modes, directions, mass_modes = fields[:m], fields[m : 2 * m], fields[2 * m : 3 * m]
    star_ext = fields[3 * m : 3 * m + 1]
    applied = band(fields[: 3 * m], stiff_tiles, tile_mask)
    applied_modes = with_halo(applied[:m])
    twice = band(applied_modes, stiff_tiles, tile_mask)

    basis = jnp.concatenate([modes, applied_modes, mass_modes, directions])
    own = basis[:, TILE:-TILE]
    rest = jnp.concatenate([twice, applied[2 * m : 3 * m], applied[m : 2 * m]])
    applied_own = jnp.concatenate([applied[:m], rest])
    gram_stiff = gram(own, applied_own)
    gram_mass = gram(own, own * star)
    sums = slab_sum(jnp.concatenate([symmetric(gram_stiff), symmetric(gram_mass)], axis=1))
    applied_basis = jnp.concatenate([applied_modes, with_halo(rest)])
    size = 4 * m
    coeffs, ritz_matrix = first_coefficients(sums[:, :size], sums[:, size:], total_rows, m)

    pair = product(coeffs, basis)
    applied_pair = product(coeffs, applied_basis)
    modes, directions = pair[:m], pair[m:]
    mass_modes = modes * star_ext
    residual = applied_pair[:m] - product(ritz_matrix, mass_modes)
    fields = jnp.concatenate(
        [residual, applied_pair[m:], mass_modes, residual * star_ext, directions * star_ext]
    )
    applied = band(fields, stiff_tiles, tile_mask)
    applied_residual = applied[:m]
    twice = band(with_halo(applied_residual), stiff_tiles, tile_mask)
    inner = slice(TILE, -TILE)
    own = jnp.concatenate(
        [
            modes[:, inner],
            residual[:, inner],
            directions[:, inner],
            applied_residual,
            fields[m:, inner],
        ]
    )
    applied_own = jnp.concatenate(
        [applied_pair[:m, inner], applied_residual, applied_pair[m:, inner], twice, applied[m:]]
    )
    gram_stiff = symmetric(gram(own, applied_own))
    gram_mass = symmetric(gram(own, own * star))
    gram_stiff, gram_mass = unpacked(slab_sum(packed(gram_stiff, gram_mass)))
    coeffs, ritz_matrix = last_coefficients(gram_stiff, gram_mass, ritz_matrix, total_rows, m)
    result = product(coeffs, own)
    return (result[:m], result[m:], ritz_matrix)


def solution(mesh):
    fine = Mesh(mesh.devices.reshape(-1, 4, 2, 4), ("z", "y", "core", "x"))
    in_specs = (
        P(SLAB, None, None, None),
        P(SLAB, None),
        P(SLAB),
        P(None, SLAB),
        P(None, SLAB),
    )
    out_specs = (P(None, SLAB), P(None, SLAB), P())
    return jax.shard_map(
        on_device, mesh=fine, in_specs=in_specs, out_specs=out_specs, check_vma=False
    )
```

profile of v0, /device:TPU:1, one launch (start us, length us, event | category | flops | bytes accessed | tf_op | source)
XLA Modules:
  0.0 216.4 jit_solution(3222065842227264730)
XLA Ops:
  0.6 1.0 broadcast_multiply_fusion.1
  1.6 0.7 broadcast_in_dim.81
  2.3 0.8 pad_maximum_fusion.13
  3.1 4.6 %collective-permute-start = (f32[56,128]{1,0:T(8,128)S(1)}, f32[56,128]{1,0:T(8,128)S(1)}, u32[]{:S(2)}, u32[]{:S(2)}) collective-permute-start(f32[56,128]{1,0:T(8,128)S(1)} %get-tuple-element.39), channel_id=1, source_target_pairs={{0,4},{4,8},{8,12},{12,16},{16,20},{20,24},{24,28},{28,32},{32,36}... | collective-permute-start | bytes 86024 | tf_op jit(solution)/shard_map/ppermute | solution.py:26
  7.7 5.5 %collective-permute-start.1 = (f32[56,128]{1,0:T(8,128)S(1)}, f32[56,128]{1,0:T(8,128)S(1)}, u32[]{:S(2)}, u32[]{:S(2)}) collective-permute-start(f32[56,128]{1,0:T(8,128)S(1)} %get-tuple-element.40), channel_id=1, source_target_pairs={{4,0},{8,4},{12,8},{16,12},{20,16},{24,20},{28,24},{32,28},{36,32}... | collective-permute-start | bytes 86024 | tf_op jit(solution)/shard_map/ppermute | solution.py:31
  13.2 0.8 copy.97.mask_ref
  14.0 1.1 pad_maximum_fusion.4
  15.3 2.8 %copy-done = f32[32,3,128,128]{3,2,1,0:T(8,128)S(1)} copy-done((f32[32,3,128,128]{3,2,1,0:T(8,128)S(1)}, f32[32,3,128,128]{3,2,1,0:T(8,128)}, u32[]{:S(2)}) %copy-start) | copy-done | bytes 6291480
  18.0 4.1 %band.4 = f32[48,4096]{1,0:T(8,128)S(1)} custom-call(s32[32,2]{1,0:T(8,128)S(1)} %copy.97.mask_ref, f32[32,3,128,128]{3,2,1,0:T(8,128)S(1)} %copy-done, f32[48,4352]{1,0:T(8,128)S(1)} %slice.241.ext_ref), custom_call_target="tpu_custom_call" | custom-call | tf_op jit(solution)/shard_map/band/pallas_call | solution.py:73
  22.1 1.9 collective-permute-start.2
  24.1 2.4 %collective-permute-start.3 = (f32[16,128]{1,0:T(8,128)S(1)}, f32[16,128]{1,0:T(8,128)S(1)}, u32[]{:S(2)}, u32[]{:S(2)}) collective-permute-start(f32[16,128]{1,0:T(8,128)S(1)} %get-tuple-element.47), channel_id=1, source_target_pairs={{4,0},{8,4},{12,8},{16,12},{20,16},{24,20},{28,24},{32,28},{36,32}... | collective-permute-start | bytes 24584 | tf_op jit(solution)/shard_map/ppermute | solution.py:31
  26.6 2.5 %collective-permute-done.3 = f32[16,128]{1,0:T(8,128)S(1)} collective-permute-done((f32[16,128]{1,0:T(8,128)S(1)}, f32[16,128]{1,0:T(8,128)S(1)}, u32[]{:S(2)}, u32[]{:S(2)}) %collective-permute-start.3) | collective-permute-done | bytes 8224 | tf_op jit(solution)/shard_map/ppermute | solution.py:31
  29.1 3.9 %band.5 = f32[16,4096]{1,0:T(8,128)S(1)} custom-call(s32[32,2]{1,0:T(8,128)S(1)} %copy.97.mask_ref, f32[32,3,128,128]{3,2,1,0:T(8,128)S(1)} %copy-done, f32[16,4352]{1,0:T(8,128)S(1)} %pad_maximum_fusion.7.ext_ref), custom_call_target="tpu_custom_call" | custom-call | tf_op jit(solution)/shard_map/band/pallas_call | solution.py:73
  33.0 1.0 fusion.33
  34.1 1.0 fusion.2
  35.2 0.7 maximum_bitcast_fusion
  35.9 7.5 %all-to-all-start = ((f32[8,8,128]{2,1,0:T(8,128)}), f32[8,8,128]{2,1,0:T(8,128)S(1)}, u32[]{:S(2)}, u32[]{:S(2)}) async-start(f32[8,8,128]{2,1,0:T(8,128)} %maximum_bitcast_fusion), calls=%async_computation | async-start | bytes 65536 | tf_op jit(solution)/shard_map/all_to_all | solution.py:17
  43.4 4.7 %all-to-all-done = f32[8,8,128]{2,1,0:T(8,128)S(1)} async-done(((f32[8,8,128]{2,1,0:T(8,128)}), f32[8,8,128]{2,1,0:T(8,128)S(1)}, u32[]{:S(2)}, u32[]{:S(2)}) %all-to-all-start) | async-done | bytes 32800 | tf_op jit(solution)/shard_map/all_to_all | solution.py:17
  48.7 16.0 %all-to-all-start.1 = ((f32[16,8,128]{2,1,0:T(8,128)}), f32[16,8,128]{2,1,0:T(8,128)S(1)}, u32[]{:S(2)}, u32[]{:S(2)}) async-start(f32[16,8,128]{2,1,0:T(8,128)} %broadcast_in_dim.82), calls=%async_computation.1 | async-start | bytes 131072 | tf_op jit(solution)/shard_map/all_to_all | solution.py:19
  64.9 11.4 %all-to-all-done.1 = f32[16,8,128]{2,1,0:T(8,128)S(1)} async-done(((f32[16,8,128]{2,1,0:T(8,128)}), f32[16,8,128]{2,1,0:T(8,128)S(1)}, u32[]{:S(2)}, u32[]{:S(2)}) %all-to-all-start.1) | async-done | bytes 65568 | tf_op jit(solution)/shard_map/all_to_all | solution.py:19
  76.9 5.4 %all-to-all-start.2 = ((f32[8,8,128]{2,1,0:T(8,128)}), f32[8,8,128]{2,1,0:T(8,128)S(1)}, u32[]{:S(2)}, u32[]{:S(2)}) async-start(f32[8,8,128]{2,1,0:T(8,128)} %broadcast_in_dim.83), calls=%async_computation.2 | async-start | bytes 65536 | tf_op jit(solution)/shard_map/all_to_all | solution.py:21
  82.3 3.5 %collective-permute-start.4 = (f32[48,128]{1,0:T(8,128)S(1)}, f32[48,128]{1,0:T(8,128)S(1)}, u32[]{:S(2)}, u32[]{:S(2)}) collective-permute-start(f32[48,128]{1,0:T(8,128)S(1)} %get-tuple-element.41), channel_id=1, source_target_pairs={{0,4},{4,8},{8,12},{12,16},{16,20},{20,24},{24,28},{28,32},{32,36}... | collective-permute-start | bytes 73736 | tf_op jit(solution)/shard_map/ppermute | solution.py:26
  85.9 1.9 collective-permute-start.5
  88.1 1.5 cholesky.131
  90.2 0.6 fusion.116
  90.9 1.2 custom-call.16
  94.1 4.4 %cholesky.142 = f32[48,48]{1,0:T(8,128)S(1)} custom-call(f32[48,48]{1,0:T(8,128)S(1)} %fusion.77), custom_call_target="Cholesky" | custom-call | tf_op jit(solution)/shard_map/jit(cholesky)/cholesky | solution.py:112
  99.1 0.7 fusion.56
  99.8 3.7 %custom-call.25 = f32[1,48,48]{1,2,0:T(8,128)S(1)} custom-call(f32[1,48,48]{2,1,0:T(8,128)S(1)} %fusion.56), custom_call_target="InvertDiagBlocksLowerTriangular" | custom-call | tf_op jit(solution)/shard_map/jit(_cho_solve)/triangular_solve | solution.py:113
  104.2 1.5 cholesky.153
  106.3 0.6 fusion.117
  107.0 1.2 custom-call.26
  109.0 0.7 fusion.4
  109.9 0.7 fusion.16
  111.3 0.8 slice-done.1
  112.1 4.5 %band.6 = f32[80,4096]{1,0:T(8,128)S(1)} custom-call(s32[32,2]{1,0:T(8,128)S(1)} %copy.97.mask_ref, f32[32,3,128,128]{3,2,1,0:T(8,128)S(1)} %bitcast.183, f32[80,4352]{1,0:T(8,128)S(1)} %get-tuple-element.23.ext_ref), custom_call_target="tpu_custom_call" | custom-call | tf_op jit(solution)/shard_map/band/pallas_call | solution.py:73
  117.2 3.6 %collective-permute-start.6 = (f32[16,128]{1,0:T(8,128)}, f32[16,128]{1,0:T(8,128)S(1)}, u32[]{:S(2)}, u32[]{:S(2)}) collective-permute-start(f32[16,128]{1,0:T(8,128)} %get-tuple-element.31), channel_id=1, source_target_pairs={{0,4},{4,8},{8,12},{12,16},{16,20},{20,24},{24,28},{28,32},{32,36}... | collective-permute-start | bytes 24584 | tf_op jit(solution)/shard_map/ppermute | solution.py:26
  120.8 2.1 collective-permute-start.7
  122.9 0.8 fusion.180
  123.8 1.3 copy-done.3
  125.1 1.9 fusion
  127.0 0.7 copy.113
  127.7 1.0 pad_maximum_fusion.8.ext_ref
  128.7 2.8 %copy-done.1 = f32[32,3,128,128]{3,2,1,0:T(8,128)S(1)} copy-done((f32[32,3,128,128]{3,2,1,0:T(8,128)S(1)}, f32[32,3,128,128]{3,2,1,0:T(8,128)}, u32[]{:S(2)}) %copy-start.1) | copy-done | bytes 6291480
  131.5 3.9 %band.7 = f32[16,4096]{1,0:T(8,128)S(1)} custom-call(s32[32,2]{1,0:T(8,128)S(1)} %copy.97.mask_ref, f32[32,3,128,128]{3,2,1,0:T(8,128)S(1)} %copy-done.1, f32[16,4352]{1,0:T(8,128)S(1)} %pad_maximum_fusion.8.ext_ref), custom_call_target="tpu_custom_call" | custom-call | tf_op jit(solution)/shard_map/band/pallas_call | solution.py:73
  135.5 1.8 fusion.187
  137.4 1.3 gather_fusion
  138.9 10.0 %all_to_all.30 = f32[8,17,128]{2,1,0:T(8,128)S(1)} all-to-all(f32[8,17,128]{2,1,0:T(8,128)S(1)} %reshape.51), channel_id=1, replica_groups=mesh['z'=16,'y'=4,'core'=2,'x'=4] {'y','core'}, dimensions={0} | all-to-all | bytes 139264 | tf_op jit(solution)/shard_map/all_to_all | solution.py:17
  149.0 19.1 %all_to_all.31 = f32[16,17,128]{2,1,0:T(8,128)S(1)} all-to-all(f32[16,17,128]{2,1,0:T(8,128)S(1)} %broadcast_in_dim.85), channel_id=1, replica_groups=mesh['z'=16,'y'=4,'core'=2,'x'=4] {'z'}, dimensions={0} | all-to-all | bytes 278528 | tf_op jit(solution)/shard_map/all_to_all | solution.py:19
  168.1 12.4 %all_to_all.32 = f32[8,17,128]{2,1,0:T(8,128)S(1)} all-to-all(f32[8,17,128]{2,1,0:T(8,128)S(1)} %broadcast_in_dim.86), channel_id=1, replica_groups=mesh['z'=16,'y'=4,'core'=2,'x'=4] {'y','core'}, dimensions={0} | all-to-all | bytes 139264 | tf_op jit(solution)/shard_map/all_to_all | solution.py:21
  180.6 1.3 gather_fusion.1
  182.3 4.4 %cholesky.164 = f32[48,48]{1,0:T(8,128)S(1)} custom-call(f32[48,48]{1,0:T(8,128)S(1)} %fusion.72), custom_call_target="Cholesky" | custom-call | tf_op jit(solution)/shard_map/jit(cholesky)/cholesky | solution.py:112
  187.3 0.7 fusion.57
  188.0 3.7 %custom-call.27 = f32[1,48,48]{1,2,0:T(8,128)S(1)} custom-call(f32[1,48,48]{2,1,0:T(8,128)S(1)} %fusion.57), custom_call_target="InvertDiagBlocksLowerTriangular" | custom-call | tf_op jit(solution)/shard_map/jit(_cho_solve)/triangular_solve | solution.py:113
  192.4 1.5 cholesky.175
  195.2 1.2 custom-call.28
  198.7 4.4 %cholesky.186 = f32[48,48]{1,0:T(8,128)S(1)} custom-call(f32[48,48]{1,0:T(8,128)S(1)} %fusion.65), custom_call_target="Cholesky" | custom-call | tf_op jit(solution)/shard_map/jit(cholesky)/cholesky | solution.py:112
  203.7 0.7 fusion.58
  204.4 3.7 %custom-call.29 = f32[1,48,48]{1,2,0:T(8,128)S(1)} custom-call(f32[1,48,48]{2,1,0:T(8,128)S(1)} %fusion.58), custom_call_target="InvertDiagBlocksLowerTriangular" | custom-call | tf_op jit(solution)/shard_map/jit(_cho_solve)/triangular_solve | solution.py:113
  208.7 1.5 cholesky.197
  211.5 1.2 custom-call.30
  213.7 0.7 copy.129
  214.4 1.2 fusion.106
  215.6 0.8 fusion.185
  (169 shorter events, 18.4 us)
Async XLA Ops:
  3.1 10.8 %collective-permute-start = (f32[56,128]{1,0:T(8,128)S(1)}, f32[56,128]{1,0:T(8,128)S(1)}, u32[]{:S(2)}, u32[]{:S(2)}) collective-permute-start(f32[56,128]{1,0:T(8,128)S(1)} %get-tuple-element.39), channel_id=1, source_target_pairs={{0,4},{4,8},{8,12},{12,16},{16,20},{20,24},{24,28},{28,32},{32,36}... | collective-permute-start | bytes 86024 | tf_op jit(solution)/shard_map/ppermute | solution.py:26
  7.7 6.3 %collective-permute-start.1 = (f32[56,128]{1,0:T(8,128)S(1)}, f32[56,128]{1,0:T(8,128)S(1)}, u32[]{:S(2)}, u32[]{:S(2)}) collective-permute-start(f32[56,128]{1,0:T(8,128)S(1)} %get-tuple-element.40), channel_id=1, source_target_pairs={{4,0},{8,4},{12,8},{16,12},{20,16},{24,20},{28,24},{32,28},{36,32}... | collective-permute-start | bytes 86024 | tf_op jit(solution)/shard_map/ppermute | solution.py:31
  15.2 2.8 %copy-start = (f32[32,3,128,128]{3,2,1,0:T(8,128)S(1)}, f32[32,3,128,128]{3,2,1,0:T(8,128)}, u32[]{:S(2)}) copy-start(f32[32,3,128,128]{3,2,1,0:T(8,128)} %tiles_ref.7) | copy-start | bytes 18874372
  22.1 4.4 %collective-permute-start.2 = (f32[16,128]{1,0:T(8,128)S(1)}, f32[16,128]{1,0:T(8,128)S(1)}, u32[]{:S(2)}, u32[]{:S(2)}) collective-permute-start(f32[16,128]{1,0:T(8,128)S(1)} %get-tuple-element.46), channel_id=1, source_target_pairs={{0,4},{4,8},{8,12},{12,16},{16,20},{20,24},{24,28},{28,32},{32,36}... | collective-permute-start | bytes 24584 | tf_op jit(solution)/shard_map/ppermute | solution.py:26
  24.1 5.0 %collective-permute-start.3 = (f32[16,128]{1,0:T(8,128)S(1)}, f32[16,128]{1,0:T(8,128)S(1)}, u32[]{:S(2)}, u32[]{:S(2)}) collective-permute-start(f32[16,128]{1,0:T(8,128)S(1)} %get-tuple-element.47), channel_id=1, source_target_pairs={{4,0},{8,4},{12,8},{16,12},{20,16},{24,20},{28,24},{32,28},{36,32}... | collective-permute-start | bytes 24584 | tf_op jit(solution)/shard_map/ppermute | solution.py:31
  26.5 55.8 %copy-start.6 = (f32[16,4096]{1,0:T(8,128)}, f32[16,4096]{1,0:T(8,128)S(1)}, u32[]{:S(2)}) copy-start(f32[16,4096]{1,0:T(8,128)S(1)} %get-tuple-element.43) | copy-start | bytes 786436
  26.5 55.8 %copy-start.8 = (f32[16,4096]{1,0:T(8,128)}, f32[16,4096]{1,0:T(8,128)S(1)}, u32[]{:S(2)}) copy-start(f32[16,4096]{1,0:T(8,128)S(1)} %get-tuple-element.44) | copy-start | bytes 786436
  33.0 1.1 copy-start.11
  34.1 30.8 %copy-start.2 = (f32[16,4096]{1,0:T(8,128)S(1)}, f32[16,4096]{1,0:T(8,128)}, u32[]{:S(2)}) copy-start(f32[16,4096]{1,0:T(8,128)} %param.14) | copy-start | bytes 786436
  34.1 30.7 %copy-start.5 = (f32[16,4096]{1,0:T(8,128)S(1)}, f32[16,4096]{1,0:T(8,128)}, u32[]{:S(2)}) copy-start(f32[16,4096]{1,0:T(8,128)} %param.15) | copy-start | bytes 786436
  35.9 12.2 %all-to-all-start = ((f32[8,8,128]{2,1,0:T(8,128)}), f32[8,8,128]{2,1,0:T(8,128)S(1)}, u32[]{:S(2)}, u32[]{:S(2)}) async-start(f32[8,8,128]{2,1,0:T(8,128)} %maximum_bitcast_fusion), calls=%async_computation | async-start | bytes 65536 | tf_op jit(solution)/shard_map/all_to_all | solution.py:17
  48.7 27.6 %all-to-all-start.1 = ((f32[16,8,128]{2,1,0:T(8,128)}), f32[16,8,128]{2,1,0:T(8,128)S(1)}, u32[]{:S(2)}, u32[]{:S(2)}) async-start(f32[16,8,128]{2,1,0:T(8,128)} %broadcast_in_dim.82), calls=%async_computation.1 | async-start | bytes 131072 | tf_op jit(solution)/shard_map/all_to_all | solution.py:19
  76.9 10.9 %all-to-all-start.2 = ((f32[8,8,128]{2,1,0:T(8,128)}), f32[8,8,128]{2,1,0:T(8,128)S(1)}, u32[]{:S(2)}, u32[]{:S(2)}) async-start(f32[8,8,128]{2,1,0:T(8,128)} %broadcast_in_dim.83), calls=%async_computation.2 | async-start | bytes 65536 | tf_op jit(solution)/shard_map/all_to_all | solution.py:21
  82.3 27.5 %collective-permute-start.4 = (f32[48,128]{1,0:T(8,128)S(1)}, f32[48,128]{1,0:T(8,128)S(1)}, u32[]{:S(2)}, u32[]{:S(2)}) collective-permute-start(f32[48,128]{1,0:T(8,128)S(1)} %get-tuple-element.41), channel_id=1, source_target_pairs={{0,4},{4,8},{8,12},{12,16},{16,20},{20,24},{24,28},{28,32},{32,36}... | collective-permute-start | bytes 73736 | tf_op jit(solution)/shard_map/ppermute | solution.py:26
  85.9 24.0 %collective-permute-start.5 = (f32[48,128]{1,0:T(8,128)S(1)}, f32[48,128]{1,0:T(8,128)S(1)}, u32[]{:S(2)}, u32[]{:S(2)}) collective-permute-start(f32[48,128]{1,0:T(8,128)S(1)} %get-tuple-element.42), channel_id=1, source_target_pairs={{4,0},{8,4},{12,8},{16,12},{20,16},{24,20},{28,24},{32,28},{36,32}... | collective-permute-start | bytes 73736 | tf_op jit(solution)/shard_map/ppermute | solution.py:31
  108.6 1.3 copy-start.7
  108.6 1.3 copy-start.9
  109.0 2.3 %slice-start = ((s8[6291456]{0:T(1024)(128)(4,1)}), s8[4194304]{0:T(1024)(128)(4,1)S(1)}, s32[]{:S(2)}) async-start(s8[6291456]{0:T(1024)(128)(4,1)} %bitcast.182), calls=%async_computation.6 | async-start | bytes 8388608
  109.8 2.2 %slice-start.1 = ((s8[6291456]{0:T(1024)(128)(4,1)}), s8[2097152]{0:T(1024)(128)(4,1)S(1)}, s32[]{:S(2)}) async-start(s8[6291456]{0:T(1024)(128)(4,1)} %bitcast.182), calls=%async_computation.7 | async-start | bytes 4194304
  117.2 10.5 %collective-permute-start.6 = (f32[16,128]{1,0:T(8,128)}, f32[16,128]{1,0:T(8,128)S(1)}, u32[]{:S(2)}, u32[]{:S(2)}) collective-permute-start(f32[16,128]{1,0:T(8,128)} %get-tuple-element.31), channel_id=1, source_target_pairs={{0,4},{4,8},{8,12},{12,16},{16,20},{20,24},{24,28},{28,32},{32,36}... | collective-permute-start | bytes 24584 | tf_op jit(solution)/shard_map/ppermute | solution.py:26
  120.8 6.9 %collective-permute-start.7 = (f32[16,128]{1,0:T(8,128)S(1)}, f32[16,128]{1,0:T(8,128)S(1)}, u32[]{:S(2)}, u32[]{:S(2)}) collective-permute-start(f32[16,128]{1,0:T(8,128)S(1)} %get-tuple-element.32), channel_id=1, source_target_pairs={{4,0},{8,4},{12,8},{16,12},{20,16},{24,20},{28,24},{32,28},{36,32}... | collective-permute-start | bytes 24584 | tf_op jit(solution)/shard_map/ppermute | solution.py:31
  123.7 1.4 copy-start.3
  128.7 2.8 %copy-start.1 = (f32[32,3,128,128]{3,2,1,0:T(8,128)S(1)}, f32[32,3,128,128]{3,2,1,0:T(8,128)}, u32[]{:S(2)}) copy-start(f32[32,3,128,128]{3,2,1,0:T(8,128)} %tiles_ref.7) | copy-start | bytes 18874372
  131.5 3.9 %copy-start.4 = (f32[128,4096]{1,0:T(8,128)S(1)}, f32[128,4096]{1,0:T(8,128)}, u32[]{:S(2)}) copy-start(f32[128,4096]{1,0:T(8,128)} %copy-done.3) | copy-start | bytes 6291460
  135.4 2.0 copy-start.10
where the time goes:
time: 217 us; the launch traced here: 216 us
  starting transfers between devices  54.5 us (25%)
  other arithmetic  49.4 us (23%)
  blocking collectives  41.5 us (19%)
  local copies, waits for them, and re-layouts  18.8 us (9%)
  waiting for transfers between devices  18.7 us (9%)
  Pallas kernels  16.3 us (8%)
  matrix products  15.7 us (7%)
    all_to_all x1, blocking collectives, slab_sum(): own = lax.all_to_all(copies, 'z', 0, 0, tiled=True).sum(0)  19.1 us
    pallas_call x4, Pallas kernels, band(): pl.pallas_call(band_kernel, grid=(width // (STEP_BLOCKS * TILE),), in_spe...  16.3 us
    all_to_all x1, starting transfers between devices, slab_sum(): own = lax.all_to_all(copies, 'z', 0, 0, tiled=True).sum(0)  16 us
    another operation x9, other arithmetic, rayleigh_ritz(): factor = jnp.linalg.cholesky(shifted)  15.2 us
    ppermute x4, starting transfers between devices, from_left(): return lax.ppermute(edge, SLAB, [(i, i + 1) for i in range(count - 1)])  13.7 us
    another operation x6, other arithmetic, rayleigh_ritz(): jax.scipy.linalg.cho_solve((factor, True), gram_mass[:, :mode_count])  13 us
    all_to_all x1, blocking collectives, slab_sum(): lax.all_to_all(copies, ('y', 'core'), 0, 0, tiled=True).reshape(rows.shape)  12.4 us
    ppermute x4, starting transfers between devices, from_right(): return lax.ppermute(edge, SLAB, [(i + 1, i) for i in range(count - 1)])  11.9 us
  transfers between devices with their start and end apart: 11, of which 4 were waited for; matrix products, arithmetic and copies ran while one was open for 12% of the time, Pallas kernels for 0%

commit v1 on v0

--- a/solution.py
+++ b/solution.py
@@ -1,3 +1,5 @@
+import functools
+
 import jax
 import jax.numpy as jnp
 from jax import lax
@@ -9,6 +11,7 @@
 SLAB = ("z", "y", "core")
 TILE = 128
 STEP_BLOCKS = 4
+WIDTH = 4
 
 
 def slab_sum(rows):
@@ -103,74 +106,179 @@
     return 0.5 * (matrix + matrix.T)
 
 
-def congruence(coeffs, matrix):
-    return symmetric(product(coeffs, gram(matrix, coeffs)))
-
-
-def rayleigh_ritz(gram_stiff, gram_mass, total_rows, mode_count):
-    shifted = gram_stiff + 1.0 * gram_mass
-    factor = jnp.linalg.cholesky(shifted)
-    coeffs = jax.scipy.linalg.cho_solve((factor, True), gram_mass[:, :mode_count])
-    normalizer = product(coeffs.T, product(gram_mass, coeffs)) / total_rows
-    chol_factor = jnp.linalg.cholesky(normalizer)
-    rotation = jax.scipy.linalg.solve_triangular(chol_factor, coeffs.T, lower=True)
-    ritz_matrix = product(rotation, product(gram_stiff, rotation.T)) / total_rows
-    return (rotation, ritz_matrix)
-
-
-def first_coefficients(gram_stiff, gram_mass, total_rows, m):
-    eye = jnp.eye(m, dtype=jnp.float32)
-    none = jnp.zeros((m, m), jnp.float32)
-    chol_factor = jnp.linalg.cholesky(gram_mass[:m, :m] / total_rows)
-    start = jax.scipy.linalg.solve_triangular(chol_factor, eye, lower=True)
-    ritz_matrix = product(start, product(gram_stiff[:m, :m], start.T)) / total_rows
-    basis = jnp.concatenate(
-        [
-            jnp.concatenate([start, none, none, none], axis=1),
-            jnp.concatenate([none, start, -product(ritz_matrix, start), none], axis=1),
-            jnp.concatenate([none, none, none, eye], axis=1),
-        ]
-    )
+def nn(left, right):
+    return jnp.dot(left, right, precision=lax.Precision.HIGHEST, preferred_element_type=jnp.float32)
+
+
+def nt(left, right):
+    return gram(left, right)
+
+
+def lanes(rows):
+    return lax.broadcasted_iota(jnp.int32, (rows, 128), 1)
+
+
+def sublanes(rows):
+    return lax.broadcasted_iota(jnp.int32, (rows, 128), 0)
+
+
+def diagonal(rows, shift):
+    return jnp.where(lanes(rows) == sublanes(rows) + shift, 1.0, 0.0).astype(jnp.float32)
+
+
+def below(matrix, limit):
+    return jnp.where(lanes(matrix.shape[0]) < limit, matrix, 0.0)
+
+
+def pivots(groups, first, lane, width):
+    columns = [
+        [jnp.broadcast_to(g[:, lane + j : lane + j + 1], (8, 128)) for g in groups]
+        for j in range(width)
+    ]
+
+    def spread(values, row):
+        return jnp.broadcast_to(values[row // 8][row % 8 : row % 8 + 1], (8, 128))
+
+    block = [[spread(columns[j], first + i) for j in range(width)] for i in range(width)]
+    rows = [spread(groups, first + i) for i in range(width)]
+    return columns, block, rows
+
+
+def solved(block, rows):
+    width = len(rows)
+    block, rows = [list(r) for r in block], list(rows)
+    for i in range(width):
+        scale = 1.0 / block[i][i]
+        block[i] = [v * scale for v in block[i]]
+        rows[i] = rows[i] * scale
+        for k in range(width):
+            if k != i:
+                factor = block[k][i]
+                for j in range(i + 1, width):
+                    block[k][j] = block[k][j] - factor * block[i][j]
+                rows[k] = rows[k] - factor * rows[i]
+    return rows
+
+
+def inverse(matrix, size):
+    matrix = matrix + diagonal(size, 64)
+    groups = [matrix[8 * t : 8 * t + 8] for t in range(size // 8)]
+    row = sublanes(8)
+    for first in range(0, size, WIDTH):
+        columns, block, rows = pivots(groups, first, first, WIDTH)
+        rows = solved(block, rows)
+        for t in range(size // 8):
+            for j in range(WIDTH):
+                groups[t] = groups[t] - columns[j][t] * rows[j]
+            for j in range(WIDTH):
+                if t == (first + j) // 8:
+                    groups[t] = jnp.where(row == (first + j) % 8, rows[j], groups[t])
+    return jnp.concatenate(groups, axis=0)
+
+
+def lower_solved(matrix, size, scale):
+    groups = [matrix[8 * t : 8 * t + 8] for t in range(size // 8)]
+    row = sublanes(8)
+    result = [jnp.zeros((8, 128), jnp.float32) for _ in groups]
+    for first in range(0, size, WIDTH):
+        columns, block, rows = pivots(groups, first, 64 + first, WIDTH)
+        whole = solved(block, rows)
+        for i in range(WIDTH):
+            inverse_root = lax.rsqrt(block[i][i]) * scale
+            t, at = (first + i) // 8, (first + i) % 8
+            result[t] = jnp.where(row == at, rows[i] * inverse_root, result[t])
+            if i + 1 < WIDTH:
+                turn = 1.0 / block[i][i]
+                for k in range(i + 1, WIDTH):
+                    factor = block[k][i] * turn
+                    block[k] = [a - factor * b for a, b in zip(block[k], block[i])]
+                    rows[k] = rows[k] - factor * rows[i]
+        for t in range(size // 8):
+            if 8 * t + 7 >= first + WIDTH:
+                for j in range(WIDTH):
+                    groups[t] = groups[t] - columns[j][t] * whole[j]
+    return jnp.concatenate(result, axis=0)
+
+
+def projected(basis, matrix):
+    tall = jnp.concatenate([basis, jnp.zeros((80, 128), jnp.float32)], axis=0)
+    return nt(nn(basis[:, : matrix.shape[0]], matrix), tall)
+
+
+def rayleigh_ritz(gram_stiff, gram_mass, total_rows):
+    m, n = 16, 48
+    inverted = inverse(gram_stiff + 1.0 * gram_mass, n)
+    coeffs = below(pltpu.roll(nn(gram_mass[:m, :n], inverted), 64, 1), n)
+    padded = jnp.concatenate(
+        [jnp.zeros((64, 128), jnp.float32), coeffs, jnp.zeros((48, 128), jnp.float32)], axis=0
+    )
+    normalizer = nt(nn(coeffs[:, :n], gram_mass), padded)
+    rotation = lower_solved(normalizer + coeffs, m, total_rows**0.5)
+    rotation = below(rotation, n)
+    ritz_matrix = nt(nn(rotation[:, :n], gram_stiff), rotation) * (1.0 / total_rows)
+    return rotation, ritz_matrix
+
+
+def pair_coefficients(rotation, basis):
+    inner = jnp.where(lanes(16) >= 16, rotation, 0.0)
+    both = jnp.concatenate([rotation, inner], axis=0)
+    return nn(both[:, :48], basis)
+
+
+def first_kernel(total_rows, sums_ref, coeffs_ref, ritz_ref):
+    m = 16
+    sums = sums_ref[...]
+    gram_stiff = below(sums, 64)
+    gram_mass = below(pltpu.roll(sums, 64, 1), 64)
+    lane = lanes(m)
+    start_mass = jnp.where((lane >= 64) & (lane < 80), sums[:m], 0.0)
+    start = below(lower_solved(start_mass + diagonal(m, 0), m, total_rows**0.5), m)
+    ritz_matrix = nt(nn(start[:, :m], gram_stiff[:m]), start) * (1.0 / total_rows)
+    pulled = nn(ritz_matrix, start)
+    residual = pltpu.roll(start, 16, 1) - pltpu.roll(pulled, 32, 1)
+    basis = jnp.concatenate([start, residual, diagonal(m, 48)], axis=0)
     rotation, ritz_matrix = rayleigh_ritz(
-        congruence(basis, gram_stiff), congruence(basis, gram_mass), total_rows, m
-    )
-    modes = product(rotation, basis)
-    directions = product(rotation[:, m:], basis[m:])
-    return jnp.concatenate([modes, directions]), ritz_matrix
-
-
-def last_coefficients(gram_stiff, gram_mass, ritz_matrix, total_rows, m):
-    none = jnp.zeros((m, m), jnp.float32)
-    rotation, next_ritz = rayleigh_ritz(
-        gram_stiff[: 3 * m, : 3 * m], gram_mass[: 3 * m, : 3 * m], total_rows, m
-    )
-    of_x, of_r, of_p = rotation[:, :m], rotation[:, m : 2 * m], rotation[:, 2 * m :]
-    pulled = product(next_ritz, rotation)
-    zeros5 = jnp.zeros((m, 5 * m), jnp.float32)
-    basis = jnp.concatenate(
-        [
-            jnp.concatenate([rotation, zeros5], axis=1),
-            jnp.concatenate(
-                [
-                    none,
-                    of_x,
-                    none,
-                    of_r,
-                    of_p,
-                    product(of_x, ritz_matrix) - pulled[:, :m],
-                    -pulled[:, m:],
-                ],
-                axis=1,
-            ),
-            jnp.concatenate([none, of_r, of_p, zeros5], axis=1),
-        ]
-    )
-    rotation, last_ritz = rayleigh_ritz(
-        congruence(basis, gram_stiff), congruence(basis, gram_mass), total_rows, m
-    )
-    modes = product(rotation, basis)
-    directions = product(rotation[:, m:], basis[m:])
-    return jnp.concatenate([modes, directions]), last_ritz
+        projected(basis, gram_stiff), projected(basis, gram_mass), total_rows
+    )
+    coeffs_ref[...] = pair_coefficients(rotation, basis)
+    ritz_ref[...] = ritz_matrix
+
+
+def last_kernel(total_rows, sums_ref, ritz_ref, coeffs_ref, out_ref):
+    m = 16
+    both = sums_ref[:128]
+    turned = both.T
+    row, lane = sublanes(128), lanes(128)
+    stiff_diagonal = jnp.broadcast_to(sums_ref[128:129], (128, 128))
+    gram_stiff = jnp.where(row > lane, both, jnp.where(row < lane, turned, stiff_diagonal))
+    gram_mass = jnp.where(row > lane, turned, both)
+    rotation, ritz_matrix = rayleigh_ritz(
+        below(gram_stiff[:48], 48), below(gram_mass[:48], 48), total_rows
+    )
+    of_x = below(rotation, m)
+    wide = nn(rotation[:, :m], jnp.concatenate([ritz_ref[...], jnp.zeros((m, 112), jnp.float32)], axis=1))
+    pulled = nn(ritz_matrix, rotation)
+    residual = (
+        pltpu.roll(of_x, 16, 1) + pltpu.roll(rotation - of_x, 32, 1) + pltpu.roll(wide - pulled, 80, 1)
+    )
+    basis = jnp.concatenate([rotation, residual, rotation - of_x], axis=0)
+    rotation, ritz_matrix = rayleigh_ritz(
+        projected(basis, gram_stiff), projected(basis, gram_mass), total_rows
+    )
+    coeffs_ref[...] = pair_coefficients(rotation, basis)
+    out_ref[...] = ritz_matrix
+
+
+def coefficients(kernel, total_rows, *operands):
+    return pl.pallas_call(
+        functools.partial(kernel, total_rows),
+        out_shape=(
+            jax.ShapeDtypeStruct((32, 128), jnp.float32),
+            jax.ShapeDtypeStruct((16, 16), jnp.float32),
+        ),
+        compiler_params=pltpu.CompilerParams(vmem_limit_bytes=16 * 1024 * 1024),
+        name=kernel.__name__,
+    )(*operands)
 
 
 def packed(gram_stiff, gram_mass):
@@ -178,14 +286,6 @@
     low = jnp.tril(jnp.ones((size, size), bool), -1)
     both = jnp.where(low, gram_stiff, gram_mass)
     return jnp.concatenate([both, jnp.broadcast_to(jnp.diagonal(gram_stiff)[None], (8, size))])
-
-
-def unpacked(rows):
-    size = rows.shape[1]
-    both, diagonal = rows[:size], rows[size]
-    low = jnp.tril(both, -1)
-    high = jnp.triu(both, 1)
-    return low + low.T + jnp.diag(diagonal), high + high.T + jnp.diag(jnp.diagonal(both))
 
 
 def on_device(stiff_tiles, tile_mask, edge_star, start_modes, start_directions):
@@ -210,9 +310,9 @@
     gram_mass = gram(own, own * star)
     sums = slab_sum(jnp.concatenate([symmetric(gram_stiff), symmetric(gram_mass)], axis=1))
     applied_basis = jnp.concatenate([applied_modes, with_halo(rest)])
-    size = 4 * m
-    coeffs, ritz_matrix = first_coefficients(sums[:, :size], sums[:, size:], total_rows, m)
-
+    coeffs, ritz_matrix = coefficients(first_kernel, total_rows, sums)
+
+    coeffs = coeffs[:, : 4 * m]
     pair = product(coeffs, basis)
     applied_pair = product(coeffs, applied_basis)
     modes, directions = pair[:m], pair[m:]
@@ -239,8 +339,8 @@
     )
     gram_stiff = symmetric(gram(own, applied_own))
     gram_mass = symmetric(gram(own, own * star))
-    gram_stiff, gram_mass = unpacked(slab_sum(packed(gram_stiff, gram_mass)))
-    coeffs, ritz_matrix = last_coefficients(gram_stiff, gram_mass, ritz_matrix, total_rows, m)
+    sums = slab_sum(packed(gram_stiff, gram_mass))
+    coeffs, ritz_matrix = coefficients(last_kernel, total_rows, sums, ritz_matrix)
     result = product(coeffs, own)
     return (result[:m], result[m:], ritz_matrix)
 

time: 217 us -> 176 us (0.81)
  other arithmetic: 49.4 us -> 4.97 us
  Pallas kernels: 16.3 us -> 30.8 us
  blocking collectives: 41.5 us -> 53.5 us
  starting transfers between devices: 54.5 us -> 47.1 us
  matrix products: 15.7 us -> 9.73 us
  local copies, waits for them, and re-layouts: 18.8 us -> 13.8 us
  waiting for transfers between devices: 18.7 us -> 14 us
    another operation x36 -> x0, other arithmetic: 44.2 us -> none  [the longest x9 15.2 us: rayleigh_ritz(): factor = jnp.linalg.cholesky(shifted)]
    pallas_call x0 -> x2, Pallas kernels: none -> 14.5 us  [coefficients(): pl.pallas_call(functools.partial(kernel, total_rows), out_shape=(jax.Shap...]
    all_to_all x1 -> x2, blocking collectives: 10 us -> 22 us  [slab_sum(): own = lax.all_to_all(shared, ('y', 'core'), 0, 0, tiled=True).sum(0)]
    all_to_all x1 -> x0, starting transfers between devices: 7.48 us -> none  [slab_sum(): own = lax.all_to_all(shared, ('y', 'core'), 0, 0, tiled=True).sum(0)]
    all_to_all x1 -> x0, waiting for transfers between devices: 4.72 us -> none  [slab_sum(): own = lax.all_to_all(shared, ('y', 'core'), 0, 0, tiled=True).sum(0)]
    dot_general x29 -> x4, matrix products: 7.32 us -> 4 us  [product(): jnp.dot(left, right, precision=lax.Precision.HIGHEST, preferred_element_t...]
    unnamed x37 -> x34, local copies, waits for them, and re-layouts: 9.43 us -> 7.75 us
    dot_general x8 -> x4, matrix products: 6.66 us -> 5.73 us  [gram(): lax.dot_general(left, right, (((1,), (1,)), ((), ())), precision=lax.Prec...]
  transfers between devices with their start and end apart: 11 -> 10, of which waited for: 4 -> 3; matrix products, arithmetic and copies ran while one was open for 12% -> 3% of each run, Pallas kernels for 0% -> 3%
where the time goes in v1:
time: 176 us; the launch traced here: 175 us
  blocking collectives  53.5 us (30%)
  starting transfers between devices  47.1 us (27%)
  Pallas kernels  30.8 us (18%)
  waiting for transfers between devices  14 us (8%)
  local copies, waits for them, and re-layouts  13.8 us (8%)
  matrix products  9.73 us (6%)
  other arithmetic  4.97 us (3%)
    all_to_all x2, blocking collectives, slab_sum(): own = lax.all_to_all(shared, ('y', 'core'), 0, 0, tiled=True).sum(0)  22 us
    all_to_all x1, blocking collectives, slab_sum(): own = lax.all_to_all(copies, 'z', 0, 0, tiled=True).sum(0)  19.1 us
    pallas_call x4, Pallas kernels, band(): pl.pallas_call(band_kernel, grid=(width // (STEP_BLOCKS * TILE),), in_spe...  16.3 us
    all_to_all x1, starting transfers between devices, slab_sum(): own = lax.all_to_all(copies, 'z', 0, 0, tiled=True).sum(0)  16 us
    pallas_call x2, Pallas kernels, coefficients(): pl.pallas_call(functools.partial(kernel, total_rows), out_shape=(jax.Shap...  14.5 us
    ppermute x4, starting transfers between devices, from_left(): return lax.ppermute(edge, SLAB, [(i, i + 1) for i in range(count - 1)])  13.8 us
    all_to_all x1, blocking collectives, slab_sum(): lax.all_to_all(copies, ('y', 'core'), 0, 0, tiled=True).reshape(rows.shape)  12.4 us
    ppermute x4, starting transfers between devices, from_right(): return lax.ppermute(edge, SLAB, [(i + 1, i) for i in range(count - 1)])  11.9 us
  transfers between devices with their start and end apart: 10, of which 3 were waited for; matrix products, arithmetic and copies ran while one was open for 3% of the time, Pallas kernels for 3%

profile of v1, /device:TPU:1, one launch (start us, length us, event | category | flops | bytes accessed | tf_op | source)
XLA Modules:
  0.0 175.2 jit_solution(12992900271073778676)
XLA Ops:
  0.6 1.0 broadcast_multiply_fusion.1
  1.6 0.7 broadcast_in_dim.16
  2.3 0.8 pad_maximum_fusion.13
  3.1 4.6 %collective-permute-start = (f32[56,128]{1,0:T(8,128)S(1)}, f32[56,128]{1,0:T(8,128)S(1)}, u32[]{:S(2)}, u32[]{:S(2)}) collective-permute-start(f32[56,128]{1,0:T(8,128)S(1)} %get-tuple-element.27), channel_id=1, source_target_pairs={{0,4},{4,8},{8,12},{12,16},{16,20},{20,24},{24,28},{28,32},{32,36}... | collective-permute-start | bytes 86024 | tf_op jit(solution)/shard_map/ppermute | solution.py:29
  7.7 5.5 %collective-permute-start.1 = (f32[56,128]{1,0:T(8,128)S(1)}, f32[56,128]{1,0:T(8,128)S(1)}, u32[]{:S(2)}, u32[]{:S(2)}) collective-permute-start(f32[56,128]{1,0:T(8,128)S(1)} %get-tuple-element.28), channel_id=1, source_target_pairs={{4,0},{8,4},{12,8},{16,12},{20,16},{24,20},{28,24},{32,28},{36,32}... | collective-permute-start | bytes 86024 | tf_op jit(solution)/shard_map/ppermute | solution.py:34
  13.2 0.8 copy.32.mask_ref
  13.9 0.1 collective-permute-done.1
  14.0 1.1 pad_maximum_fusion.4
  15.1 0.1 slice.139.ext_ref
  15.2 0.1 fusion.57
  15.2 0.0 copy-start
  15.3 2.8 %copy-done = f32[32,3,128,128]{3,2,1,0:T(8,128)S(1)} copy-done((f32[32,3,128,128]{3,2,1,0:T(8,128)S(1)}, f32[32,3,128,128]{3,2,1,0:T(8,128)}, u32[]{:S(2)}) %copy-start) | copy-done | bytes 6291480
  18.0 4.1 %band.4 = f32[48,4096]{1,0:T(8,128)S(1)} custom-call(s32[32,2]{1,0:T(8,128)S(1)} %copy.32.mask_ref, f32[32,3,128,128]{3,2,1,0:T(8,128)S(1)} %copy-done, f32[48,4352]{1,0:T(8,128)S(1)} %slice.139.ext_ref), custom_call_target="tpu_custom_call" | custom-call | tf_op jit(solution)/shard_map/band/pallas_call | solution.py:76
  22.1 1.9 %collective-permute-start.2 = (f32[16,128]{1,0:T(8,128)S(1)}, f32[16,128]{1,0:T(8,128)S(1)}, u32[]{:S(2)}, u32[]{:S(2)}) collective-permute-start(f32[16,128]{1,0:T(8,128)S(1)} %get-tuple-element.34), channel_id=1, source_target_pairs={{0,4},{4,8},{8,12},{12,16},{16,20},{20,24},{24,28},{28,32},{32,36}... | collective-permute-start | bytes 24584 | tf_op jit(solution)/shard_map/ppermute | solution.py:29
  24.1 2.4 %collective-permute-start.3 = (f32[16,128]{1,0:T(8,128)S(1)}, f32[16,128]{1,0:T(8,128)S(1)}, u32[]{:S(2)}, u32[]{:S(2)}) collective-permute-start(f32[16,128]{1,0:T(8,128)S(1)} %get-tuple-element.35), channel_id=1, source_target_pairs={{4,0},{8,4},{12,8},{16,12},{20,16},{24,20},{28,24},{32,28},{36,32}... | collective-permute-start | bytes 24584 | tf_op jit(solution)/shard_map/ppermute | solution.py:34
  26.5 0.1 fusion.58
  26.5 0.0 copy-start.6
  26.6 2.5 %collective-permute-done.3 = f32[16,128]{1,0:T(8,128)S(1)} collective-permute-done((f32[16,128]{1,0:T(8,128)S(1)}, f32[16,128]{1,0:T(8,128)S(1)}, u32[]{:S(2)}, u32[]{:S(2)}) %collective-permute-start.3) | collective-permute-done | bytes 8224 | tf_op jit(solution)/shard_map/ppermute | solution.py:34
  29.1 3.9 %band.5 = f32[16,4096]{1,0:T(8,128)S(1)} custom-call(s32[32,2]{1,0:T(8,128)S(1)} %copy.32.mask_ref, f32[32,3,128,128]{3,2,1,0:T(8,128)S(1)} %copy-done, f32[16,4352]{1,0:T(8,128)S(1)} %pad_maximum_fusion.7.ext_ref), custom_call_target="tpu_custom_call" | custom-call | tf_op jit(solution)/shard_map/band/pallas_call | solution.py:76
  33.0 1.0 fusion.33
  33.9 0.1 copy.34
  34.0 0.0 copy-start.2
  34.1 0.0 copy-start.5
  34.1 1.0 fusion.2
  35.1 0.1 copy.35
  35.2 0.1 maximum_bitcast_fusion
  35.3 12.0 %all_to_all.30 = f32[8,8,128]{2,1,0:T(8,128)S(1)} all-to-all(f32[8,8,128]{2,1,0:T(8,128)S(1)} %maximum_bitcast_fusion), channel_id=1, replica_groups=mesh['z'=16,'y'=4,'core'=2,'x'=4] {'y','core'}, dimensions={0} | all-to-all | bytes 65536 | tf_op jit(solution)/shard_map/all_to_all | solution.py:20
  47.3 0.6 broadcast_in_dim.19
  47.9 16.0 %all-to-all-start.1 = ((f32[16,8,128]{2,1,0:T(8,128)}), f32[16,8,128]{2,1,0:T(8,128)S(1)}, u32[]{:S(2)}, u32[]{:S(2)}) async-start(f32[16,8,128]{2,1,0:T(8,128)} %broadcast_in_dim.19), calls=%async_computation.1 | async-start | bytes 131072 | tf_op jit(solution)/shard_map/all_to_all | solution.py:22
  64.0 11.5 %all-to-all-done.1 = f32[16,8,128]{2,1,0:T(8,128)S(1)} async-done(((f32[16,8,128]{2,1,0:T(8,128)}), f32[16,8,128]{2,1,0:T(8,128)S(1)}, u32[]{:S(2)}, u32[]{:S(2)}) %all-to-all-start.1) | async-done | bytes 65568 | tf_op jit(solution)/shard_map/all_to_all | solution.py:22
  75.5 0.6 broadcast_in_dim.20
  76.1 5.4 %all-to-all-start.2 = ((f32[8,8,128]{2,1,0:T(8,128)}), f32[8,8,128]{2,1,0:T(8,128)S(1)}, u32[]{:S(2)}, u32[]{:S(2)}) async-start(f32[8,8,128]{2,1,0:T(8,128)} %broadcast_in_dim.20), calls=%async_computation.2 | async-start | bytes 65536 | tf_op jit(solution)/shard_map/all_to_all | solution.py:24
  81.5 0.6 pad_maximum_fusion.16
  82.1 3.7 %collective-permute-start.4 = (f32[48,128]{1,0:T(8,128)}, f32[48,128]{1,0:T(8,128)}, u32[]{:S(2)}, u32[]{:S(2)}) collective-permute-start(f32[48,128]{1,0:T(8,128)} %get-tuple-element.29), channel_id=1, source_target_pairs={{0,4},{4,8},{8,12},{12,16},{16,20},{20,24},{24,28},{28,32},{32,36}... | collective-permute-start | bytes 73736 | tf_op jit(solution)/shard_map/ppermute | solution.py:29
  85.8 1.9 %collective-permute-start.5 = (f32[48,128]{1,0:T(8,128)S(1)}, f32[48,128]{1,0:T(8,128)}, u32[]{:S(2)}, u32[]{:S(2)}) collective-permute-start(f32[48,128]{1,0:T(8,128)S(1)} %get-tuple-element.30), channel_id=1, source_target_pairs={{4,0},{8,4},{12,8},{16,12},{20,16},{24,20},{28,24},{32,28},{36,32}... | collective-permute-start | bytes 73736 | tf_op jit(solution)/shard_map/ppermute | solution.py:34
  87.7 0.0 copy-start.9
  87.7 5.4 %first_kernel.1 = (f32[32,128]{1,0:T(8,128)S(1)}, f32[16,16]{1,0:T(8,128)S(1)}) custom-call(f32[64,128]{1,0:T(8,128)S(1)} %bitcast.33), custom_call_target="tpu_custom_call" | custom-call | tf_op jit(solution)/shard_map/first_kernel/pallas_call | solution.py:273
  93.1 0.7 fusion.4
  93.9 0.0 slice-start.1
  93.9 1.8 %fusion.16 = f32[32,4352]{1,0:T(8,128)S(1)} fusion(f32[48,128]{1,0:T(8,128)} %collective-permute-done.5, f32[16,4096]{1,0:T(8,128)S(1)} %copy-done.9, f32[16,4096]{1,0:T(8,128)S(1)} %copy-done.7, f32[16,4096]{1,0:T(8,128)S(1)} %band.5, f32[48,128]{1,0:T(8,128)} %collective-permute-done.4, f32[16,128]{1,0:T(8,128)S(1)} %collective-permute-done.3, ...), kind=kOutput, calls=%fused_computation.17 | convolution fusion | flops 108904448 | bytes 1687552 | tf_op jit(solution)/shard_map/dot_general | solution.py:102
  95.7 0.4 constant_dynamic-update-slice_fusion.4
  96.4 4.5 %band.6 = f32[80,4096]{1,0:T(8,128)S(1)} custom-call(s32[32,2]{1,0:T(8,128)S(1)} %copy.32.mask_ref, f32[32,3,128,128]{3,2,1,0:T(8,128)S(1)} %bitcast.32, f32[80,4352]{1,0:T(8,128)S(1)} %get-tuple-element.13.ext_ref), custom_call_target="tpu_custom_call" | custom-call | tf_op jit(solution)/shard_map/band/pallas_call | solution.py:76
  100.9 3.6 %collective-permute-start.6 = (f32[16,128]{1,0:T(8,128)S(1)}, f32[16,128]{1,0:T(8,128)S(1)}, u32[]{:S(2)}, u32[]{:S(2)}) collective-permute-start(f32[16,128]{1,0:T(8,128)S(1)} %get-tuple-element.19), channel_id=1, source_target_pairs={{0,4},{4,8},{8,12},{12,16},{16,20},{20,24},{24,28},{28,32},{32,36}... | collective-permute-start | bytes 24584 | tf_op jit(solution)/shard_map/ppermute | solution.py:29
  104.5 2.1 %collective-permute-start.7 = (f32[16,128]{1,0:T(8,128)S(1)}, f32[16,128]{1,0:T(8,128)S(1)}, u32[]{:S(2)}, u32[]{:S(2)}) collective-permute-start(f32[16,128]{1,0:T(8,128)S(1)} %get-tuple-element.20), channel_id=1, source_target_pairs={{4,0},{8,4},{12,8},{16,12},{20,16},{24,20},{28,24},{32,28},{36,32}... | collective-permute-start | bytes 24584 | tf_op jit(solution)/shard_map/ppermute | solution.py:34
  106.6 0.8 fusion.56
  107.4 0.1 fusion.32
  107.5 1.2 copy-done.3
  108.8 1.9 %fusion = f32[128,128]{1,0:T(8,128)S(1)} fusion(f32[128,4096]{1,0:T(8,128)S(1)} %fusion.32, f32[4096]{0:T(1024)S(1)} %copy-done.11), kind=kOutput, calls=%fused_computation.1 | convolution fusion | flops 805830656 | bytes 2179072 | tf_op jit(solution)/shard_map/dot_general | solution.py:92
  110.7 0.7 copy.39
  111.4 1.0 pad_maximum_fusion.8.ext_ref
  112.4 0.0 copy-start.1
  112.4 2.8 %copy-done.1 = f32[32,3,128,128]{3,2,1,0:T(8,128)S(1)} copy-done((f32[32,3,128,128]{3,2,1,0:T(8,128)S(1)}, f32[32,3,128,128]{3,2,1,0:T(8,128)}, u32[]{:S(2)}) %copy-start.1) | copy-done | bytes 6291480
  115.2 3.9 %band.7 = f32[16,4096]{1,0:T(8,128)S(1)} custom-call(s32[32,2]{1,0:T(8,128)S(1)} %copy.32.mask_ref, f32[32,3,128,128]{3,2,1,0:T(8,128)S(1)} %copy-done.1, f32[16,4352]{1,0:T(8,128)S(1)} %pad_maximum_fusion.8.ext_ref), custom_call_target="tpu_custom_call" | custom-call | tf_op jit(solution)/shard_map/band/pallas_call | solution.py:76
  119.1 0.1 slice_dynamic-update-slice_fusion
  119.2 1.9 %fusion.62 = f32[128,128]{1,0:T(8,128)S(1)} fusion(f32[128,4096]{1,0:T(8,128)S(1)} %fusion.32, f32[128,4096]{1,0:T(8,128)S(1)} %slice_dynamic-update-slice_fusion), kind=kOutput, calls=%fused_computation.105 | convolution fusion | flops 805306368 | bytes 4259840 | tf_op jit(solution)/shard_map/dot_general | solution.py:92
  121.0 0.1 copy.38
  121.1 0.1 fusion.44
  121.2 1.2 gather_fusion
  122.5 10.0 %all_to_all.31 = f32[8,17,128]{2,1,0:T(8,128)S(1)} all-to-all(f32[8,17,128]{2,1,0:T(8,128)S(1)} %reshape.26), channel_id=1, replica_groups=mesh['z'=16,'y'=4,'core'=2,'x'=4] {'y','core'}, dimensions={0} | all-to-all | bytes 139264 | tf_op jit(solution)/shard_map/all_to_all | solution.py:20
  132.6 19.1 %all_to_all.32 = f32[16,17,128]{2,1,0:T(8,128)S(1)} all-to-all(f32[16,17,128]{2,1,0:T(8,128)S(1)} %broadcast_in_dim.22), channel_id=1, replica_groups=mesh['z'=16,'y'=4,'core'=2,'x'=4] {'z'}, dimensions={0} | all-to-all | bytes 278528 | tf_op jit(solution)/shard_map/all_to_all | solution.py:22
  151.7 12.4 %all_to_all.33 = f32[8,17,128]{2,1,0:T(8,128)S(1)} all-to-all(f32[8,17,128]{2,1,0:T(8,128)S(1)} %broadcast_in_dim.23), channel_id=1, replica_groups=mesh['z'=16,'y'=4,'core'=2,'x'=4] {'y','core'}, dimensions={0} | all-to-all | bytes 139264 | tf_op jit(solution)/shard_map/all_to_all | solution.py:24
  164.1 9.1 %last_kernel.1 = (f32[32,128]{1,0:T(8,128)S(1)}, f32[16,16]{1,0:T(8,128)}) custom-call(f32[136,128]{1,0:T(8,128)S(1)} %reshape.27.sums_ref, f32[16,16]{1,0:T(8,128)S(1)} %get-tuple-element.8.ritz_ref), custom_call_target="tpu_custom_call" | custom-call | tf_op jit(solution)/shard_map/last_kernel/pallas_call | solution.py:273
  173.2 1.2 fusion.63
  174.4 0.8 fusion.61
  (54 shorter events, 0.6 us)
Async XLA Ops:
  3.1 10.8 %collective-permute-start = (f32[56,128]{1,0:T(8,128)S(1)}, f32[56,128]{1,0:T(8,128)S(1)}, u32[]{:S(2)}, u32[]{:S(2)}) collective-permute-start(f32[56,128]{1,0:T(8,128)S(1)} %get-tuple-element.27), channel_id=1, source_target_pairs={{0,4},{4,8},{8,12},{12,16},{16,20},{20,24},{24,28},{28,32},{32,36}... | collective-permute-start | bytes 86024 | tf_op jit(solution)/shard_map/ppermute | solution.py:29
  7.7 6.3 %collective-permute-start.1 = (f32[56,128]{1,0:T(8,128)S(1)}, f32[56,128]{1,0:T(8,128)S(1)}, u32[]{:S(2)}, u32[]{:S(2)}) collective-permute-start(f32[56,128]{1,0:T(8,128)S(1)} %get-tuple-element.28), channel_id=1, source_target_pairs={{4,0},{8,4},{12,8},{16,12},{20,16},{24,20},{28,24},{32,28},{36,32}... | collective-permute-start | bytes 86024 | tf_op jit(solution)/shard_map/ppermute | solution.py:34
  15.2 2.8 %copy-start = (f32[32,3,128,128]{3,2,1,0:T(8,128)S(1)}, f32[32,3,128,128]{3,2,1,0:T(8,128)}, u32[]{:S(2)}) copy-start(f32[32,3,128,128]{3,2,1,0:T(8,128)} %tiles_ref.7) | copy-start | bytes 18874372
  22.1 4.4 %collective-permute-start.2 = (f32[16,128]{1,0:T(8,128)S(1)}, f32[16,128]{1,0:T(8,128)S(1)}, u32[]{:S(2)}, u32[]{:S(2)}) collective-permute-start(f32[16,128]{1,0:T(8,128)S(1)} %get-tuple-element.34), channel_id=1, source_target_pairs={{0,4},{4,8},{8,12},{12,16},{16,20},{20,24},{24,28},{28,32},{32,36}... | collective-permute-start | bytes 24584 | tf_op jit(solution)/shard_map/ppermute | solution.py:29
  24.1 5.0 %collective-permute-start.3 = (f32[16,128]{1,0:T(8,128)S(1)}, f32[16,128]{1,0:T(8,128)S(1)}, u32[]{:S(2)}, u32[]{:S(2)}) collective-permute-start(f32[16,128]{1,0:T(8,128)S(1)} %get-tuple-element.35), channel_id=1, source_target_pairs={{4,0},{8,4},{12,8},{16,12},{20,16},{24,20},{28,24},{32,28},{36,32}... | collective-permute-start | bytes 24584 | tf_op jit(solution)/shard_map/ppermute | solution.py:34
  26.5 55.0 %copy-start.6 = (f32[16,4096]{1,0:T(8,128)}, f32[16,4096]{1,0:T(8,128)S(1)}, u32[]{:S(2)}) copy-start(f32[16,4096]{1,0:T(8,128)S(1)} %get-tuple-element.31) | copy-start | bytes 786436
  26.5 55.0 %copy-start.8 = (f32[16,4096]{1,0:T(8,128)}, f32[16,4096]{1,0:T(8,128)S(1)}, u32[]{:S(2)}) copy-start(f32[16,4096]{1,0:T(8,128)S(1)} %get-tuple-element.32) | copy-start | bytes 786436
  32.9 1.1 copy-start.11
  34.0 29.9 %copy-start.2 = (f32[16,4096]{1,0:T(8,128)S(1)}, f32[16,4096]{1,0:T(8,128)}, u32[]{:S(2)}) copy-start(f32[16,4096]{1,0:T(8,128)} %param.8) | copy-start | bytes 786436
  34.1 29.9 %copy-start.5 = (f32[16,4096]{1,0:T(8,128)S(1)}, f32[16,4096]{1,0:T(8,128)}, u32[]{:S(2)}) copy-start(f32[16,4096]{1,0:T(8,128)} %param.9) | copy-start | bytes 786436
  47.9 27.6 %all-to-all-start.1 = ((f32[16,8,128]{2,1,0:T(8,128)}), f32[16,8,128]{2,1,0:T(8,128)S(1)}, u32[]{:S(2)}, u32[]{:S(2)}) async-start(f32[16,8,128]{2,1,0:T(8,128)} %broadcast_in_dim.19), calls=%async_computation.1 | async-start | bytes 131072 | tf_op jit(solution)/shard_map/all_to_all | solution.py:22
  76.1 11.6 %all-to-all-start.2 = ((f32[8,8,128]{2,1,0:T(8,128)}), f32[8,8,128]{2,1,0:T(8,128)S(1)}, u32[]{:S(2)}, u32[]{:S(2)}) async-start(f32[8,8,128]{2,1,0:T(8,128)} %broadcast_in_dim.20), calls=%async_computation.2 | async-start | bytes 65536 | tf_op jit(solution)/shard_map/all_to_all | solution.py:24
  82.1 11.8 %copy-start.7 = (f32[16,4096]{1,0:T(8,128)S(1)}, f32[16,4096]{1,0:T(8,128)}, u32[]{:S(2)}) copy-start(f32[16,4096]{1,0:T(8,128)} %copy-done.6) | copy-start | bytes 786436
  82.1 11.8 %collective-permute-start.4 = (f32[48,128]{1,0:T(8,128)}, f32[48,128]{1,0:T(8,128)}, u32[]{:S(2)}, u32[]{:S(2)}) collective-permute-start(f32[48,128]{1,0:T(8,128)} %get-tuple-element.29), channel_id=1, source_target_pairs={{0,4},{4,8},{8,12},{12,16},{16,20},{20,24},{24,28},{28,32},{32,36}... | collective-permute-start | bytes 73736 | tf_op jit(solution)/shard_map/ppermute | solution.py:29
  85.8 8.1 %collective-permute-start.5 = (f32[48,128]{1,0:T(8,128)S(1)}, f32[48,128]{1,0:T(8,128)}, u32[]{:S(2)}, u32[]{:S(2)}) collective-permute-start(f32[48,128]{1,0:T(8,128)S(1)} %get-tuple-element.30), channel_id=1, source_target_pairs={{4,0},{8,4},{12,8},{16,12},{20,16},{24,20},{28,24},{32,28},{36,32}... | collective-permute-start | bytes 73736 | tf_op jit(solution)/shard_map/ppermute | solution.py:34
  87.7 6.2 %copy-start.9 = (f32[16,4096]{1,0:T(8,128)S(1)}, f32[16,4096]{1,0:T(8,128)}, u32[]{:S(2)}) copy-start(f32[16,4096]{1,0:T(8,128)} %copy-done.8) | copy-start | bytes 786436
  93.1 3.2 %slice-start = ((s8[6291456]{0:T(1024)(128)(4,1)}), s8[4194304]{0:T(1024)(128)(4,1)S(1)}, s32[]{:S(2)}) async-start(s8[6291456]{0:T(1024)(128)(4,1)} %bitcast.31), calls=%async_computation.6 | async-start | bytes 8388608
  93.9 2.5 %slice-start.1 = ((s8[6291456]{0:T(1024)(128)(4,1)}), s8[2097152]{0:T(1024)(128)(4,1)S(1)}, s32[]{:S(2)}) async-start(s8[6291456]{0:T(1024)(128)(4,1)} %bitcast.31), calls=%async_computation.7 | async-start | bytes 4194304
  100.9 10.5 %collective-permute-start.6 = (f32[16,128]{1,0:T(8,128)S(1)}, f32[16,128]{1,0:T(8,128)S(1)}, u32[]{:S(2)}, u32[]{:S(2)}) collective-permute-start(f32[16,128]{1,0:T(8,128)S(1)} %get-tuple-element.19), channel_id=1, source_target_pairs={{0,4},{4,8},{8,12},{12,16},{16,20},{20,24},{24,28},{28,32},{32,36}... | collective-permute-start | bytes 24584 | tf_op jit(solution)/shard_map/ppermute | solution.py:29
  104.5 6.9 %collective-permute-start.7 = (f32[16,128]{1,0:T(8,128)S(1)}, f32[16,128]{1,0:T(8,128)S(1)}, u32[]{:S(2)}, u32[]{:S(2)}) collective-permute-start(f32[16,128]{1,0:T(8,128)S(1)} %get-tuple-element.20), channel_id=1, source_target_pairs={{4,0},{8,4},{12,8},{16,12},{20,16},{24,20},{28,24},{32,28},{36,32}... | collective-permute-start | bytes 24584 | tf_op jit(solution)/shard_map/ppermute | solution.py:34
  107.4 1.3 copy-start.3
  112.4 2.8 %copy-start.1 = (f32[32,3,128,128]{3,2,1,0:T(8,128)S(1)}, f32[32,3,128,128]{3,2,1,0:T(8,128)}, u32[]{:S(2)}) copy-start(f32[32,3,128,128]{3,2,1,0:T(8,128)} %tiles_ref.7) | copy-start | bytes 18874372
  115.2 3.9 %copy-start.4 = (f32[128,4096]{1,0:T(8,128)S(1)}, f32[128,4096]{1,0:T(8,128)}, u32[]{:S(2)}) copy-start(f32[128,4096]{1,0:T(8,128)} %copy-done.3) | copy-start | bytes 6291460
  119.2 2.0 %copy-start.10 = (f32[128,128]{0,1:T(8,128)S(1)}, f32[128,128]{0,1:T(8,128)}, u32[]{:S(2)}) copy-start(f32[128,128]{0,1:T(8,128)} %copy.39) | copy-start | bytes 196612

commit v2 on v1

--- a/solution.py
+++ b/solution.py
@@ -11,6 +11,8 @@
 SLAB = ("z", "y", "core")
 TILE = 128
 STEP_BLOCKS = 4
+STEP = STEP_BLOCKS * TILE
+VMEM = 56 * 1024 * 1024
 WIDTH = 4
 
 
@@ -34,58 +36,10 @@
     return lax.ppermute(edge, SLAB, [(i + 1, i) for i in range(count - 1)])
 
 
-def with_halo(block):
-    low = from_left(block[:, -TILE:])
-    high = from_right(block[:, :TILE])
-    return jnp.concatenate([low, block, high], axis=1)
-
-
 def split(values):
     high = values.astype(jnp.bfloat16)
     low = (values - high.astype(jnp.float32)).astype(jnp.bfloat16)
     return high, low
-
-
-def band_kernel(mask_ref, tiles_ref, ext_ref, out_ref):
-    step = pl.program_id(0)
-    count = ext_ref.shape[0]
-    start = pl.multiple_of(step * STEP_BLOCKS * TILE, TILE)
-    window = ext_ref[:, pl.ds(start, (STEP_BLOCKS + 2) * TILE)]
-    left = jnp.concatenate(split(window), axis=0)
-    for k in range(STEP_BLOCKS):
-        block = step * STEP_BLOCKS + k
-        weight_low = mask_ref[block, 0].astype(jnp.float32)
-        weight_high = mask_ref[block, 1].astype(jnp.float32)
-        row = jnp.concatenate(
-            [tiles_ref[k, 0] * weight_low, tiles_ref[k, 1], tiles_ref[k, 2] * weight_high], axis=1
-        )
-        right = jnp.concatenate(split(row), axis=0)
-        term = lax.dot_general(
-            left[:, k * TILE : (k + 3) * TILE],
-            right,
-            (((1,), (1,)), ((), ())),
-            preferred_element_type=jnp.float32,
-        )
-        term = term[:, :TILE] + term[:, TILE:]
-        out_ref[:, k * TILE : (k + 1) * TILE] = term[:count] + term[count:]
-
-
-def band(extended, tile_set, coupling):
-    count, width = extended.shape
-    width -= 2 * TILE
-    return pl.pallas_call(
-        band_kernel,
-        grid=(width // (STEP_BLOCKS * TILE),),
-        in_specs=[
-            pl.BlockSpec(memory_space=pltpu.SMEM),
-            pl.BlockSpec((STEP_BLOCKS, 3, TILE, TILE), lambda i: (i, 0, 0, 0)),
-            pl.BlockSpec((count, width + 2 * TILE), lambda i: (0, 0)),
-        ],
-        out_specs=pl.BlockSpec((count, STEP_BLOCKS * TILE), lambda i: (0, i)),
-        out_shape=jax.ShapeDtypeStruct((count, width), jnp.float32),
-        compiler_params=pltpu.CompilerParams(vmem_limit_bytes=32 * 1024 * 1024),
-        name="band",
-    )(coupling, tile_set, extended)
 
 
 def gram(left, right):
@@ -96,14 +50,6 @@
         precision=lax.Precision.HIGHEST,
         preferred_element_type=jnp.float32,
     )
-
-
-def product(left, right):
-    return jnp.dot(left, right, precision=lax.Precision.HIGHEST, preferred_element_type=jnp.float32)
-
-
-def symmetric(matrix):
-    return 0.5 * (matrix + matrix.T)
 
 
 def nn(left, right):
@@ -244,7 +190,214 @@
     ritz_ref[...] = ritz_matrix
 
 
-def last_kernel(total_rows, sums_ref, ritz_ref, coeffs_ref, out_ref):
+def nn3(left, right):
+    count = left.shape[0]
+    left_high, left_low = split(left)
+    right_high, right_low = split(right)
+    by_high = jnp.dot(
+        jnp.concatenate([left_high, left_low], axis=0), right_high, preferred_element_type=jnp.float32
+    )
+    by_low = jnp.dot(left_high, right_low, preferred_element_type=jnp.float32)
+    return by_high[:count] + by_high[count:] + by_low
+
+
+def both_parts(values):
+    return jnp.concatenate(split(values), axis=0)
+
+
+def nt_parts(left, right):
+    return lax.dot_general(left, right, (((1,), (1,)), ((), ())), preferred_element_type=jnp.float32)
+
+
+def folded(term):
+    rows, columns = term.shape[0] // 2, term.shape[1] // 2
+    term = term[:, :columns] + term[:, columns:]
+    return term[:rows] + term[rows:]
+
+
+def weight(mask_ref, block, side):
+    return mask_ref[block, side].astype(jnp.float32)
+
+
+def full_rows(mask_ref, tiles_ref, k):
+    block = pl.program_id(0) * STEP_BLOCKS + k
+    return jnp.concatenate(
+        [
+            tiles_ref[k, 0] * weight(mask_ref, block, 0),
+            tiles_ref[k, 1],
+            tiles_ref[k, 2] * weight(mask_ref, block, 1),
+        ],
+        axis=1,
+    )
+
+
+def apply_blocks(mask_ref, tiles_ref, parts_ref, store):
+    start = pl.multiple_of(pl.program_id(0) * STEP, TILE)
+    window = parts_ref[:, pl.ds(start, STEP + 2 * TILE)]
+    for k in range(STEP_BLOCKS):
+        right = both_parts(full_rows(mask_ref, tiles_ref, k))
+        store(k, folded(nt_parts(window[:, k * TILE : (k + 3) * TILE], right)))
+
+
+def fill_parts(parts_ref, row, start, values):
+    count, width = values.shape
+    high, low = split(values)
+    half = parts_ref.shape[0] // 2
+    parts_ref[row : row + count, start : start + width] = high
+    parts_ref[half + row : half + row + count, start : start + width] = low
+
+
+def chunks(width):
+    return [slice(c, c + STEP) for c in range(0, width, STEP)]
+
+
+def edges_of(ref, step, low_ref, high_ref):
+    @pl.when(step == 0)
+    def _():
+        high_ref[...] = ref[:, :TILE]
+
+    @pl.when(step == pl.num_programs(0) - 1)
+    def _():
+        low_ref[...] = ref[:, STEP - TILE :]
+
+
+def start_kernel(mask_ref, tiles_ref, x_ref, p_ref, star_ref, left_ref, right_ref, *rest):
+    ax_ref, other_ref, ax_low, ax_high, parts_ref = rest
+    step, width = pl.program_id(0), x_ref.shape[1]
+
+    @pl.when(step == 0)
+    def _():
+        for start, ref in ((0, left_ref), (TILE + width, right_ref)):
+            x, p, star = ref[:16], ref[16:32], ref[32:33]
+            fill_parts(parts_ref, 0, start, jnp.concatenate([x, x * star, p], axis=0))
+        for c in chunks(width):
+            x, p = x_ref[:, c], p_ref[:, c]
+            fields = jnp.concatenate([x, x * star_ref[:, c], p], axis=0)
+            fill_parts(parts_ref, 0, TILE + c.start, fields)
+
+    def store(k, term):
+        at = slice(k * TILE, (k + 1) * TILE)
+        ax_ref[:, at] = term[:16]
+        other_ref[:, at] = term[16:]
+
+    apply_blocks(mask_ref, tiles_ref, parts_ref, store)
+    edges_of(ax_ref, step, ax_low, ax_high)
+
+
+def gram_kernel(mask_ref, tiles_ref, x_ref, p_ref, star_ref, ax_ref, other_ref, *rest):
+    left_ref, right_ref, twice_ref, sums_ref, low_ref, high_ref, parts_ref, total_ref, edge_ref = rest
+    step, width = pl.program_id(0), ax_ref.shape[1]
+
+    @pl.when(step == 0)
+    def _():
+        fill_parts(parts_ref, 0, 0, left_ref[...])
+        fill_parts(parts_ref, 0, TILE + width, right_ref[...])
+        for c in chunks(width):
+            fill_parts(parts_ref, 0, TILE + c.start, ax_ref[:, c])
+        total_ref[...] = jnp.zeros_like(total_ref)
+
+    def store(k, term):
+        twice_ref[:, k * TILE : (k + 1) * TILE] = term
+
+    apply_blocks(mask_ref, tiles_ref, parts_ref, store)
+    here = pl.ds(pl.multiple_of(step * STEP, TILE), STEP)
+    x, p, star, ax, other = (r[:, here] for r in (x_ref, p_ref, star_ref, ax_ref, other_ref))
+    basis = jnp.concatenate([x, ax, x * star, p], axis=0)
+    applied = jnp.concatenate([ax, twice_ref[...], other, basis * star], axis=0)
+    total_ref[...] += nt_parts(both_parts(basis), both_parts(applied))
+    edge_ref[...] = jnp.concatenate([twice_ref[...], other], axis=0)
+    edges_of(edge_ref, step, low_ref, high_ref)
+
+    @pl.when(step == pl.num_programs(0) - 1)
+    def _():
+        sums = folded(total_ref[...])
+        turned = jnp.concatenate([sums, jnp.zeros((64, 128), jnp.float32)], axis=0).T
+        turned = jnp.where(lanes(64) < 64, turned[:64], pltpu.roll(turned[64:], 64, 1))
+        sums_ref[...] = 0.5 * (sums + turned)
+
+
+def middle_kernel(mask_ref, tiles_ref, coeffs_ref, ritz_ref, *rest):
+    own_refs, left_refs, right_refs = rest[:6], rest[6:9], rest[9:12]
+    out_ref, residual_ref, ax_ref, applied_ref, high_ref, parts_ref, all_ref = rest[12:]
+    step, width = pl.program_id(0), own_refs[0].shape[1]
+
+    def update(start, x, p, star, ax, twice, other):
+        coeffs = coeffs_ref[:, :64]
+        pair = nn3(coeffs, jnp.concatenate([x, ax, x * star, p], axis=0))
+        applied = nn3(coeffs, jnp.concatenate([ax, twice, other], axis=0))
+        x, p = pair[:16], pair[16:]
+        mx = x * star
+        r = applied[:16] - nn(ritz_ref[...], mx)
+        fields = jnp.concatenate([r, applied[16:], mx, r * star, p * star], axis=0)
+        fill_parts(parts_ref, 0, start, fields)
+        if TILE <= start < TILE + width:
+            here = slice(start - TILE, start - TILE + x.shape[1])
+            all_ref[:, here] = jnp.concatenate([x, r, p, fields[16:], applied[:16]], axis=0)
+
+    @pl.when(step == 0)
+    def _():
+        for start, refs in ((0, left_refs), (TILE + width, right_refs)):
+            first, ax, last = (r[...] for r in refs)
+            update(start, first[:16], first[16:32], first[32:33], ax, last[:16], last[16:])
+        for c in chunks(width):
+            update(TILE + c.start, *(r[:, c] for r in own_refs))
+
+    def store(k, term):
+        at = slice(k * TILE, (k + 1) * TILE)
+        residual_ref[:, at] = term[:16]
+        applied_ref[:, at] = term[16:]
+
+    apply_blocks(mask_ref, tiles_ref, parts_ref, store)
+    here = pl.ds(pl.multiple_of(step * STEP, TILE), STEP)
+    out_ref[...] = all_ref[:112, here]
+    ax_ref[...] = all_ref[112:, here]
+
+    @pl.when(step == 0)
+    def _():
+        high_ref[...] = residual_ref[:, :TILE]
+
+
+def pack_kernel(mask_ref, tiles_ref, star_ref, own_ref, ar_ref, ax_ref, applied_ref, right_ref, *rest):
+    sums_ref, parts_ref, stiff_ref, mass_ref = rest
+    step, width = pl.program_id(0), star_ref.shape[1]
+
+    @pl.when(step == 0)
+    def _():
+        fill_parts(parts_ref, 0, width, right_ref[...])
+        for c in chunks(width):
+            fill_parts(parts_ref, 0, c.start, ar_ref[:, c])
+        stiff_ref[...] = jnp.zeros_like(stiff_ref)
+        mass_ref[...] = jnp.zeros_like(mass_ref)
+
+    start = pl.multiple_of(step * STEP, TILE)
+    window = parts_ref[:, pl.ds(start, STEP + TILE)]
+    terms = []
+    for k in range(STEP_BLOCKS):
+        twofold = 2.0 * weight(mask_ref, step * STEP_BLOCKS + k, 1)
+        row = jnp.concatenate([tiles_ref[k, 1], tiles_ref[k, 2] * twofold], axis=1)
+        terms.append(folded(nt_parts(window[:, k * TILE : (k + 2) * TILE], both_parts(row))))
+    twice = jnp.concatenate(terms, axis=1)
+    here = pl.ds(start, STEP)
+    own, ar, star = own_ref[:, here], ar_ref[:, here], star_ref[:, here]
+    basis = jnp.concatenate([own, ar], axis=0)
+    applied = jnp.concatenate(
+        [ax_ref[:, here], ar, own[48:64], applied_ref[:, here], twice], axis=0
+    )
+    left = both_parts(basis)
+    stiff_ref[...] += nt_parts(left, both_parts(applied))
+    mass_ref[...] += nt_parts(left, both_parts(basis * star))
+
+    @pl.when(step == pl.num_programs(0) - 1)
+    def _():
+        stiff, mass = folded(stiff_ref[...]), folded(mass_ref[...])
+        row, lane = sublanes(128), lanes(128)
+        stiff = jnp.where((row >= 112) & (lane >= 112), 0.5 * (stiff + stiff.T), stiff)
+        sums_ref[:128] = jnp.where(row > lane, stiff, mass)
+        along = jnp.sum(jnp.where(row == lane, stiff, 0.0), axis=0, keepdims=True)
+        sums_ref[128:] = jnp.broadcast_to(along, (8, 128))
+
+
+def last_kernel(total_rows, sums_ref, ritz_ref, own_ref, ar_ref, modes_ref, directions_ref, out_ref):
     m = 16
     both = sums_ref[:128]
     turned = both.T
@@ -256,93 +409,107 @@
         below(gram_stiff[:48], 48), below(gram_mass[:48], 48), total_rows
     )
     of_x = below(rotation, m)
+    of_r = below(rotation, 2 * m) - of_x
+    of_p = rotation - of_x - of_r
     wide = nn(rotation[:, :m], jnp.concatenate([ritz_ref[...], jnp.zeros((m, 112), jnp.float32)], axis=1))
     pulled = nn(ritz_matrix, rotation)
     residual = (
-        pltpu.roll(of_x, 16, 1) + pltpu.roll(rotation - of_x, 32, 1) + pltpu.roll(wide - pulled, 80, 1)
+        pltpu.roll(of_x, 16, 1)
+        + pltpu.roll(of_r, 96, 1)
+        + pltpu.roll(of_p, 16, 1)
+        + pltpu.roll(wide - pulled, 64, 1)
     )
     basis = jnp.concatenate([rotation, residual, rotation - of_x], axis=0)
     rotation, ritz_matrix = rayleigh_ritz(
         projected(basis, gram_stiff), projected(basis, gram_mass), total_rows
     )
-    coeffs_ref[...] = pair_coefficients(rotation, basis)
     out_ref[...] = ritz_matrix
-
-
-def coefficients(kernel, total_rows, *operands):
+    coeffs = pair_coefficients(rotation, basis)
+    for c in chunks(own_ref.shape[1]):
+        pair = nn3(coeffs, jnp.concatenate([own_ref[:, c], ar_ref[:, c]], axis=0))
+        modes_ref[:, c] = pair[:m]
+        directions_ref[:, c] = pair[m:]
+
+
+def shape(*dims):
+    return jax.ShapeDtypeStruct(dims, jnp.float32)
+
+
+def params():
+    return pltpu.CompilerParams(vmem_limit_bytes=VMEM)
+
+
+def on_blocks(kernel, stepped, whole, scratch, mask, tiles, *operands):
+    width = tiles.shape[0] * TILE
     return pl.pallas_call(
-        functools.partial(kernel, total_rows),
-        out_shape=(
-            jax.ShapeDtypeStruct((32, 128), jnp.float32),
-            jax.ShapeDtypeStruct((16, 16), jnp.float32),
-        ),
-        compiler_params=pltpu.CompilerParams(vmem_limit_bytes=16 * 1024 * 1024),
+        kernel,
+        grid=(tiles.shape[0] // STEP_BLOCKS,),
+        in_specs=[
+            pl.BlockSpec(memory_space=pltpu.SMEM),
+            pl.BlockSpec((STEP_BLOCKS, 3, TILE, TILE), lambda i: (i, 0, 0, 0)),
+        ]
+        + [pl.BlockSpec(o.shape, lambda i: (0, 0)) for o in operands],
+        out_specs=[pl.BlockSpec((r, STEP), lambda i: (0, i)) for r in stepped]
+        + [pl.BlockSpec(w, lambda i: (0, 0)) for w in whole],
+        out_shape=[shape(r, width) for r in stepped] + [shape(*w) for w in whole],
+        scratch_shapes=scratch,
+        compiler_params=params(),
         name=kernel.__name__,
-    )(*operands)
-
-
-def packed(gram_stiff, gram_mass):
-    size = gram_stiff.shape[0]
-    low = jnp.tril(jnp.ones((size, size), bool), -1)
-    both = jnp.where(low, gram_stiff, gram_mass)
-    return jnp.concatenate([both, jnp.broadcast_to(jnp.diagonal(gram_stiff)[None], (8, size))])
+    )(mask, tiles, *operands)
 
 
 def on_device(stiff_tiles, tile_mask, edge_star, start_modes, start_directions):
-    m = start_modes.shape[0]
-    total_rows = edge_star.shape[0] * lax.axis_size(SLAB)
+    m, width = start_modes.shape
+    total_rows = width * lax.axis_size(SLAB)
     star = edge_star[None, :]
-    fields = jnp.concatenate(
-        [start_modes, start_directions, start_modes * star, jnp.broadcast_to(star, (8, star.shape[1]))]
-    )
-    fields = with_halo(fields)
-    modes, directions, mass_modes = fields[:m], fields[m : 2 * m], fields[2 * m : 3 * m]
-    star_ext = fields[3 * m : 3 * m + 1]
-    applied = band(fields[: 3 * m], stiff_tiles, tile_mask)
-    applied_modes = with_halo(applied[:m])
-    twice = band(applied_modes, stiff_tiles, tile_mask)
-
-    basis = jnp.concatenate([modes, applied_modes, mass_modes, directions])
-    own = basis[:, TILE:-TILE]
-    rest = jnp.concatenate([twice, applied[2 * m : 3 * m], applied[m : 2 * m]])
-    applied_own = jnp.concatenate([applied[:m], rest])
-    gram_stiff = gram(own, applied_own)
-    gram_mass = gram(own, own * star)
-    sums = slab_sum(jnp.concatenate([symmetric(gram_stiff), symmetric(gram_mass)], axis=1))
-    applied_basis = jnp.concatenate([applied_modes, with_halo(rest)])
-    coeffs, ritz_matrix = coefficients(first_kernel, total_rows, sums)
-
-    coeffs = coeffs[:, : 4 * m]
-    pair = product(coeffs, basis)
-    applied_pair = product(coeffs, applied_basis)
-    modes, directions = pair[:m], pair[m:]
-    mass_modes = modes * star_ext
-    residual = applied_pair[:m] - product(ritz_matrix, mass_modes)
-    fields = jnp.concatenate(
-        [residual, applied_pair[m:], mass_modes, residual * star_ext, directions * star_ext]
-    )
-    applied = band(fields, stiff_tiles, tile_mask)
-    applied_residual = applied[:m]
-    twice = band(with_halo(applied_residual), stiff_tiles, tile_mask)
-    inner = slice(TILE, -TILE)
-    own = jnp.concatenate(
-        [
-            modes[:, inner],
-            residual[:, inner],
-            directions[:, inner],
-            applied_residual,
-            fields[m:, inner],
-        ]
-    )
-    applied_own = jnp.concatenate(
-        [applied_pair[:m, inner], applied_residual, applied_pair[m:, inner], twice, applied[m:]]
-    )
-    gram_stiff = symmetric(gram(own, applied_own))
-    gram_mass = symmetric(gram(own, own * star))
-    sums = slab_sum(packed(gram_stiff, gram_mass))
-    coeffs, ritz_matrix = coefficients(last_kernel, total_rows, sums, ritz_matrix)
-    result = product(coeffs, own)
-    return (result[:m], result[m:], ritz_matrix)
+
+    def edge(at):
+        tail = jnp.broadcast_to(star[:, at], (8, TILE))
+        return jnp.concatenate([start_modes[:, at], start_directions[:, at], tail])
+
+    def parts(rows, halos):
+        return pltpu.VMEM((2 * rows, width + halos * TILE), jnp.bfloat16)
+
+    left = [from_left(edge(slice(width - TILE, width)))]
+    right = [from_right(edge(slice(0, TILE)))]
+    vectors = (start_modes, start_directions, star)
+    applied, other, low, high = on_blocks(
+        start_kernel, (m, 2 * m), ((m, TILE),) * 2, [parts(3 * m, 2)],
+        tile_mask, stiff_tiles, *vectors, left[0], right[0],
+    )
+    left.append(from_left(low))
+    right.append(from_right(high))
+    twice, sums, low, high = on_blocks(
+        gram_kernel, (m,), ((4 * m, 128), (3 * m, TILE), (3 * m, TILE)),
+        [parts(m, 2), pltpu.VMEM((8 * m, 256), jnp.float32), pltpu.VMEM((3 * m, STEP), jnp.float32)],
+        tile_mask, stiff_tiles, *vectors, applied, other, left[1], right[1],
+    )
+    left.append(from_left(low))
+    right.append(from_right(high))
+    sums = slab_sum(sums)
+    coeffs, ritz_matrix = pl.pallas_call(
+        functools.partial(first_kernel, total_rows),
+        out_shape=(shape(2 * m, 128), shape(m, m)),
+        compiler_params=params(),
+        name="first_kernel",
+    )(sums)
+    own, applied_residual, applied, other, high = on_blocks(
+        middle_kernel, (7 * m, m, m, 4 * m), ((m, TILE),),
+        [parts(5 * m, 2), pltpu.VMEM((8 * m, width), jnp.float32)],
+        tile_mask, stiff_tiles, coeffs, ritz_matrix, *vectors, applied, twice, other, *left, *right,
+    )
+    (sums,) = on_blocks(
+        pack_kernel, (), ((8 * m + 8, 128),),
+        [parts(m, 1)] + [pltpu.VMEM((16 * m, 256), jnp.float32)] * 2,
+        tile_mask, stiff_tiles, star, own, applied_residual, applied, other, from_right(high),
+    )
+    sums = slab_sum(sums)
+    return pl.pallas_call(
+        functools.partial(last_kernel, total_rows),
+        out_shape=(shape(m, width), shape(m, width), shape(m, m)),
+        compiler_params=params(),
+        name="last_kernel",
+    )(sums, ritz_matrix, own, applied_residual)
 
 
 def solution(mesh):

time: 176 us -> 178 us (1.011)
  blocking collectives: 53.5 us -> 78.8 us
  Pallas kernels: 30.8 us -> 55.6 us
  starting transfers between devices: 47.1 us -> 27.2 us
  matrix products: 9.73 us -> 0 us
  waiting for transfers between devices: 14 us -> 6.02 us
  local copies, waits for them, and re-layouts: 13.8 us -> 8.54 us
  other arithmetic: 4.97 us -> 0.07 us
    all_to_all x1 -> x2, blocking collectives: 19.1 us -> 44.9 us  [slab_sum(): own = lax.all_to_all(copies, 'z', 0, 0, tiled=True).sum(0)]
    pallas_call x6, Pallas kernels: 30.8 us -> 55.6 us  [the longest x4 37.5 us: on_blocks(): pl.pallas_call(kernel, grid=(tiles.shape[0] // STEP_BLOCKS,), in_specs=[p...]
    all_to_all x1 -> x0, starting transfers between devices: 16 us -> none  [slab_sum(): own = lax.all_to_all(copies, 'z', 0, 0, tiled=True).sum(0)]
    all_to_all x1 -> x0, waiting for transfers between devices: 11.5 us -> none  [slab_sum(): own = lax.all_to_all(copies, 'z', 0, 0, tiled=True).sum(0)]
    dot_general x8 -> x0, matrix products: 9.73 us -> none  [the longest x4 5.73 us: gram(): lax.dot_general(left, right, (((1,), (1,)), ((), ())), precision=lax.Prec...]
    ppermute x4 -> x3, starting transfers between devices: 13.8 us -> 10 us  [from_left(): return lax.ppermute(edge, SLAB, [(i, i + 1) for i in range(count - 1)])]
    ppermute x4, waiting for transfers between devices: 2.54 us -> 6.01 us  [from_right(): return lax.ppermute(edge, SLAB, [(i + 1, i) for i in range(count - 1)])]
    unnamed x34 -> x17, local copies, waits for them, and re-layouts: 7.75 us -> 4.96 us
  transfers between devices with their start and end apart: 10 -> 8, of which waited for: 3 -> 2; matrix products, arithmetic and copies ran while one was open for 3% -> 1% of each run, Pallas kernels for 3% -> 4%
where the time goes in v2:
time: 178 us; the launch traced here: 177 us
  blocking collectives  78.8 us (44%)
  Pallas kernels  55.6 us (31%)
  starting transfers between devices  27.2 us (15%)
  local copies, waits for them, and re-layouts  8.54 us (5%)
  waiting for transfers between devices  6.02 us (3%)
    all_to_all x2, blocking collectives, slab_sum(): own = lax.all_to_all(copies, 'z', 0, 0, tiled=True).sum(0)  44.9 us
    pallas_call x4, Pallas kernels, on_blocks(): pl.pallas_call(kernel, grid=(tiles.shape[0] // STEP_BLOCKS,), in_specs=[p...  37.5 us
    all_to_all x2, blocking collectives, slab_sum(): own = lax.all_to_all(shared, ('y', 'core'), 0, 0, tiled=True).sum(0)  21.5 us
    all_to_all x1, blocking collectives, slab_sum(): lax.all_to_all(copies, ('y', 'core'), 0, 0, tiled=True).reshape(rows.shape)  12.4 us
    ppermute x4, starting transfers between devices, from_right(): return lax.ppermute(edge, SLAB, [(i + 1, i) for i in range(count - 1)])  11.7 us
    pallas_call x1, Pallas kernels, on_device(): pl.pallas_call(functools.partial(last_kernel, total_rows), out_shape=(sha...  11.3 us
    ppermute x3, starting transfers between devices, from_left(): return lax.ppermute(edge, SLAB, [(i, i + 1) for i in range(count - 1)])  10 us
    pallas_call x1, Pallas kernels, on_device(): pl.pallas_call(functools.partial(first_kernel, total_rows), out_shape=(sh...  6.78 us
  transfers between devices with their start and end apart: 8, of which 2 were waited for; matrix products, arithmetic and copies ran while one was open for 1% of the time, Pallas kernels for 4%

profile of v2, /device:TPU:1, one launch (start us, length us, event | category | flops | bytes accessed | tf_op | source)
XLA Modules:
  0.0 177.0 jit_solution(9081844212275767213)
XLA Ops:
  0.6 0.7 slice_bitcast_fusion
  1.3 0.7 fusion
  2.1 4.6 %collective-permute-start = (f32[40,128]{1,0:T(8,128)S(1)}, f32[40,128]{1,0:T(8,128)S(1)}, u32[]{:S(2)}, u32[]{:S(2)}) collective-permute-start(f32[40,128]{1,0:T(8,128)S(1)} %pad_maximum_fusion), channel_id=1, source_target_pairs={{0,4},{4,8},{8,12},{12,16},{16,20},{20,24},{24,28},{28,32},{32,36}... | collective-permute-start | bytes 61448 | tf_op jit(solution)/shard_map/ppermute | solution.py:31
  6.7 5.5 %collective-permute-start.1 = (f32[40,128]{1,0:T(8,128)S(1)}, f32[40,128]{1,0:T(8,128)S(1)}, u32[]{:S(2)}, u32[]{:S(2)}) collective-permute-start(f32[40,128]{1,0:T(8,128)S(1)} %pad_maximum_fusion.1), channel_id=1, source_target_pairs={{4,0},{8,4},{12,8},{16,12},{20,16},{24,20},{28,24},{32,28},{36,32}... | collective-permute-start | bytes 61448 | tf_op jit(solution)/shard_map/ppermute | solution.py:36
  12.2 1.4 copy.23.mask_ref
  13.5 0.0 collective-permute-done.left_ref.rest_6_
  13.5 0.0 copy-start.1
  13.5 0.0 collective-permute-done.1.right_ref.rest_9_
  13.6 0.6 copy-done.1
  14.1 0.0 copy-start.2
  14.1 0.6 copy-done.2
  14.8 8.0 %start_kernel.1 = (f32[16,4096]{1,0:T(8,128)}, f32[32,4096]{1,0:T(8,128)}, f32[16,128]{1,0:T(8,128)}, f32[16,128]{1,0:T(8,128)}) custom-call(s32[32,2]{1,0:T(8,128)} %copy.23.mask_ref, f32[32,3,128,128]{3,2,1,0:T(8,128)} %tiles_ref.7, f32[16,4096]{1,0:T(8,128)} %rest_0_.1, f32[16,4096]{1,0:T(8,128)} %rest_1_.1, f32[1,4096]{1,0:T(1,128)} %bitcast.8, ...), custom_call_target="tpu_custom_call" | custom-call | tf_op jit(solution)/shard_map/start_kernel/pallas_call | solution.py:444
  22.7 1.9 %collective-permute-start.2 = (f32[16,128]{1,0:T(8,128)}, f32[16,128]{1,0:T(8,128)S(1)}, u32[]{:S(2)}, u32[]{:S(2)}) collective-permute-start(f32[16,128]{1,0:T(8,128)} %get-tuple-element.20), channel_id=1, source_target_pairs={{0,4},{4,8},{8,12},{12,16},{16,20},{20,24},{24,28},{28,32},{32,36}... | collective-permute-start | bytes 24584 | tf_op jit(solution)/shard_map/ppermute | solution.py:31
  24.7 2.4 %collective-permute-start.3 = (f32[16,128]{1,0:T(8,128)}, f32[16,128]{1,0:T(8,128)S(1)}, u32[]{:S(2)}, u32[]{:S(2)}) collective-permute-start(f32[16,128]{1,0:T(8,128)} %get-tuple-element.21), channel_id=1, source_target_pairs={{4,0},{8,4},{12,8},{16,12},{20,16},{24,20},{28,24},{32,28},{36,32}... | collective-permute-start | bytes 24584 | tf_op jit(solution)/shard_map/ppermute | solution.py:36
  27.1 0.0 collective-permute-done.2.rest_0_.rest_7_
  27.1 0.0 copy-start.3
  27.1 2.7 %collective-permute-done.3.rest_1_.rest_10_ = f32[16,128]{1,0:T(8,128)S(1)} collective-permute-done((f32[16,128]{1,0:T(8,128)}, f32[16,128]{1,0:T(8,128)S(1)}, u32[]{:S(2)}, u32[]{:S(2)}) %collective-permute-start.3) | collective-permute-done | bytes 8224 | tf_op jit(solution)/shard_map/ppermute | solution.py:36
  29.8 0.0 copy-start.4
  29.8 0.0 copy-done.3
  29.8 0.6 copy-done.4
  30.4 9.3 %gram_kernel.1 = (f32[16,4096]{1,0:T(8,128)}, f32[64,128]{1,0:T(8,128)}, f32[48,128]{1,0:T(8,128)}, f32[48,128]{1,0:T(8,128)}) custom-call(s32[32,2]{1,0:T(8,128)} %copy.23.mask_ref, f32[32,3,128,128]{3,2,1,0:T(8,128)} %tiles_ref.7, f32[16,4096]{1,0:T(8,128)} %rest_0_.1, f32[16,4096]{1,0:T(8,128)} %rest_1_.1, f32[1,4096]{1,0:T(1,128)} %bitcast.9, ...), custom_call_target="tpu_custom_call" | custom-call | tf_op jit(solution)/shard_map/gram_kernel/pallas_call | solution.py:444
  39.7 11.5 %all_to_all.30 = f32[8,8,128]{2,1,0:T(8,128)S(1)} all-to-all(f32[8,8,128]{2,1,0:T(8,128)} %bitcast.13), channel_id=1, replica_groups=mesh['z'=16,'y'=4,'core'=2,'x'=4] {'y','core'}, dimensions={0} | all-to-all | bytes 65536 | tf_op jit(solution)/shard_map/all_to_all | solution.py:22
  51.2 27.3 %all_to_all.31 = f32[16,8,128]{2,1,0:T(8,128)S(1)} all-to-all(f32[16,8,128]{2,1,0:T(8,128)S(1)} %broadcast_in_dim.46), channel_id=1, replica_groups=mesh['z'=16,'y'=4,'core'=2,'x'=4] {'z'}, dimensions={0} | all-to-all | bytes 131072 | tf_op jit(solution)/shard_map/all_to_all | solution.py:24
  78.6 0.6 broadcast_in_dim.47
  79.2 5.4 %all-to-all-start.2 = ((f32[8,8,128]{2,1,0:T(8,128)}), f32[8,8,128]{2,1,0:T(8,128)S(1)}, u32[]{:S(2)}, u32[]{:S(2)}) async-start(f32[8,8,128]{2,1,0:T(8,128)} %broadcast_in_dim.47), calls=%async_computation.2 | async-start | bytes 65536 | tf_op jit(solution)/shard_map/all_to_all | solution.py:26
  84.6 3.5 %collective-permute-start.4 = (f32[48,128]{1,0:T(8,128)}, f32[48,128]{1,0:T(8,128)S(1)}, u32[]{:S(2)}, u32[]{:S(2)}) collective-permute-start(f32[48,128]{1,0:T(8,128)} %get-tuple-element.26), channel_id=1, source_target_pairs={{0,4},{4,8},{8,12},{12,16},{16,20},{20,24},{24,28},{28,32},{32,36}... | collective-permute-start | bytes 73736 | tf_op jit(solution)/shard_map/ppermute | solution.py:31
  88.2 1.9 %collective-permute-start.5 = (f32[48,128]{1,0:T(8,128)}, f32[48,128]{1,0:T(8,128)S(1)}, u32[]{:S(2)}, u32[]{:S(2)}) collective-permute-start(f32[48,128]{1,0:T(8,128)} %get-tuple-element.27), channel_id=1, source_target_pairs={{4,0},{8,4},{12,8},{16,12},{20,16},{24,20},{28,24},{32,28},{36,32}... | collective-permute-start | bytes 73736 | tf_op jit(solution)/shard_map/ppermute | solution.py:36
  90.1 0.0 all-to-all-done.2
  90.1 0.0 copy-start
  90.1 0.6 copy-done
  90.7 6.8 %first_kernel.1 = (f32[32,128]{1,0:T(8,128)}, f32[16,16]{1,0:T(8,128)}) custom-call(f32[64,128]{1,0:T(8,128)} %bitcast.12), custom_call_target="tpu_custom_call" | custom-call | tf_op jit(solution)/shard_map/first_kernel/pallas_call | solution.py:490
  97.5 0.0 collective-permute-done.4.rest_8_
  97.5 0.0 copy-start.5
  97.5 0.0 collective-permute-done.5.rest_11_
  97.5 0.0 copy-start.6
  97.5 0.6 copy-done.5
  98.1 0.0 copy-done.6
  98.1 10.9 %middle_kernel.1 = (f32[112,4096]{1,0:T(8,128)}, f32[16,4096]{1,0:T(8,128)}, f32[16,4096]{1,0:T(8,128)}, f32[64,4096]{1,0:T(8,128)}, f32[16,128]{1,0:T(8,128)}) custom-call(s32[32,2]{1,0:T(8,128)} %copy.23.mask_ref, f32[32,3,128,128]{3,2,1,0:T(8,128)} %tiles_ref.7, f32[32,128]{1,0:T(8,128)} %get-tuple-element.23.coeffs_ref, ...), custom_call_target="tpu_custom_call" | custom-call | tf_op jit(solution)/shard_map/middle_kernel/pallas_call | solution.py:444
  109.0 1.9 %collective-permute-start.6 = (f32[16,128]{1,0:T(8,128)}, f32[16,128]{1,0:T(8,128)S(1)}, u32[]{:S(2)}, u32[]{:S(2)}) collective-permute-start(f32[16,128]{1,0:T(8,128)} %get-tuple-element.32), channel_id=1, source_target_pairs={{4,0},{8,4},{12,8},{16,12},{20,16},{24,20},{28,24},{32,28},{36,32}... | collective-permute-start | bytes 24584 | tf_op jit(solution)/shard_map/ppermute | solution.py:36
  110.9 3.3 %collective-permute-done.6.right_ref = f32[16,128]{1,0:T(8,128)S(1)} collective-permute-done((f32[16,128]{1,0:T(8,128)}, f32[16,128]{1,0:T(8,128)S(1)}, u32[]{:S(2)}, u32[]{:S(2)}) %collective-permute-start.6) | collective-permute-done | bytes 8224 | tf_op jit(solution)/shard_map/ppermute | solution.py:36
  114.2 0.0 copy-start.7
  114.2 0.6 copy-done.7
  114.8 9.3 %pack_kernel.1 = f32[136,128]{1,0:T(8,128)} custom-call(s32[32,2]{1,0:T(8,128)} %copy.23.mask_ref, f32[32,3,128,128]{3,2,1,0:T(8,128)} %tiles_ref.7, f32[1,4096]{1,0:T(1,128)} %bitcast.11, f32[112,4096]{1,0:T(8,128)} %get-tuple-element.28.own_ref, f32[16,4096]{1,0:T(8,128)} %get-tuple-element.29.ar_ref, f32[16,4096]{1,0:T(8,128)} %get-tuple-element.30.ax_ref, ...), custom_call_target="tpu_custom_call" | custom-call | tf_op jit(solution)/shard_map/pack_kernel/pallas_call | solution.py:444
  124.1 0.9 reshape.24
  125.0 10.0 %all_to_all.32 = f32[8,17,128]{2,1,0:T(8,128)S(1)} all-to-all(f32[8,17,128]{2,1,0:T(8,128)S(1)} %reshape.24), channel_id=1, replica_groups=mesh['z'=16,'y'=4,'core'=2,'x'=4] {'y','core'}, dimensions={0} | all-to-all | bytes 139264 | tf_op jit(solution)/shard_map/all_to_all | solution.py:22
  135.1 17.6 %all_to_all.33 = f32[16,17,128]{2,1,0:T(8,128)S(1)} all-to-all(f32[16,17,128]{2,1,0:T(8,128)S(1)} %broadcast_in_dim.48), channel_id=1, replica_groups=mesh['z'=16,'y'=4,'core'=2,'x'=4] {'z'}, dimensions={0} | all-to-all | bytes 278528 | tf_op jit(solution)/shard_map/all_to_all | solution.py:24
  152.7 12.4 %all_to_all.34 = f32[8,17,128]{2,1,0:T(8,128)S(1)} all-to-all(f32[8,17,128]{2,1,0:T(8,128)S(1)} %broadcast_in_dim.49), channel_id=1, replica_groups=mesh['z'=16,'y'=4,'core'=2,'x'=4] {'y','core'}, dimensions={0} | all-to-all | bytes 139264 | tf_op jit(solution)/shard_map/all_to_all | solution.py:26
  165.0 0.6 reshape.25.sums_ref
  165.6 11.3 %last_kernel.1 = (f32[16,4096]{1,0:T(8,128)}, f32[16,4096]{1,0:T(8,128)}, f32[16,16]{1,0:T(8,128)}) custom-call(f32[136,128]{1,0:T(8,128)} %reshape.25.sums_ref, f32[16,16]{1,0:T(8,128)} %get-tuple-element.24.ritz_ref, f32[112,4096]{1,0:T(8,128)} %get-tuple-element.28.own_ref, f32[16,4096]{1,0:T(8,128)} %get-tuple-element.29.ar_ref), custom_call_target="tpu_custom_call" | custom-call | tf_op jit(solution)/shard_map/last_kernel/pallas_call | solution.py:507
  (11 shorter events, 0.1 us)
Async XLA Ops:
  2.1 11.5 %collective-permute-start = (f32[40,128]{1,0:T(8,128)S(1)}, f32[40,128]{1,0:T(8,128)S(1)}, u32[]{:S(2)}, u32[]{:S(2)}) collective-permute-start(f32[40,128]{1,0:T(8,128)S(1)} %pad_maximum_fusion), channel_id=1, source_target_pairs={{0,4},{4,8},{8,12},{12,16},{16,20},{20,24},{24,28},{28,32},{32,36}... | collective-permute-start | bytes 61448 | tf_op jit(solution)/shard_map/ppermute | solution.py:31
  6.7 6.9 %collective-permute-start.1 = (f32[40,128]{1,0:T(8,128)S(1)}, f32[40,128]{1,0:T(8,128)S(1)}, u32[]{:S(2)}, u32[]{:S(2)}) collective-permute-start(f32[40,128]{1,0:T(8,128)S(1)} %pad_maximum_fusion.1), channel_id=1, source_target_pairs={{4,0},{8,4},{12,8},{16,12},{20,16},{24,20},{28,24},{32,28},{36,32}... | collective-permute-start | bytes 61448 | tf_op jit(solution)/shard_map/ppermute | solution.py:36
  13.5 0.6 copy-start.1
  14.1 0.6 copy-start.2
  22.7 4.3 %collective-permute-start.2 = (f32[16,128]{1,0:T(8,128)}, f32[16,128]{1,0:T(8,128)S(1)}, u32[]{:S(2)}, u32[]{:S(2)}) collective-permute-start(f32[16,128]{1,0:T(8,128)} %get-tuple-element.20), channel_id=1, source_target_pairs={{0,4},{4,8},{8,12},{12,16},{16,20},{20,24},{24,28},{28,32},{32,36}... | collective-permute-start | bytes 24584 | tf_op jit(solution)/shard_map/ppermute | solution.py:31
  24.7 5.2 %collective-permute-start.3 = (f32[16,128]{1,0:T(8,128)}, f32[16,128]{1,0:T(8,128)S(1)}, u32[]{:S(2)}, u32[]{:S(2)}) collective-permute-start(f32[16,128]{1,0:T(8,128)} %get-tuple-element.21), channel_id=1, source_target_pairs={{4,0},{8,4},{12,8},{16,12},{20,16},{24,20},{28,24},{32,28},{36,32}... | collective-permute-start | bytes 24584 | tf_op jit(solution)/shard_map/ppermute | solution.py:36
  27.1 2.8 %copy-start.3 = (f32[16,128]{1,0:T(8,128)}, f32[16,128]{1,0:T(8,128)S(1)}, u32[]{:S(2)}) copy-start(f32[16,128]{1,0:T(8,128)S(1)} %collective-permute-done.2.rest_0_.rest_7_) | copy-start | bytes 24580
  29.8 0.6 copy-start.4
  79.2 10.9 %all-to-all-start.2 = ((f32[8,8,128]{2,1,0:T(8,128)}), f32[8,8,128]{2,1,0:T(8,128)S(1)}, u32[]{:S(2)}, u32[]{:S(2)}) async-start(f32[8,8,128]{2,1,0:T(8,128)} %broadcast_in_dim.47), calls=%async_computation.2 | async-start | bytes 65536 | tf_op jit(solution)/shard_map/all_to_all | solution.py:26
  84.6 12.9 %collective-permute-start.4 = (f32[48,128]{1,0:T(8,128)}, f32[48,128]{1,0:T(8,128)S(1)}, u32[]{:S(2)}, u32[]{:S(2)}) collective-permute-start(f32[48,128]{1,0:T(8,128)} %get-tuple-element.26), channel_id=1, source_target_pairs={{0,4},{4,8},{8,12},{12,16},{16,20},{20,24},{24,28},{28,32},{32,36}... | collective-permute-start | bytes 73736 | tf_op jit(solution)/shard_map/ppermute | solution.py:31
  88.2 9.3 %collective-permute-start.5 = (f32[48,128]{1,0:T(8,128)}, f32[48,128]{1,0:T(8,128)S(1)}, u32[]{:S(2)}, u32[]{:S(2)}) collective-permute-start(f32[48,128]{1,0:T(8,128)} %get-tuple-element.27), channel_id=1, source_target_pairs={{4,0},{8,4},{12,8},{16,12},{20,16},{24,20},{28,24},{32,28},{36,32}... | collective-permute-start | bytes 73736 | tf_op jit(solution)/shard_map/ppermute | solution.py:36
  90.1 0.6 copy-start
  97.5 0.6 copy-start.5
  97.5 0.6 copy-start.6
  109.0 5.2 %collective-permute-start.6 = (f32[16,128]{1,0:T(8,128)}, f32[16,128]{1,0:T(8,128)S(1)}, u32[]{:S(2)}, u32[]{:S(2)}) collective-permute-start(f32[16,128]{1,0:T(8,128)} %get-tuple-element.32), channel_id=1, source_target_pairs={{4,0},{8,4},{12,8},{16,12},{20,16},{24,20},{28,24},{32,28},{36,32}... | collective-permute-start | bytes 24584 | tf_op jit(solution)/shard_map/ppermute | solution.py:36
  114.2 0.6 copy-start.7

commit v3 on v2

--- a/solution.py
+++ b/solution.py
@@ -10,9 +10,9 @@
 
 SLAB = ("z", "y", "core")
 TILE = 128
-STEP_BLOCKS = 4
+STEP_BLOCKS = 8
 STEP = STEP_BLOCKS * TILE
-VMEM = 56 * 1024 * 1024
+VMEM = 20 * 1024 * 1024
 WIDTH = 4
 
 
@@ -392,19 +392,36 @@
         stiff, mass = folded(stiff_ref[...]), folded(mass_ref[...])
         row, lane = sublanes(128), lanes(128)
         stiff = jnp.where((row >= 112) & (lane >= 112), 0.5 * (stiff + stiff.T), stiff)
-        sums_ref[:128] = jnp.where(row > lane, stiff, mass)
-        along = jnp.sum(jnp.where(row == lane, stiff, 0.0), axis=0, keepdims=True)
-        sums_ref[128:] = jnp.broadcast_to(along, (8, 128))
+        sums_ref[...] = jnp.where(row > lane, stiff, mass)
+        along = jnp.sum(jnp.where(row == lane, stiff, 0.0), axis=1, keepdims=True)
+        placed = nn(of_groups(8, 128), jnp.where(lane == 64 + row % 16, along, 0.0))
+        taken = lanes(8)
+        taken = (taken >= 64) & (taken < 80)
+        sums_ref[16:24] = jnp.where(taken, placed, sums_ref[16:24])
+
+
+def of_groups(groups, size):
+    row = lax.broadcasted_iota(jnp.int32, (groups, size), 0)
+    column = lax.broadcasted_iota(jnp.int32, (groups, size), 1)
+    return jnp.where(column // 16 == row, 1.0, 0.0).astype(jnp.float32)
 
 
 def last_kernel(total_rows, sums_ref, ritz_ref, own_ref, ar_ref, modes_ref, directions_ref, out_ref):
     m = 16
-    both = sums_ref[:128]
+    both = sums_ref[...]
     turned = both.T
     row, lane = sublanes(128), lanes(128)
-    stiff_diagonal = jnp.broadcast_to(sums_ref[128:129], (128, 128))
-    gram_stiff = jnp.where(row > lane, both, jnp.where(row < lane, turned, stiff_diagonal))
+    group = lax.broadcasted_iota(jnp.int32, (128, 8), 0) // 16
+    member = lax.broadcasted_iota(jnp.int32, (128, 8), 1)
+    spread = nn(jnp.where(group == member, 1.0, 0.0).astype(jnp.float32), both[16:24])
+    along = jnp.sum(jnp.where(lane == 64 + row % 16, spread, 0.0), axis=1, keepdims=True)
+    gram_stiff = jnp.where(row > lane, both, jnp.where(row < lane, turned, along))
     gram_mass = jnp.where(row > lane, turned, both)
+    of_r = jnp.where((lanes(m) >= 64) & (lanes(m) < 80), pltpu.roll(gram_mass[80:96], 64, 1), gram_mass[16:32])
+    of_mx = jnp.where((lanes(m) >= 16) & (lanes(m) < 32), pltpu.roll(gram_mass[:16], 64, 1), gram_mass[64:80])
+    gram_mass = jnp.concatenate(
+        [gram_mass[:16], of_r, gram_mass[32:64], of_mx, gram_mass[80:]], axis=0
+    )
     rotation, ritz_matrix = rayleigh_ritz(
         below(gram_stiff[:48], 48), below(gram_mass[:48], 48), total_rows
     )
@@ -499,7 +516,7 @@
         tile_mask, stiff_tiles, coeffs, ritz_matrix, *vectors, applied, twice, other, *left, *right,
     )
     (sums,) = on_blocks(
-        pack_kernel, (), ((8 * m + 8, 128),),
+        pack_kernel, (), ((8 * m, 128),),
         [parts(m, 1)] + [pltpu.VMEM((16 * m, 256), jnp.float32)] * 2,
         tile_mask, stiff_tiles, star, own, applied_residual, applied, other, from_right(high),
     )

time: 178 us -> 160 us (0.90)
  Pallas kernels: 55.6 us -> 33.9 us
  local copies, waits for them, and re-layouts: 8.54 us -> 12.7 us
    pallas_call x4, Pallas kernels: 37.5 us -> 18.1 us  [on_blocks(): pl.pallas_call(kernel, grid=(tiles.shape[0] // STEP_BLOCKS,), in_specs=[p...]
    unnamed x17 -> x21, local copies, waits for them, and re-layouts: 4.96 us -> 10.6 us
  transfers between devices with their start and end apart: 8 -> 8, of which waited for: 2 -> 2; matrix products, arithmetic and copies ran while one was open for 1% -> 0% of each run, Pallas kernels for 4% -> 3%
where the time goes in v3:
time: 160 us; the launch traced here: 159 us
  blocking collectives  78.4 us (49%)
  Pallas kernels  33.9 us (21%)
  starting transfers between devices  27.2 us (17%)
  local copies, waits for them, and re-layouts  12.7 us (8%)
  waiting for transfers between devices  5.65 us (4%)
    all_to_all x2, blocking collectives, slab_sum(): own = lax.all_to_all(copies, 'z', 0, 0, tiled=True).sum(0)  45.6 us
    all_to_all x2, blocking collectives, slab_sum(): own = lax.all_to_all(shared, ('y', 'core'), 0, 0, tiled=True).sum(0)  21.8 us
    pallas_call x4, Pallas kernels, on_blocks(): pl.pallas_call(kernel, grid=(tiles.shape[0] // STEP_BLOCKS,), in_specs=[p...  18.1 us
    ppermute x4, starting transfers between devices, from_right(): return lax.ppermute(edge, SLAB, [(i + 1, i) for i in range(count - 1)])  11.7 us
    all_to_all x1, blocking collectives, slab_sum(): lax.all_to_all(copies, ('y', 'core'), 0, 0, tiled=True).reshape(rows.shape)  11 us
    unnamed x21, local copies, waits for them, and re-layouts  10.6 us
    pallas_call x1, Pallas kernels, on_device(): pl.pallas_call(functools.partial(last_kernel, total_rows), out_shape=(sha...  10.3 us
    ppermute x3, starting transfers between devices, from_left(): return lax.ppermute(edge, SLAB, [(i, i + 1) for i in range(count - 1)])  10 us
  transfers between devices with their start and end apart: 8, of which 2 were waited for; matrix products, arithmetic and copies ran while one was open for 0% of the time, Pallas kernels for 3%

profile of v3, /device:TPU:1, one launch (start us, length us, event | category | flops | bytes accessed | tf_op | source)
XLA Modules:
  0.0 158.7 jit_solution(11734093327781281610)
XLA Ops:
  0.6 0.7 slice_bitcast_fusion
  1.3 0.7 fusion
  2.1 4.6 %collective-permute-start = (f32[40,128]{1,0:T(8,128)S(1)}, f32[40,128]{1,0:T(8,128)S(1)}, u32[]{:S(2)}, u32[]{:S(2)}) collective-permute-start(f32[40,128]{1,0:T(8,128)S(1)} %pad_maximum_fusion), channel_id=1, source_target_pairs={{0,4},{4,8},{8,12},{12,16},{16,20},{20,24},{24,28},{28,32},{32,36}... | collective-permute-start | bytes 61448 | tf_op jit(solution)/shard_map/ppermute | solution.py:31
  6.7 5.5 %collective-permute-start.1 = (f32[40,128]{1,0:T(8,128)S(1)}, f32[40,128]{1,0:T(8,128)S(1)}, u32[]{:S(2)}, u32[]{:S(2)}) collective-permute-start(f32[40,128]{1,0:T(8,128)S(1)} %pad_maximum_fusion.1), channel_id=1, source_target_pairs={{4,0},{8,4},{12,8},{16,12},{20,16},{24,20},{28,24},{32,28},{36,32}... | collective-permute-start | bytes 61448 | tf_op jit(solution)/shard_map/ppermute | solution.py:36
  12.2 0.0 copy-start.7
  12.2 0.8 copy.15.mask_ref
  13.0 0.0 collective-permute-done.left_ref.rest_6_
  13.0 0.0 collective-permute-done.1.right_ref.rest_9_
  13.0 0.0 copy-start
  13.0 2.8 %copy-done = f32[32,3,128,128]{3,2,1,0:T(8,128)S(1)} copy-done((f32[32,3,128,128]{3,2,1,0:T(8,128)S(1)}, f32[32,3,128,128]{3,2,1,0:T(8,128)}, u32[]{:S(2)}) %copy-start) | copy-done | bytes 6291480
  15.8 0.0 copy-start.2
  15.8 0.9 copy-done.2
  16.7 0.0 copy-start.4
  16.7 0.9 copy-done.4
  17.7 0.0 copy-start.6
  17.7 0.7 copy-done.6
  18.4 0.0 copy-start.3
  18.4 0.0 copy-start.5
  18.4 3.6 %start_kernel.1 = (f32[16,4096]{1,0:T(8,128)S(1)}, f32[32,4096]{1,0:T(8,128)S(1)}, f32[16,128]{1,0:T(8,128)S(1)}, f32[16,128]{1,0:T(8,128)S(1)}) custom-call(s32[32,2]{1,0:T(8,128)S(1)} %copy.15.mask_ref, f32[32,3,128,128]{3,2,1,0:T(8,128)S(1)} %copy-done, f32[16,4096]{1,0:T(8,128)S(1)} %copy-done.2, f32[16,4096]{1,0:T(8,128)S(1)} %copy-done.4, ...), custom_call_target="tpu_custom_call" | custom-call | tf_op jit(solution)/shard_map/start_kernel/pallas_call | solution.py:461
  22.0 1.9 %collective-permute-start.2 = (f32[16,128]{1,0:T(8,128)S(1)}, f32[16,128]{1,0:T(8,128)S(1)}, u32[]{:S(2)}, u32[]{:S(2)}) collective-permute-start(f32[16,128]{1,0:T(8,128)S(1)} %get-tuple-element.20), channel_id=1, source_target_pairs={{0,4},{4,8},{8,12},{12,16},{16,20},{20,24},{24,28},{28,32},{32,36}... | collective-permute-start | bytes 24584 | tf_op jit(solution)/shard_map/ppermute | solution.py:31
  23.9 2.4 %collective-permute-start.3 = (f32[16,128]{1,0:T(8,128)S(1)}, f32[16,128]{1,0:T(8,128)S(1)}, u32[]{:S(2)}, u32[]{:S(2)}) collective-permute-start(f32[16,128]{1,0:T(8,128)S(1)} %get-tuple-element.21), channel_id=1, source_target_pairs={{4,0},{8,4},{12,8},{16,12},{20,16},{24,20},{28,24},{32,28},{36,32}... | collective-permute-start | bytes 24584 | tf_op jit(solution)/shard_map/ppermute | solution.py:36
  26.3 0.0 collective-permute-done.2.rest_0_.rest_7_
  26.4 2.5 %collective-permute-done.3.rest_1_.rest_10_ = f32[16,128]{1,0:T(8,128)S(1)} collective-permute-done((f32[16,128]{1,0:T(8,128)S(1)}, f32[16,128]{1,0:T(8,128)S(1)}, u32[]{:S(2)}, u32[]{:S(2)}) %collective-permute-start.3) | collective-permute-done | bytes 8224 | tf_op jit(solution)/shard_map/ppermute | solution.py:36
  28.9 4.8 %gram_kernel.1 = (f32[16,4096]{1,0:T(8,128)S(1)}, f32[64,128]{1,0:T(8,128)S(1)}, f32[48,128]{1,0:T(8,128)S(1)}, f32[48,128]{1,0:T(8,128)S(1)}) custom-call(s32[32,2]{1,0:T(8,128)S(1)} %copy.15.mask_ref, f32[32,3,128,128]{3,2,1,0:T(8,128)S(1)} %copy-done, f32[16,4096]{1,0:T(8,128)S(1)} %copy-done.2, f32[16,4096]{1,0:T(8,128)S(1)} %copy-done.4, ...), custom_call_target="tpu_custom_call" | custom-call | tf_op jit(solution)/shard_map/gram_kernel/pallas_call | solution.py:461
  33.7 0.0 copy-start.8
  33.7 0.7 copy-done.8
  34.4 11.9 %all_to_all.30 = f32[8,8,128]{2,1,0:T(8,128)S(1)} all-to-all(f32[8,8,128]{2,1,0:T(8,128)S(1)} %bitcast.17), channel_id=1, replica_groups=mesh['z'=16,'y'=4,'core'=2,'x'=4] {'y','core'}, dimensions={0} | all-to-all | bytes 65536 | tf_op jit(solution)/shard_map/all_to_all | solution.py:22
  46.3 27.3 %all_to_all.31 = f32[16,8,128]{2,1,0:T(8,128)S(1)} all-to-all(f32[16,8,128]{2,1,0:T(8,128)S(1)} %broadcast_in_dim.46), channel_id=1, replica_groups=mesh['z'=16,'y'=4,'core'=2,'x'=4] {'z'}, dimensions={0} | all-to-all | bytes 131072 | tf_op jit(solution)/shard_map/all_to_all | solution.py:24
  73.7 0.6 broadcast_in_dim.47
  74.3 5.4 %all-to-all-start.2 = ((f32[8,8,128]{2,1,0:T(8,128)}), f32[8,8,128]{2,1,0:T(8,128)S(1)}, u32[]{:S(2)}, u32[]{:S(2)}) async-start(f32[8,8,128]{2,1,0:T(8,128)} %broadcast_in_dim.47), calls=%async_computation.2 | async-start | bytes 65536 | tf_op jit(solution)/shard_map/all_to_all | solution.py:26
  79.7 3.5 %collective-permute-start.4 = (f32[48,128]{1,0:T(8,128)S(1)}, f32[48,128]{1,0:T(8,128)S(1)}, u32[]{:S(2)}, u32[]{:S(2)}) collective-permute-start(f32[48,128]{1,0:T(8,128)S(1)} %get-tuple-element.26), channel_id=1, source_target_pairs={{0,4},{4,8},{8,12},{12,16},{16,20},{20,24},{24,28},{28,32},{32,36}... | collective-permute-start | bytes 73736 | tf_op jit(solution)/shard_map/ppermute | solution.py:31
  83.3 1.9 %collective-permute-start.5 = (f32[48,128]{1,0:T(8,128)S(1)}, f32[48,128]{1,0:T(8,128)S(1)}, u32[]{:S(2)}, u32[]{:S(2)}) collective-permute-start(f32[48,128]{1,0:T(8,128)S(1)} %get-tuple-element.27), channel_id=1, source_target_pairs={{4,0},{8,4},{12,8},{16,12},{20,16},{24,20},{28,24},{32,28},{36,32}... | collective-permute-start | bytes 73736 | tf_op jit(solution)/shard_map/ppermute | solution.py:36
  85.2 0.0 all-to-all-done.2
  85.2 5.4 %first_kernel.1 = (f32[32,128]{1,0:T(8,128)S(1)}, f32[16,16]{1,0:T(8,128)S(1)}) custom-call(f32[64,128]{1,0:T(8,128)S(1)} %bitcast.16), custom_call_target="tpu_custom_call" | custom-call | tf_op jit(solution)/shard_map/first_kernel/pallas_call | solution.py:507
  90.6 0.0 collective-permute-done.4.rest_8_
  90.6 0.0 collective-permute-done.5.rest_11_
  90.6 0.0 copy-done.7
  90.6 0.0 copy-done.3
  90.7 0.0 copy-done.5
  90.7 0.0 copy-start.1
  90.7 2.8 %copy-done.1 = f32[32,3,128,128]{3,2,1,0:T(8,128)S(1)} copy-done((f32[32,3,128,128]{3,2,1,0:T(8,128)S(1)}, f32[32,3,128,128]{3,2,1,0:T(8,128)}, u32[]{:S(2)}) %copy-start.1) | copy-done | bytes 6291480
  93.5 0.0 copy-start.9
  93.5 0.9 copy-done.9
  94.4 5.4 %middle_kernel.1 = (f32[112,4096]{1,0:T(8,128)S(1)}, f32[16,4096]{1,0:T(8,128)S(1)}, f32[16,4096]{1,0:T(8,128)S(1)}, f32[64,4096]{1,0:T(8,128)S(1)}, f32[16,128]{1,0:T(8,128)S(1)}) custom-call(s32[32,2]{1,0:T(8,128)S(1)} %copy.15.mask_ref, f32[32,3,128,128]{3,2,1,0:T(8,128)S(1)} %copy-done.1, f32[32,128]{1,0:T(8,128)S(1)} %get-tuple-element.23.coeffs_ref, ...), custom_call_target="tpu_custom_call" | custom-call | tf_op jit(solution)/shard_map/middle_kernel/pallas_call | solution.py:461
  99.8 1.9 %collective-permute-start.6 = (f32[16,128]{1,0:T(8,128)S(1)}, f32[16,128]{1,0:T(8,128)S(1)}, u32[]{:S(2)}, u32[]{:S(2)}) collective-permute-start(f32[16,128]{1,0:T(8,128)S(1)} %get-tuple-element.32), channel_id=1, source_target_pairs={{4,0},{8,4},{12,8},{16,12},{20,16},{24,20},{28,24},{32,28},{36,32}... | collective-permute-start | bytes 24584 | tf_op jit(solution)/shard_map/ppermute | solution.py:36
  101.7 3.0 %collective-permute-done.6.right_ref = f32[16,128]{1,0:T(8,128)S(1)} collective-permute-done((f32[16,128]{1,0:T(8,128)S(1)}, f32[16,128]{1,0:T(8,128)S(1)}, u32[]{:S(2)}, u32[]{:S(2)}) %collective-permute-start.6) | collective-permute-done | bytes 8224 | tf_op jit(solution)/shard_map/ppermute | solution.py:36
  104.8 4.4 %pack_kernel.1 = f32[128,128]{1,0:T(8,128)S(1)} custom-call(s32[32,2]{1,0:T(8,128)S(1)} %copy.15.mask_ref, f32[32,3,128,128]{3,2,1,0:T(8,128)S(1)} %copy-done.1, f32[1,4096]{1,0:T(1,128)S(1)} %bitcast.13, f32[112,4096]{1,0:T(8,128)S(1)} %get-tuple-element.28.own_ref, f32[16,4096]{1,0:T(8,128)S(1)} %get-tuple-element.29.ar_ref, ...), custom_call_target="tpu_custom_call" | custom-call | tf_op jit(solution)/shard_map/pack_kernel/pallas_call | solution.py:461
  109.2 9.9 %all_to_all.32 = f32[8,16,128]{2,1,0:T(8,128)S(1)} all-to-all(f32[8,16,128]{2,1,0:T(8,128)S(1)} %bitcast.14), channel_id=1, replica_groups=mesh['z'=16,'y'=4,'core'=2,'x'=4] {'y','core'}, dimensions={0} | all-to-all | bytes 131072 | tf_op jit(solution)/shard_map/all_to_all | solution.py:22
  119.1 18.2 %all_to_all.33 = f32[16,16,128]{2,1,0:T(8,128)S(1)} all-to-all(f32[16,16,128]{2,1,0:T(8,128)S(1)} %broadcast_in_dim.48), channel_id=1, replica_groups=mesh['z'=16,'y'=4,'core'=2,'x'=4] {'z'}, dimensions={0} | all-to-all | bytes 262144 | tf_op jit(solution)/shard_map/all_to_all | solution.py:24
  137.4 11.0 %all_to_all.34 = f32[8,16,128]{2,1,0:T(8,128)S(1)} all-to-all(f32[8,16,128]{2,1,0:T(8,128)S(1)} %broadcast_in_dim.49), channel_id=1, replica_groups=mesh['z'=16,'y'=4,'core'=2,'x'=4] {'y','core'}, dimensions={0} | all-to-all | bytes 131072 | tf_op jit(solution)/shard_map/all_to_all | solution.py:26
  148.4 10.3 %last_kernel.1 = (f32[16,4096]{1,0:T(8,128)}, f32[16,4096]{1,0:T(8,128)}, f32[16,16]{1,0:T(8,128)}) custom-call(f32[128,128]{1,0:T(8,128)S(1)} %bitcast.15, f32[16,16]{1,0:T(8,128)S(1)} %get-tuple-element.24.ritz_ref, f32[112,4096]{1,0:T(8,128)S(1)} %get-tuple-element.28.own_ref, f32[16,4096]{1,0:T(8,128)S(1)} %get-tuple-element.29.ar_ref), custom_call_target="tpu_custom_call" | custom-call | tf_op jit(solution)/shard_map/last_kernel/pallas_call | solution.py:524
  (11 shorter events, 0.1 us)
Async XLA Ops:
  2.1 10.9 %collective-permute-start = (f32[40,128]{1,0:T(8,128)S(1)}, f32[40,128]{1,0:T(8,128)S(1)}, u32[]{:S(2)}, u32[]{:S(2)}) collective-permute-start(f32[40,128]{1,0:T(8,128)S(1)} %pad_maximum_fusion), channel_id=1, source_target_pairs={{0,4},{4,8},{8,12},{12,16},{16,20},{20,24},{24,28},{28,32},{32,36}... | collective-permute-start | bytes 61448 | tf_op jit(solution)/shard_map/ppermute | solution.py:31
  6.7 6.3 %collective-permute-start.1 = (f32[40,128]{1,0:T(8,128)S(1)}, f32[40,128]{1,0:T(8,128)S(1)}, u32[]{:S(2)}, u32[]{:S(2)}) collective-permute-start(f32[40,128]{1,0:T(8,128)S(1)} %pad_maximum_fusion.1), channel_id=1, source_target_pairs={{4,0},{8,4},{12,8},{16,12},{20,16},{24,20},{28,24},{32,28},{36,32}... | collective-permute-start | bytes 61448 | tf_op jit(solution)/shard_map/ppermute | solution.py:36
  12.2 78.5 %copy-start.7 = (f32[4096]{0:T(1024)S(1)}, f32[4096]{0:T(1024)}, u32[]{:S(2)}) copy-start(f32[4096]{0:T(1024)} %param.7) | copy-start | bytes 49156
  13.0 2.8 %copy-start = (f32[32,3,128,128]{3,2,1,0:T(8,128)S(1)}, f32[32,3,128,128]{3,2,1,0:T(8,128)}, u32[]{:S(2)}) copy-start(f32[32,3,128,128]{3,2,1,0:T(8,128)} %tiles_ref.7) | copy-start | bytes 18874372
  15.8 0.9 copy-start.2
  16.7 0.9 copy-start.4
  17.7 0.7 copy-start.6
  18.4 72.2 %copy-start.3 = (f32[16,4096]{1,0:T(8,128)S(1)}, f32[16,4096]{1,0:T(8,128)}, u32[]{:S(2)}) copy-start(f32[16,4096]{1,0:T(8,128)} %rest_0_.1) | copy-start | bytes 786436
  18.4 72.2 %copy-start.5 = (f32[16,4096]{1,0:T(8,128)S(1)}, f32[16,4096]{1,0:T(8,128)}, u32[]{:S(2)}) copy-start(f32[16,4096]{1,0:T(8,128)} %rest_1_.1) | copy-start | bytes 786436
  22.0 4.3 %collective-permute-start.2 = (f32[16,128]{1,0:T(8,128)S(1)}, f32[16,128]{1,0:T(8,128)S(1)}, u32[]{:S(2)}, u32[]{:S(2)}) collective-permute-start(f32[16,128]{1,0:T(8,128)S(1)} %get-tuple-element.20), channel_id=1, source_target_pairs={{0,4},{4,8},{8,12},{12,16},{16,20},{20,24},{24,28},{28,32},{32,36}... | collective-permute-start | bytes 24584 | tf_op jit(solution)/shard_map/ppermute | solution.py:31
  23.9 5.0 %collective-permute-start.3 = (f32[16,128]{1,0:T(8,128)S(1)}, f32[16,128]{1,0:T(8,128)S(1)}, u32[]{:S(2)}, u32[]{:S(2)}) collective-permute-start(f32[16,128]{1,0:T(8,128)S(1)} %get-tuple-element.21), channel_id=1, source_target_pairs={{4,0},{8,4},{12,8},{16,12},{20,16},{24,20},{28,24},{32,28},{36,32}... | collective-permute-start | bytes 24584 | tf_op jit(solution)/shard_map/ppermute | solution.py:36
  33.7 0.7 copy-start.8
  74.3 10.9 %all-to-all-start.2 = ((f32[8,8,128]{2,1,0:T(8,128)}), f32[8,8,128]{2,1,0:T(8,128)S(1)}, u32[]{:S(2)}, u32[]{:S(2)}) async-start(f32[8,8,128]{2,1,0:T(8,128)} %broadcast_in_dim.47), calls=%async_computation.2 | async-start | bytes 65536 | tf_op jit(solution)/shard_map/all_to_all | solution.py:26
  79.7 10.9 %collective-permute-start.4 = (f32[48,128]{1,0:T(8,128)S(1)}, f32[48,128]{1,0:T(8,128)S(1)}, u32[]{:S(2)}, u32[]{:S(2)}) collective-permute-start(f32[48,128]{1,0:T(8,128)S(1)} %get-tuple-element.26), channel_id=1, source_target_pairs={{0,4},{4,8},{8,12},{12,16},{16,20},{20,24},{24,28},{28,32},{32,36}... | collective-permute-start | bytes 73736 | tf_op jit(solution)/shard_map/ppermute | solution.py:31
  83.3 7.4 %collective-permute-start.5 = (f32[48,128]{1,0:T(8,128)S(1)}, f32[48,128]{1,0:T(8,128)S(1)}, u32[]{:S(2)}, u32[]{:S(2)}) collective-permute-start(f32[48,128]{1,0:T(8,128)S(1)} %get-tuple-element.27), channel_id=1, source_target_pairs={{4,0},{8,4},{12,8},{16,12},{20,16},{24,20},{28,24},{32,28},{36,32}... | collective-permute-start | bytes 73736 | tf_op jit(solution)/shard_map/ppermute | solution.py:36
  90.7 2.8 %copy-start.1 = (f32[32,3,128,128]{3,2,1,0:T(8,128)S(1)}, f32[32,3,128,128]{3,2,1,0:T(8,128)}, u32[]{:S(2)}) copy-start(f32[32,3,128,128]{3,2,1,0:T(8,128)} %tiles_ref.7) | copy-start | bytes 18874372
  93.5 0.9 copy-start.9
  99.8 5.0 %collective-permute-start.6 = (f32[16,128]{1,0:T(8,128)S(1)}, f32[16,128]{1,0:T(8,128)S(1)}, u32[]{:S(2)}, u32[]{:S(2)}) collective-permute-start(f32[16,128]{1,0:T(8,128)S(1)} %get-tuple-element.32), channel_id=1, source_target_pairs={{4,0},{8,4},{12,8},{16,12},{20,16},{24,20},{28,24},{32,28},{36,32}... | collective-permute-start | bytes 24584 | tf_op jit(solution)/shard_map/ppermute | solution.py:36

commit v4 on v3

--- a/solution.py
+++ b/solution.py
@@ -13,7 +13,7 @@
 STEP_BLOCKS = 8
 STEP = STEP_BLOCKS * TILE
 VMEM = 20 * 1024 * 1024
-WIDTH = 4
+WIDTH = 8
 
 
 def slab_sum(rows):
@@ -247,6 +247,10 @@
     parts_ref[half + row : half + row + count, start : start + width] = low
 
 
+def views(fields_ref):
+    return fields_ref.at[:16], fields_ref.at[16:32], fields_ref.at[32:33]
+
+
 def chunks(width):
     return [slice(c, c + STEP) for c in range(0, width, STEP)]
 
@@ -261,9 +265,10 @@
         low_ref[...] = ref[:, STEP - TILE :]
 
 
-def start_kernel(mask_ref, tiles_ref, x_ref, p_ref, star_ref, left_ref, right_ref, *rest):
+def start_kernel(mask_ref, tiles_ref, fields_ref, left_ref, right_ref, *rest):
     ax_ref, other_ref, ax_low, ax_high, parts_ref = rest
-    step, width = pl.program_id(0), x_ref.shape[1]
+    x_ref, p_ref, star_ref = views(fields_ref)
+    step, width = pl.program_id(0), fields_ref.shape[1]
 
     @pl.when(step == 0)
     def _():
@@ -284,8 +289,9 @@
     edges_of(ax_ref, step, ax_low, ax_high)
 
 
-def gram_kernel(mask_ref, tiles_ref, x_ref, p_ref, star_ref, ax_ref, other_ref, *rest):
+def gram_kernel(mask_ref, tiles_ref, fields_ref, ax_ref, other_ref, *rest):
     left_ref, right_ref, twice_ref, sums_ref, low_ref, high_ref, parts_ref, total_ref, edge_ref = rest
+    x_ref, p_ref, star_ref = views(fields_ref)
     step, width = pl.program_id(0), ax_ref.shape[1]
 
     @pl.when(step == 0)
@@ -490,16 +496,17 @@
     left = [from_left(edge(slice(width - TILE, width)))]
     right = [from_right(edge(slice(0, TILE)))]
     vectors = (start_modes, start_directions, star)
+    fields = jnp.concatenate([start_modes, start_directions, jnp.broadcast_to(star, (8, width))])
     applied, other, low, high = on_blocks(
         start_kernel, (m, 2 * m), ((m, TILE),) * 2, [parts(3 * m, 2)],
-        tile_mask, stiff_tiles, *vectors, left[0], right[0],
+        tile_mask, stiff_tiles, fields, left[0], right[0],
     )
     left.append(from_left(low))
     right.append(from_right(high))
     twice, sums, low, high = on_blocks(
         gram_kernel, (m,), ((4 * m, 128), (3 * m, TILE), (3 * m, TILE)),
         [parts(m, 2), pltpu.VMEM((8 * m, 256), jnp.float32), pltpu.VMEM((3 * m, STEP), jnp.float32)],
-        tile_mask, stiff_tiles, *vectors, applied, other, left[1], right[1],
+        tile_mask, stiff_tiles, fields, applied, other, left[1], right[1],
     )
     left.append(from_left(low))
     right.append(from_right(high))

time: 160 us -> 157 us (0.981)
  local copies, waits for them, and re-layouts: 12.7 us -> 10.8 us
    unnamed x21 -> x15, local copies, waits for them, and re-layouts: 10.6 us -> 7.99 us
  transfers between devices with their start and end apart: 8 -> 8, of which waited for: 2 -> 2; matrix products, arithmetic and copies ran while one was open for 0% -> 2% of each run, Pallas kernels for 3% -> 3%
where the time goes in v4:
time: 157 us; the launch traced here: 156 us
  blocking collectives  78.3 us (50%)
  Pallas kernels  32.4 us (21%)
  starting transfers between devices  27.2 us (17%)
  local copies, waits for them, and re-layouts  10.8 us (7%)
  waiting for transfers between devices  5.61 us (4%)
    all_to_all x2, blocking collectives, slab_sum(): own = lax.all_to_all(copies, 'z', 0, 0, tiled=True).sum(0)  45.9 us
    all_to_all x2, blocking collectives, slab_sum(): own = lax.all_to_all(shared, ('y', 'core'), 0, 0, tiled=True).sum(0)  21.5 us
    pallas_call x4, Pallas kernels, on_blocks(): pl.pallas_call(kernel, grid=(tiles.shape[0] // STEP_BLOCKS,), in_specs=[p...  18.1 us
    ppermute x4, starting transfers between devices, from_right(): return lax.ppermute(edge, SLAB, [(i + 1, i) for i in range(count - 1)])  11.7 us
    all_to_all x1, blocking collectives, slab_sum(): lax.all_to_all(copies, ('y', 'core'), 0, 0, tiled=True).reshape(rows.shape)  11 us
    ppermute x3, starting transfers between devices, from_left(): return lax.ppermute(edge, SLAB, [(i, i + 1) for i in range(count - 1)])  10 us
    pallas_call x1, Pallas kernels, on_device(): pl.pallas_call(functools.partial(last_kernel, total_rows), out_shape=(sha...  9.48 us
    unnamed x15, local copies, waits for them, and re-layouts  7.99 us
  transfers between devices with their start and end apart: 8, of which 2 were waited for; matrix products, arithmetic and copies ran while one was open for 2% of the time, Pallas kernels for 3%

profile of v4, /device:TPU:1, one launch (start us, length us, event | category | flops | bytes accessed | tf_op | source)
XLA Modules:
  0.0 156.4 jit_solution(18047476676248883839)
XLA Ops:
  0.6 0.7 slice_bitcast_fusion
  1.3 0.7 fusion
  2.1 4.6 %collective-permute-start = (f32[40,128]{1,0:T(8,128)S(1)}, f32[40,128]{1,0:T(8,128)S(1)}, u32[]{:S(2)}, u32[]{:S(2)}) collective-permute-start(f32[40,128]{1,0:T(8,128)S(1)} %pad_maximum_fusion.1), channel_id=1, source_target_pairs={{0,4},{4,8},{8,12},{12,16},{16,20},{20,24},{24,28},{28,32},{32,36}... | collective-permute-start | bytes 61448 | tf_op jit(solution)/shard_map/ppermute | solution.py:31
  6.7 5.5 %collective-permute-start.1 = (f32[40,128]{1,0:T(8,128)S(1)}, f32[40,128]{1,0:T(8,128)S(1)}, u32[]{:S(2)}, u32[]{:S(2)}) collective-permute-start(f32[40,128]{1,0:T(8,128)S(1)} %pad_maximum_fusion.2), channel_id=1, source_target_pairs={{4,0},{8,4},{12,8},{16,12},{20,16},{24,20},{28,24},{32,28},{36,32}... | collective-permute-start | bytes 61448 | tf_op jit(solution)/shard_map/ppermute | solution.py:36
  12.2 0.7 broadcast_in_dim.21
  12.9 1.1 pad_maximum_fusion.fields_ref
  14.0 0.0 copy-start.6
  14.0 0.8 copy.15.mask_ref
  14.8 0.0 collective-permute-done.left_ref.rest_6_
  14.8 0.0 collective-permute-done.1.right_ref.rest_9_
  14.8 0.0 copy-start
  14.8 2.8 %copy-done = f32[32,3,128,128]{3,2,1,0:T(8,128)S(1)} copy-done((f32[32,3,128,128]{3,2,1,0:T(8,128)S(1)}, f32[32,3,128,128]{3,2,1,0:T(8,128)}, u32[]{:S(2)}) %copy-start) | copy-done | bytes 6291480
  17.6 0.0 copy-start.2
  17.6 0.0 copy-start.3
  17.6 3.6 %start_kernel.1 = (f32[16,4096]{1,0:T(8,128)S(1)}, f32[32,4096]{1,0:T(8,128)S(1)}, f32[16,128]{1,0:T(8,128)S(1)}, f32[16,128]{1,0:T(8,128)S(1)}) custom-call(s32[32,2]{1,0:T(8,128)S(1)} %copy.15.mask_ref, f32[32,3,128,128]{3,2,1,0:T(8,128)S(1)} %copy-done, f32[40,4096]{1,0:T(8,128)S(1)} %pad_maximum_fusion.fields_ref, ...), custom_call_target="tpu_custom_call" | custom-call | tf_op jit(solution)/shard_map/start_kernel/pallas_call | solution.py:467
  21.2 1.9 %collective-permute-start.2 = (f32[16,128]{1,0:T(8,128)S(1)}, f32[16,128]{1,0:T(8,128)S(1)}, u32[]{:S(2)}, u32[]{:S(2)}) collective-permute-start(f32[16,128]{1,0:T(8,128)S(1)} %get-tuple-element.20), channel_id=1, source_target_pairs={{0,4},{4,8},{8,12},{12,16},{16,20},{20,24},{24,28},{28,32},{32,36}... | collective-permute-start | bytes 24584 | tf_op jit(solution)/shard_map/ppermute | solution.py:31
  23.1 2.4 %collective-permute-start.3 = (f32[16,128]{1,0:T(8,128)S(1)}, f32[16,128]{1,0:T(8,128)S(1)}, u32[]{:S(2)}, u32[]{:S(2)}) collective-permute-start(f32[16,128]{1,0:T(8,128)S(1)} %get-tuple-element.21), channel_id=1, source_target_pairs={{4,0},{8,4},{12,8},{16,12},{20,16},{24,20},{28,24},{32,28},{36,32}... | collective-permute-start | bytes 24584 | tf_op jit(solution)/shard_map/ppermute | solution.py:36
  25.5 0.0 collective-permute-done.2.rest_0_.rest_7_
  25.5 2.5 %collective-permute-done.3.rest_1_.rest_10_ = f32[16,128]{1,0:T(8,128)S(1)} collective-permute-done((f32[16,128]{1,0:T(8,128)S(1)}, f32[16,128]{1,0:T(8,128)S(1)}, u32[]{:S(2)}, u32[]{:S(2)}) %collective-permute-start.3) | collective-permute-done | bytes 8224 | tf_op jit(solution)/shard_map/ppermute | solution.py:36
  28.1 4.8 %gram_kernel.1 = (f32[16,4096]{1,0:T(8,128)S(1)}, f32[64,128]{1,0:T(8,128)S(1)}, f32[48,128]{1,0:T(8,128)S(1)}, f32[48,128]{1,0:T(8,128)S(1)}) custom-call(s32[32,2]{1,0:T(8,128)S(1)} %copy.15.mask_ref, f32[32,3,128,128]{3,2,1,0:T(8,128)S(1)} %copy-done, f32[40,4096]{1,0:T(8,128)S(1)} %pad_maximum_fusion.fields_ref, ...), custom_call_target="tpu_custom_call" | custom-call | tf_op jit(solution)/shard_map/gram_kernel/pallas_call | solution.py:467
  32.8 0.0 copy-start.4
  32.8 0.7 copy-done.4
  33.5 11.3 %all_to_all.30 = f32[8,8,128]{2,1,0:T(8,128)S(1)} all-to-all(f32[8,8,128]{2,1,0:T(8,128)S(1)} %bitcast.15), channel_id=1, replica_groups=mesh['z'=16,'y'=4,'core'=2,'x'=4] {'y','core'}, dimensions={0} | all-to-all | bytes 65536 | tf_op jit(solution)/shard_map/all_to_all | solution.py:22
  44.8 27.3 %all_to_all.31 = f32[16,8,128]{2,1,0:T(8,128)S(1)} all-to-all(f32[16,8,128]{2,1,0:T(8,128)S(1)} %broadcast_in_dim.52), channel_id=1, replica_groups=mesh['z'=16,'y'=4,'core'=2,'x'=4] {'z'}, dimensions={0} | all-to-all | bytes 131072 | tf_op jit(solution)/shard_map/all_to_all | solution.py:24
  72.2 0.6 broadcast_in_dim.53
  72.8 5.4 %all-to-all-start.2 = ((f32[8,8,128]{2,1,0:T(8,128)}), f32[8,8,128]{2,1,0:T(8,128)S(1)}, u32[]{:S(2)}, u32[]{:S(2)}) async-start(f32[8,8,128]{2,1,0:T(8,128)} %broadcast_in_dim.53), calls=%async_computation.2 | async-start | bytes 65536 | tf_op jit(solution)/shard_map/all_to_all | solution.py:26
  78.2 3.5 %collective-permute-start.4 = (f32[48,128]{1,0:T(8,128)S(1)}, f32[48,128]{1,0:T(8,128)S(1)}, u32[]{:S(2)}, u32[]{:S(2)}) collective-permute-start(f32[48,128]{1,0:T(8,128)S(1)} %get-tuple-element.26), channel_id=1, source_target_pairs={{0,4},{4,8},{8,12},{12,16},{16,20},{20,24},{24,28},{28,32},{32,36}... | collective-permute-start | bytes 73736 | tf_op jit(solution)/shard_map/ppermute | solution.py:31
  81.8 1.9 %collective-permute-start.5 = (f32[48,128]{1,0:T(8,128)S(1)}, f32[48,128]{1,0:T(8,128)S(1)}, u32[]{:S(2)}, u32[]{:S(2)}) collective-permute-start(f32[48,128]{1,0:T(8,128)S(1)} %get-tuple-element.27), channel_id=1, source_target_pairs={{4,0},{8,4},{12,8},{16,12},{20,16},{24,20},{28,24},{32,28},{36,32}... | collective-permute-start | bytes 73736 | tf_op jit(solution)/shard_map/ppermute | solution.py:36
  83.7 0.0 all-to-all-done.2
  83.7 4.8 %first_kernel.1 = (f32[32,128]{1,0:T(8,128)S(1)}, f32[16,16]{1,0:T(8,128)S(1)}) custom-call(f32[64,128]{1,0:T(8,128)S(1)} %bitcast.14), custom_call_target="tpu_custom_call" | custom-call | tf_op jit(solution)/shard_map/first_kernel/pallas_call | solution.py:514
  88.5 0.0 collective-permute-done.4.rest_8_
  88.5 0.0 collective-permute-done.5.rest_11_
  88.6 0.0 copy-done.6
  88.6 0.0 copy-done.2
  88.6 0.0 copy-done.3
  88.6 0.0 copy-start.1
  88.6 2.8 %copy-done.1 = f32[32,3,128,128]{3,2,1,0:T(8,128)S(1)} copy-done((f32[32,3,128,128]{3,2,1,0:T(8,128)S(1)}, f32[32,3,128,128]{3,2,1,0:T(8,128)}, u32[]{:S(2)}) %copy-start.1) | copy-done | bytes 6291480
  91.4 0.0 copy-start.5
  91.4 0.9 copy-done.5
  92.3 5.4 %middle_kernel.1 = (f32[112,4096]{1,0:T(8,128)S(1)}, f32[16,4096]{1,0:T(8,128)S(1)}, f32[16,4096]{1,0:T(8,128)S(1)}, f32[64,4096]{1,0:T(8,128)S(1)}, f32[16,128]{1,0:T(8,128)S(1)}) custom-call(s32[32,2]{1,0:T(8,128)S(1)} %copy.15.mask_ref, f32[32,3,128,128]{3,2,1,0:T(8,128)S(1)} %copy-done.1, f32[32,128]{1,0:T(8,128)S(1)} %get-tuple-element.23.coeffs_ref, ...), custom_call_target="tpu_custom_call" | custom-call | tf_op jit(solution)/shard_map/middle_kernel/pallas_call | solution.py:467
  97.7 1.9 %collective-permute-start.6 = (f32[16,128]{1,0:T(8,128)S(1)}, f32[16,128]{1,0:T(8,128)S(1)}, u32[]{:S(2)}, u32[]{:S(2)}) collective-permute-start(f32[16,128]{1,0:T(8,128)S(1)} %get-tuple-element.32), channel_id=1, source_target_pairs={{4,0},{8,4},{12,8},{16,12},{20,16},{24,20},{28,24},{32,28},{36,32}... | collective-permute-start | bytes 24584 | tf_op jit(solution)/shard_map/ppermute | solution.py:36
  99.7 3.0 %collective-permute-done.6.right_ref = f32[16,128]{1,0:T(8,128)S(1)} collective-permute-done((f32[16,128]{1,0:T(8,128)S(1)}, f32[16,128]{1,0:T(8,128)S(1)}, u32[]{:S(2)}, u32[]{:S(2)}) %collective-permute-start.6) | collective-permute-done | bytes 8224 | tf_op jit(solution)/shard_map/ppermute | solution.py:36
  102.7 4.4 %pack_kernel.1 = f32[128,128]{1,0:T(8,128)S(1)} custom-call(s32[32,2]{1,0:T(8,128)S(1)} %copy.15.mask_ref, f32[32,3,128,128]{3,2,1,0:T(8,128)S(1)} %copy-done.1, f32[1,4096]{1,0:T(1,128)S(1)} %bitcast.13, f32[112,4096]{1,0:T(8,128)S(1)} %get-tuple-element.28.own_ref, f32[16,4096]{1,0:T(8,128)S(1)} %get-tuple-element.29.ar_ref, ...), custom_call_target="tpu_custom_call" | custom-call | tf_op jit(solution)/shard_map/pack_kernel/pallas_call | solution.py:467
  107.1 10.2 %all_to_all.32 = f32[8,16,128]{2,1,0:T(8,128)S(1)} all-to-all(f32[8,16,128]{2,1,0:T(8,128)S(1)} %bitcast.9), channel_id=1, replica_groups=mesh['z'=16,'y'=4,'core'=2,'x'=4] {'y','core'}, dimensions={0} | all-to-all | bytes 131072 | tf_op jit(solution)/shard_map/all_to_all | solution.py:22
  117.3 18.6 %all_to_all.33 = f32[16,16,128]{2,1,0:T(8,128)S(1)} all-to-all(f32[16,16,128]{2,1,0:T(8,128)S(1)} %broadcast_in_dim.54), channel_id=1, replica_groups=mesh['z'=16,'y'=4,'core'=2,'x'=4] {'z'}, dimensions={0} | all-to-all | bytes 262144 | tf_op jit(solution)/shard_map/all_to_all | solution.py:24
  135.9 11.0 %all_to_all.34 = f32[8,16,128]{2,1,0:T(8,128)S(1)} all-to-all(f32[8,16,128]{2,1,0:T(8,128)S(1)} %broadcast_in_dim.55), channel_id=1, replica_groups=mesh['z'=16,'y'=4,'core'=2,'x'=4] {'y','core'}, dimensions={0} | all-to-all | bytes 131072 | tf_op jit(solution)/shard_map/all_to_all | solution.py:26
  146.9 9.5 %last_kernel.1 = (f32[16,4096]{1,0:T(8,128)}, f32[16,4096]{1,0:T(8,128)}, f32[16,16]{1,0:T(8,128)}) custom-call(f32[128,128]{1,0:T(8,128)S(1)} %bitcast.10, f32[16,16]{1,0:T(8,128)S(1)} %get-tuple-element.24.ritz_ref, f32[112,4096]{1,0:T(8,128)S(1)} %get-tuple-element.28.own_ref, f32[16,4096]{1,0:T(8,128)S(1)} %get-tuple-element.29.ar_ref), custom_call_target="tpu_custom_call" | custom-call | tf_op jit(solution)/shard_map/last_kernel/pallas_call | solution.py:531
  (11 shorter events, 0.1 us)
Async XLA Ops:
  2.1 12.7 %collective-permute-start = (f32[40,128]{1,0:T(8,128)S(1)}, f32[40,128]{1,0:T(8,128)S(1)}, u32[]{:S(2)}, u32[]{:S(2)}) collective-permute-start(f32[40,128]{1,0:T(8,128)S(1)} %pad_maximum_fusion.1), channel_id=1, source_target_pairs={{0,4},{4,8},{8,12},{12,16},{16,20},{20,24},{24,28},{28,32},{32,36}... | collective-permute-start | bytes 61448 | tf_op jit(solution)/shard_map/ppermute | solution.py:31
  6.7 8.1 %collective-permute-start.1 = (f32[40,128]{1,0:T(8,128)S(1)}, f32[40,128]{1,0:T(8,128)S(1)}, u32[]{:S(2)}, u32[]{:S(2)}) collective-permute-start(f32[40,128]{1,0:T(8,128)S(1)} %pad_maximum_fusion.2), channel_id=1, source_target_pairs={{4,0},{8,4},{12,8},{16,12},{20,16},{24,20},{28,24},{32,28},{36,32}... | collective-permute-start | bytes 61448 | tf_op jit(solution)/shard_map/ppermute | solution.py:36
  14.0 74.6 %copy-start.6 = (f32[4096]{0:T(1024)S(1)}, f32[4096]{0:T(1024)}, u32[]{:S(2)}) copy-start(f32[4096]{0:T(1024)} %param.7) | copy-start | bytes 49156
  14.8 2.8 %copy-start = (f32[32,3,128,128]{3,2,1,0:T(8,128)S(1)}, f32[32,3,128,128]{3,2,1,0:T(8,128)}, u32[]{:S(2)}) copy-start(f32[32,3,128,128]{3,2,1,0:T(8,128)} %tiles_ref.7) | copy-start | bytes 18874372
  17.6 71.0 %copy-start.2 = (f32[16,4096]{1,0:T(8,128)S(1)}, f32[16,4096]{1,0:T(8,128)}, u32[]{:S(2)}) copy-start(f32[16,4096]{1,0:T(8,128)} %rest_1_.1) | copy-start | bytes 786436
  17.6 71.0 %copy-start.3 = (f32[16,4096]{1,0:T(8,128)S(1)}, f32[16,4096]{1,0:T(8,128)}, u32[]{:S(2)}) copy-start(f32[16,4096]{1,0:T(8,128)} %rest_0_.1) | copy-start | bytes 786436
  21.2 4.3 %collective-permute-start.2 = (f32[16,128]{1,0:T(8,128)S(1)}, f32[16,128]{1,0:T(8,128)S(1)}, u32[]{:S(2)}, u32[]{:S(2)}) collective-permute-start(f32[16,128]{1,0:T(8,128)S(1)} %get-tuple-element.20), channel_id=1, source_target_pairs={{0,4},{4,8},{8,12},{12,16},{16,20},{20,24},{24,28},{28,32},{32,36}... | collective-permute-start | bytes 24584 | tf_op jit(solution)/shard_map/ppermute | solution.py:31
  23.1 5.0 %collective-permute-start.3 = (f32[16,128]{1,0:T(8,128)S(1)}, f32[16,128]{1,0:T(8,128)S(1)}, u32[]{:S(2)}, u32[]{:S(2)}) collective-permute-start(f32[16,128]{1,0:T(8,128)S(1)} %get-tuple-element.21), channel_id=1, source_target_pairs={{4,0},{8,4},{12,8},{16,12},{20,16},{24,20},{28,24},{32,28},{36,32}... | collective-permute-start | bytes 24584 | tf_op jit(solution)/shard_map/ppermute | solution.py:36
  32.8 0.7 copy-start.4
  72.8 10.9 %all-to-all-start.2 = ((f32[8,8,128]{2,1,0:T(8,128)}), f32[8,8,128]{2,1,0:T(8,128)S(1)}, u32[]{:S(2)}, u32[]{:S(2)}) async-start(f32[8,8,128]{2,1,0:T(8,128)} %broadcast_in_dim.53), calls=%async_computation.2 | async-start | bytes 65536 | tf_op jit(solution)/shard_map/all_to_all | solution.py:26
  78.2 10.3 %collective-permute-start.4 = (f32[48,128]{1,0:T(8,128)S(1)}, f32[48,128]{1,0:T(8,128)S(1)}, u32[]{:S(2)}, u32[]{:S(2)}) collective-permute-start(f32[48,128]{1,0:T(8,128)S(1)} %get-tuple-element.26), channel_id=1, source_target_pairs={{0,4},{4,8},{8,12},{12,16},{16,20},{20,24},{24,28},{28,32},{32,36}... | collective-permute-start | bytes 73736 | tf_op jit(solution)/shard_map/ppermute | solution.py:31
  81.8 6.8 %collective-permute-start.5 = (f32[48,128]{1,0:T(8,128)S(1)}, f32[48,128]{1,0:T(8,128)S(1)}, u32[]{:S(2)}, u32[]{:S(2)}) collective-permute-start(f32[48,128]{1,0:T(8,128)S(1)} %get-tuple-element.27), channel_id=1, source_target_pairs={{4,0},{8,4},{12,8},{16,12},{20,16},{24,20},{28,24},{32,28},{36,32}... | collective-permute-start | bytes 73736 | tf_op jit(solution)/shard_map/ppermute | solution.py:36
  88.6 2.8 %copy-start.1 = (f32[32,3,128,128]{3,2,1,0:T(8,128)S(1)}, f32[32,3,128,128]{3,2,1,0:T(8,128)}, u32[]{:S(2)}) copy-start(f32[32,3,128,128]{3,2,1,0:T(8,128)} %tiles_ref.7) | copy-start | bytes 18874372
  91.4 0.9 copy-start.5
  97.7 5.0 %collective-permute-start.6 = (f32[16,128]{1,0:T(8,128)S(1)}, f32[16,128]{1,0:T(8,128)S(1)}, u32[]{:S(2)}, u32[]{:S(2)}) collective-permute-start(f32[16,128]{1,0:T(8,128)S(1)} %get-tuple-element.32), channel_id=1, source_target_pairs={{4,0},{8,4},{12,8},{16,12},{20,16},{24,20},{28,24},{32,28},{36,32}... | collective-permute-start | bytes 24584 | tf_op jit(solution)/shard_map/ppermute | solution.py:36

commit v5 on v4

--- a/solution.py
+++ b/solution.py
@@ -10,7 +10,7 @@
 
 SLAB = ("z", "y", "core")
 TILE = 128
-STEP_BLOCKS = 8
+STEP_BLOCKS = 16
 STEP = STEP_BLOCKS * TILE
 VMEM = 20 * 1024 * 1024
 WIDTH = 8

time: 157 us -> 155 us (0.987)
  Pallas kernels: 32.4 us -> 30.4 us
    pallas_call x4, Pallas kernels: 18.1 us -> 16.1 us  [on_blocks(): pl.pallas_call(kernel, grid=(tiles.shape[0] // STEP_BLOCKS,), in_specs=[p...]
where the time goes in v5:
time: 155 us; the launch traced here: 154 us
  blocking collectives  78.3 us (51%)
  Pallas kernels  30.4 us (20%)
  starting transfers between devices  27.2 us (18%)
  local copies, waits for them, and re-layouts  10.8 us (7%)
  waiting for transfers between devices  5.62 us (4%)
    all_to_all x2, blocking collectives, slab_sum(): own = lax.all_to_all(copies, 'z', 0, 0, tiled=True).sum(0)  45.9 us
    all_to_all x2, blocking collectives, slab_sum(): own = lax.all_to_all(shared, ('y', 'core'), 0, 0, tiled=True).sum(0)  21.4 us
    pallas_call x4, Pallas kernels, on_blocks(): pl.pallas_call(kernel, grid=(tiles.shape[0] // STEP_BLOCKS,), in_specs=[p...  16.1 us
    ppermute x4, starting transfers between devices, from_right(): return lax.ppermute(edge, SLAB, [(i + 1, i) for i in range(count - 1)])  11.7 us
    all_to_all x1, blocking collectives, slab_sum(): lax.all_to_all(copies, ('y', 'core'), 0, 0, tiled=True).reshape(rows.shape)  11 us
    ppermute x3, starting transfers between devices, from_left(): return lax.ppermute(edge, SLAB, [(i, i + 1) for i in range(count - 1)])  10 us
    pallas_call x1, Pallas kernels, on_device(): pl.pallas_call(functools.partial(last_kernel, total_rows), out_shape=(sha...  9.47 us
    unnamed x15, local copies, waits for them, and re-layouts  7.99 us
  transfers between devices with their start and end apart: 8, of which 2 were waited for; matrix products, arithmetic and copies ran while one was open for 2% of the time, Pallas kernels for 3%

profile of v5, /device:TPU:1, one launch (start us, length us, event | category | flops | bytes accessed | tf_op | source)
XLA Modules:
  0.0 154.3 jit_solution(13423583331438173097)
XLA Ops:
  0.6 0.7 slice_bitcast_fusion
  1.3 0.7 fusion
  2.1 4.6 %collective-permute-start = (f32[40,128]{1,0:T(8,128)S(1)}, f32[40,128]{1,0:T(8,128)S(1)}, u32[]{:S(2)}, u32[]{:S(2)}) collective-permute-start(f32[40,128]{1,0:T(8,128)S(1)} %pad_maximum_fusion.1), channel_id=1, source_target_pairs={{0,4},{4,8},{8,12},{12,16},{16,20},{20,24},{24,28},{28,32},{32,36}... | collective-permute-start | bytes 61448 | tf_op jit(solution)/shard_map/ppermute | solution.py:31
  6.7 5.5 %collective-permute-start.1 = (f32[40,128]{1,0:T(8,128)S(1)}, f32[40,128]{1,0:T(8,128)S(1)}, u32[]{:S(2)}, u32[]{:S(2)}) collective-permute-start(f32[40,128]{1,0:T(8,128)S(1)} %pad_maximum_fusion.2), channel_id=1, source_target_pairs={{4,0},{8,4},{12,8},{16,12},{20,16},{24,20},{28,24},{32,28},{36,32}... | collective-permute-start | bytes 61448 | tf_op jit(solution)/shard_map/ppermute | solution.py:36
  12.2 0.7 broadcast_in_dim.21
  12.9 1.1 pad_maximum_fusion.fields_ref
  14.0 0.0 copy-start.6
  14.0 0.8 copy.15.mask_ref
  14.8 0.0 collective-permute-done.left_ref.rest_6_
  14.8 0.0 collective-permute-done.1.right_ref.rest_9_
  14.8 0.0 copy-start
  14.8 2.8 %copy-done = f32[32,3,128,128]{3,2,1,0:T(8,128)S(1)} copy-done((f32[32,3,128,128]{3,2,1,0:T(8,128)S(1)}, f32[32,3,128,128]{3,2,1,0:T(8,128)}, u32[]{:S(2)}) %copy-start) | copy-done | bytes 6291480
  17.6 0.0 copy-start.2
  17.6 0.0 copy-start.3
  17.6 3.3 %start_kernel.1 = (f32[16,4096]{1,0:T(8,128)S(1)}, f32[32,4096]{1,0:T(8,128)S(1)}, f32[16,128]{1,0:T(8,128)S(1)}, f32[16,128]{1,0:T(8,128)S(1)}) custom-call(s32[32,2]{1,0:T(8,128)S(1)} %copy.15.mask_ref, f32[32,3,128,128]{3,2,1,0:T(8,128)S(1)} %copy-done, f32[40,4096]{1,0:T(8,128)S(1)} %pad_maximum_fusion.fields_ref, ...), custom_call_target="tpu_custom_call" | custom-call | tf_op jit(solution)/shard_map/start_kernel/pallas_call | solution.py:467
  20.9 1.9 %collective-permute-start.2 = (f32[16,128]{1,0:T(8,128)S(1)}, f32[16,128]{1,0:T(8,128)S(1)}, u32[]{:S(2)}, u32[]{:S(2)}) collective-permute-start(f32[16,128]{1,0:T(8,128)S(1)} %get-tuple-element.20), channel_id=1, source_target_pairs={{0,4},{4,8},{8,12},{12,16},{16,20},{20,24},{24,28},{28,32},{32,36}... | collective-permute-start | bytes 24584 | tf_op jit(solution)/shard_map/ppermute | solution.py:31
  22.8 2.4 %collective-permute-start.3 = (f32[16,128]{1,0:T(8,128)S(1)}, f32[16,128]{1,0:T(8,128)S(1)}, u32[]{:S(2)}, u32[]{:S(2)}) collective-permute-start(f32[16,128]{1,0:T(8,128)S(1)} %get-tuple-element.21), channel_id=1, source_target_pairs={{4,0},{8,4},{12,8},{16,12},{20,16},{24,20},{28,24},{32,28},{36,32}... | collective-permute-start | bytes 24584 | tf_op jit(solution)/shard_map/ppermute | solution.py:36
  25.2 0.0 collective-permute-done.2.rest_0_.rest_7_
  25.2 2.5 %collective-permute-done.3.rest_1_.rest_10_ = f32[16,128]{1,0:T(8,128)S(1)} collective-permute-done((f32[16,128]{1,0:T(8,128)S(1)}, f32[16,128]{1,0:T(8,128)S(1)}, u32[]{:S(2)}, u32[]{:S(2)}) %collective-permute-start.3) | collective-permute-done | bytes 8224 | tf_op jit(solution)/shard_map/ppermute | solution.py:36
  27.8 4.1 %gram_kernel.1 = (f32[16,4096]{1,0:T(8,128)S(1)}, f32[64,128]{1,0:T(8,128)S(1)}, f32[48,128]{1,0:T(8,128)S(1)}, f32[48,128]{1,0:T(8,128)S(1)}) custom-call(s32[32,2]{1,0:T(8,128)S(1)} %copy.15.mask_ref, f32[32,3,128,128]{3,2,1,0:T(8,128)S(1)} %copy-done, f32[40,4096]{1,0:T(8,128)S(1)} %pad_maximum_fusion.fields_ref, ...), custom_call_target="tpu_custom_call" | custom-call | tf_op jit(solution)/shard_map/gram_kernel/pallas_call | solution.py:467
  31.8 0.0 copy-start.4
  31.8 0.7 copy-done.4
  32.5 11.3 %all_to_all.30 = f32[8,8,128]{2,1,0:T(8,128)S(1)} all-to-all(f32[8,8,128]{2,1,0:T(8,128)S(1)} %bitcast.15), channel_id=1, replica_groups=mesh['z'=16,'y'=4,'core'=2,'x'=4] {'y','core'}, dimensions={0} | all-to-all | bytes 65536 | tf_op jit(solution)/shard_map/all_to_all | solution.py:22
  43.8 27.3 %all_to_all.31 = f32[16,8,128]{2,1,0:T(8,128)S(1)} all-to-all(f32[16,8,128]{2,1,0:T(8,128)S(1)} %broadcast_in_dim.52), channel_id=1, replica_groups=mesh['z'=16,'y'=4,'core'=2,'x'=4] {'z'}, dimensions={0} | all-to-all | bytes 131072 | tf_op jit(solution)/shard_map/all_to_all | solution.py:24
  71.2 0.6 broadcast_in_dim.53
  71.8 5.4 %all-to-all-start.2 = ((f32[8,8,128]{2,1,0:T(8,128)}), f32[8,8,128]{2,1,0:T(8,128)S(1)}, u32[]{:S(2)}, u32[]{:S(2)}) async-start(f32[8,8,128]{2,1,0:T(8,128)} %broadcast_in_dim.53), calls=%async_computation.2 | async-start | bytes 65536 | tf_op jit(solution)/shard_map/all_to_all | solution.py:26
  77.2 3.5 %collective-permute-start.4 = (f32[48,128]{1,0:T(8,128)S(1)}, f32[48,128]{1,0:T(8,128)S(1)}, u32[]{:S(2)}, u32[]{:S(2)}) collective-permute-start(f32[48,128]{1,0:T(8,128)S(1)} %get-tuple-element.26), channel_id=1, source_target_pairs={{0,4},{4,8},{8,12},{12,16},{16,20},{20,24},{24,28},{28,32},{32,36}... | collective-permute-start | bytes 73736 | tf_op jit(solution)/shard_map/ppermute | solution.py:31
  80.8 1.9 %collective-permute-start.5 = (f32[48,128]{1,0:T(8,128)S(1)}, f32[48,128]{1,0:T(8,128)S(1)}, u32[]{:S(2)}, u32[]{:S(2)}) collective-permute-start(f32[48,128]{1,0:T(8,128)S(1)} %get-tuple-element.27), channel_id=1, source_target_pairs={{4,0},{8,4},{12,8},{16,12},{20,16},{24,20},{28,24},{32,28},{36,32}... | collective-permute-start | bytes 73736 | tf_op jit(solution)/shard_map/ppermute | solution.py:36
  82.7 0.0 all-to-all-done.2
  82.7 4.8 %first_kernel.1 = (f32[32,128]{1,0:T(8,128)S(1)}, f32[16,16]{1,0:T(8,128)S(1)}) custom-call(f32[64,128]{1,0:T(8,128)S(1)} %bitcast.14), custom_call_target="tpu_custom_call" | custom-call | tf_op jit(solution)/shard_map/first_kernel/pallas_call | solution.py:514
  87.5 0.0 collective-permute-done.4.rest_8_
  87.5 0.0 collective-permute-done.5.rest_11_
  87.5 0.0 copy-done.6
  87.6 0.0 copy-done.2
  87.6 0.0 copy-done.3
  87.6 0.0 copy-start.1
  87.6 2.8 %copy-done.1 = f32[32,3,128,128]{3,2,1,0:T(8,128)S(1)} copy-done((f32[32,3,128,128]{3,2,1,0:T(8,128)S(1)}, f32[32,3,128,128]{3,2,1,0:T(8,128)}, u32[]{:S(2)}) %copy-start.1) | copy-done | bytes 6291480
  90.4 0.0 copy-start.5
  90.4 0.9 copy-done.5
  91.3 4.8 %middle_kernel.1 = (f32[112,4096]{1,0:T(8,128)S(1)}, f32[16,4096]{1,0:T(8,128)S(1)}, f32[16,4096]{1,0:T(8,128)S(1)}, f32[64,4096]{1,0:T(8,128)S(1)}, f32[16,128]{1,0:T(8,128)S(1)}) custom-call(s32[32,2]{1,0:T(8,128)S(1)} %copy.15.mask_ref, f32[32,3,128,128]{3,2,1,0:T(8,128)S(1)} %copy-done.1, f32[32,128]{1,0:T(8,128)S(1)} %get-tuple-element.23.coeffs_ref, ...), custom_call_target="tpu_custom_call" | custom-call | tf_op jit(solution)/shard_map/middle_kernel/pallas_call | solution.py:467
  96.1 1.9 %collective-permute-start.6 = (f32[16,128]{1,0:T(8,128)S(1)}, f32[16,128]{1,0:T(8,128)S(1)}, u32[]{:S(2)}, u32[]{:S(2)}) collective-permute-start(f32[16,128]{1,0:T(8,128)S(1)} %get-tuple-element.32), channel_id=1, source_target_pairs={{4,0},{8,4},{12,8},{16,12},{20,16},{24,20},{28,24},{32,28},{36,32}... | collective-permute-start | bytes 24584 | tf_op jit(solution)/shard_map/ppermute | solution.py:36
  98.0 3.1 %collective-permute-done.6.right_ref = f32[16,128]{1,0:T(8,128)S(1)} collective-permute-done((f32[16,128]{1,0:T(8,128)S(1)}, f32[16,128]{1,0:T(8,128)S(1)}, u32[]{:S(2)}, u32[]{:S(2)}) %collective-permute-start.6) | collective-permute-done | bytes 8224 | tf_op jit(solution)/shard_map/ppermute | solution.py:36
  101.1 4.0 %pack_kernel.1 = f32[128,128]{1,0:T(8,128)S(1)} custom-call(s32[32,2]{1,0:T(8,128)S(1)} %copy.15.mask_ref, f32[32,3,128,128]{3,2,1,0:T(8,128)S(1)} %copy-done.1, f32[1,4096]{1,0:T(1,128)S(1)} %bitcast.13, f32[112,4096]{1,0:T(8,128)S(1)} %get-tuple-element.28.own_ref, f32[16,4096]{1,0:T(8,128)S(1)} %get-tuple-element.29.ar_ref, ...), custom_call_target="tpu_custom_call" | custom-call | tf_op jit(solution)/shard_map/pack_kernel/pallas_call | solution.py:467
  105.1 10.2 %all_to_all.32 = f32[8,16,128]{2,1,0:T(8,128)S(1)} all-to-all(f32[8,16,128]{2,1,0:T(8,128)S(1)} %bitcast.9), channel_id=1, replica_groups=mesh['z'=16,'y'=4,'core'=2,'x'=4] {'y','core'}, dimensions={0} | all-to-all | bytes 131072 | tf_op jit(solution)/shard_map/all_to_all | solution.py:22
  115.2 18.6 %all_to_all.33 = f32[16,16,128]{2,1,0:T(8,128)S(1)} all-to-all(f32[16,16,128]{2,1,0:T(8,128)S(1)} %broadcast_in_dim.54), channel_id=1, replica_groups=mesh['z'=16,'y'=4,'core'=2,'x'=4] {'z'}, dimensions={0} | all-to-all | bytes 262144 | tf_op jit(solution)/shard_map/all_to_all | solution.py:24
  133.9 11.0 %all_to_all.34 = f32[8,16,128]{2,1,0:T(8,128)S(1)} all-to-all(f32[8,16,128]{2,1,0:T(8,128)S(1)} %broadcast_in_dim.55), channel_id=1, replica_groups=mesh['z'=16,'y'=4,'core'=2,'x'=4] {'y','core'}, dimensions={0} | all-to-all | bytes 131072 | tf_op jit(solution)/shard_map/all_to_all | solution.py:26
  144.8 9.5 %last_kernel.1 = (f32[16,4096]{1,0:T(8,128)}, f32[16,4096]{1,0:T(8,128)}, f32[16,16]{1,0:T(8,128)}) custom-call(f32[128,128]{1,0:T(8,128)S(1)} %bitcast.10, f32[16,16]{1,0:T(8,128)S(1)} %get-tuple-element.24.ritz_ref, f32[112,4096]{1,0:T(8,128)S(1)} %get-tuple-element.28.own_ref, f32[16,4096]{1,0:T(8,128)S(1)} %get-tuple-element.29.ar_ref), custom_call_target="tpu_custom_call" | custom-call | tf_op jit(solution)/shard_map/last_kernel/pallas_call | solution.py:531
  (11 shorter events, 0.1 us)
Async XLA Ops:
  2.1 12.7 %collective-permute-start = (f32[40,128]{1,0:T(8,128)S(1)}, f32[40,128]{1,0:T(8,128)S(1)}, u32[]{:S(2)}, u32[]{:S(2)}) collective-permute-start(f32[40,128]{1,0:T(8,128)S(1)} %pad_maximum_fusion.1), channel_id=1, source_target_pairs={{0,4},{4,8},{8,12},{12,16},{16,20},{20,24},{24,28},{28,32},{32,36}... | collective-permute-start | bytes 61448 | tf_op jit(solution)/shard_map/ppermute | solution.py:31
  6.7 8.1 %collective-permute-start.1 = (f32[40,128]{1,0:T(8,128)S(1)}, f32[40,128]{1,0:T(8,128)S(1)}, u32[]{:S(2)}, u32[]{:S(2)}) collective-permute-start(f32[40,128]{1,0:T(8,128)S(1)} %pad_maximum_fusion.2), channel_id=1, source_target_pairs={{4,0},{8,4},{12,8},{16,12},{20,16},{24,20},{28,24},{32,28},{36,32}... | collective-permute-start | bytes 61448 | tf_op jit(solution)/shard_map/ppermute | solution.py:36
  14.0 73.6 %copy-start.6 = (f32[4096]{0:T(1024)S(1)}, f32[4096]{0:T(1024)}, u32[]{:S(2)}) copy-start(f32[4096]{0:T(1024)} %param.7) | copy-start | bytes 49156
  14.8 2.8 %copy-start = (f32[32,3,128,128]{3,2,1,0:T(8,128)S(1)}, f32[32,3,128,128]{3,2,1,0:T(8,128)}, u32[]{:S(2)}) copy-start(f32[32,3,128,128]{3,2,1,0:T(8,128)} %tiles_ref.7) | copy-start | bytes 18874372
  17.6 70.0 %copy-start.2 = (f32[16,4096]{1,0:T(8,128)S(1)}, f32[16,4096]{1,0:T(8,128)}, u32[]{:S(2)}) copy-start(f32[16,4096]{1,0:T(8,128)} %rest_1_.1) | copy-start | bytes 786436
  17.6 70.0 %copy-start.3 = (f32[16,4096]{1,0:T(8,128)S(1)}, f32[16,4096]{1,0:T(8,128)}, u32[]{:S(2)}) copy-start(f32[16,4096]{1,0:T(8,128)} %rest_0_.1) | copy-start | bytes 786436
  20.9 4.3 %collective-permute-start.2 = (f32[16,128]{1,0:T(8,128)S(1)}, f32[16,128]{1,0:T(8,128)S(1)}, u32[]{:S(2)}, u32[]{:S(2)}) collective-permute-start(f32[16,128]{1,0:T(8,128)S(1)} %get-tuple-element.20), channel_id=1, source_target_pairs={{0,4},{4,8},{8,12},{12,16},{16,20},{20,24},{24,28},{28,32},{32,36}... | collective-permute-start | bytes 24584 | tf_op jit(solution)/shard_map/ppermute | solution.py:31
  22.8 5.0 %collective-permute-start.3 = (f32[16,128]{1,0:T(8,128)S(1)}, f32[16,128]{1,0:T(8,128)S(1)}, u32[]{:S(2)}, u32[]{:S(2)}) collective-permute-start(f32[16,128]{1,0:T(8,128)S(1)} %get-tuple-element.21), channel_id=1, source_target_pairs={{4,0},{8,4},{12,8},{16,12},{20,16},{24,20},{28,24},{32,28},{36,32}... | collective-permute-start | bytes 24584 | tf_op jit(solution)/shard_map/ppermute | solution.py:36
  31.8 0.7 copy-start.4
  71.8 10.9 %all-to-all-start.2 = ((f32[8,8,128]{2,1,0:T(8,128)}), f32[8,8,128]{2,1,0:T(8,128)S(1)}, u32[]{:S(2)}, u32[]{:S(2)}) async-start(f32[8,8,128]{2,1,0:T(8,128)} %broadcast_in_dim.53), calls=%async_computation.2 | async-start | bytes 65536 | tf_op jit(solution)/shard_map/all_to_all | solution.py:26
  77.2 10.3 %collective-permute-start.4 = (f32[48,128]{1,0:T(8,128)S(1)}, f32[48,128]{1,0:T(8,128)S(1)}, u32[]{:S(2)}, u32[]{:S(2)}) collective-permute-start(f32[48,128]{1,0:T(8,128)S(1)} %get-tuple-element.26), channel_id=1, source_target_pairs={{0,4},{4,8},{8,12},{12,16},{16,20},{20,24},{24,28},{28,32},{32,36}... | collective-permute-start | bytes 73736 | tf_op jit(solution)/shard_map/ppermute | solution.py:31
  80.8 6.8 %collective-permute-start.5 = (f32[48,128]{1,0:T(8,128)S(1)}, f32[48,128]{1,0:T(8,128)S(1)}, u32[]{:S(2)}, u32[]{:S(2)}) collective-permute-start(f32[48,128]{1,0:T(8,128)S(1)} %get-tuple-element.27), channel_id=1, source_target_pairs={{4,0},{8,4},{12,8},{16,12},{20,16},{24,20},{28,24},{32,28},{36,32}... | collective-permute-start | bytes 73736 | tf_op jit(solution)/shard_map/ppermute | solution.py:36
  87.6 2.8 %copy-start.1 = (f32[32,3,128,128]{3,2,1,0:T(8,128)S(1)}, f32[32,3,128,128]{3,2,1,0:T(8,128)}, u32[]{:S(2)}) copy-start(f32[32,3,128,128]{3,2,1,0:T(8,128)} %tiles_ref.7) | copy-start | bytes 18874372
  90.4 0.9 copy-start.5
  96.1 5.0 %collective-permute-start.6 = (f32[16,128]{1,0:T(8,128)S(1)}, f32[16,128]{1,0:T(8,128)S(1)}, u32[]{:S(2)}, u32[]{:S(2)}) collective-permute-start(f32[16,128]{1,0:T(8,128)S(1)} %get-tuple-element.32), channel_id=1, source_target_pairs={{4,0},{8,4},{12,8},{16,12},{20,16},{24,20},{28,24},{32,28},{36,32}... | collective-permute-start | bytes 24584 | tf_op jit(solution)/shard_map/ppermute | solution.py:36

commit v6 on v5

--- a/solution.py
+++ b/solution.py
@@ -10,7 +10,7 @@
 
 SLAB = ("z", "y", "core")
 TILE = 128
-STEP_BLOCKS = 16
+STEP_BLOCKS = 32
 STEP = STEP_BLOCKS * TILE
 VMEM = 20 * 1024 * 1024
 WIDTH = 8

time: 155 us -> 153 us (0.987)
  Pallas kernels: 30.4 us -> 28.6 us
    pallas_call x4, Pallas kernels: 16.1 us -> 14.2 us  [on_blocks(): pl.pallas_call(kernel, grid=(tiles.shape[0] // STEP_BLOCKS,), in_specs=[p...]
where the time goes in v6:
time: 153 us
  blocking collectives  78.4 us (51%)
  Pallas kernels  28.6 us (19%)
  starting transfers between devices  27.4 us (18%)
  local copies, waits for them, and re-layouts  10.8 us (7%)
  waiting for transfers between devices  5.43 us (4%)
    all_to_all x2, blocking collectives, slab_sum(): own = lax.all_to_all(copies, 'z', 0, 0, tiled=True).sum(0)  45.9 us
    all_to_all x2, blocking collectives, slab_sum(): own = lax.all_to_all(shared, ('y', 'core'), 0, 0, tiled=True).sum(0)  21.5 us
    pallas_call x4, Pallas kernels, on_blocks(): pl.pallas_call(kernel, grid=(tiles.shape[0] // STEP_BLOCKS,), in_specs=[p...  14.2 us
    ppermute x4, starting transfers between devices, from_right(): return lax.ppermute(edge, SLAB, [(i + 1, i) for i in range(count - 1)])  11.9 us
    all_to_all x1, blocking collectives, slab_sum(): lax.all_to_all(copies, ('y', 'core'), 0, 0, tiled=True).reshape(rows.shape)  11 us
    ppermute x3, starting transfers between devices, from_left(): return lax.ppermute(edge, SLAB, [(i, i + 1) for i in range(count - 1)])  10 us
    pallas_call x1, Pallas kernels, on_device(): pl.pallas_call(functools.partial(last_kernel, total_rows), out_shape=(sha...  9.53 us
    unnamed x15, local copies, waits for them, and re-layouts  7.99 us
  transfers between devices with their start and end apart: 8, of which 2 were waited for; matrix products, arithmetic and copies ran while one was open for 2% of the time, Pallas kernels for 3%

profile of v6, /device:TPU:1, one launch (start us, length us, event | category | flops | bytes accessed | tf_op | source)
XLA Modules:
  0.0 152.5 jit_solution(16520543567749085687)
XLA Ops:
  0.6 0.7 slice_bitcast_fusion
  1.3 0.7 fusion
  2.1 4.6 %collective-permute-start = (f32[40,128]{1,0:T(8,128)S(1)}, f32[40,128]{1,0:T(8,128)S(1)}, u32[]{:S(2)}, u32[]{:S(2)}) collective-permute-start(f32[40,128]{1,0:T(8,128)S(1)} %pad_maximum_fusion.1), channel_id=1, source_target_pairs={{0,4},{4,8},{8,12},{12,16},{16,20},{20,24},{24,28},{28,32},{32,36}... | collective-permute-start | bytes 61448 | tf_op jit(solution)/shard_map/ppermute | solution.py:31
  6.7 5.5 %collective-permute-start.1 = (f32[40,128]{1,0:T(8,128)S(1)}, f32[40,128]{1,0:T(8,128)S(1)}, u32[]{:S(2)}, u32[]{:S(2)}) collective-permute-start(f32[40,128]{1,0:T(8,128)S(1)} %pad_maximum_fusion.2), channel_id=1, source_target_pairs={{4,0},{8,4},{12,8},{16,12},{20,16},{24,20},{28,24},{32,28},{36,32}... | collective-permute-start | bytes 61448 | tf_op jit(solution)/shard_map/ppermute | solution.py:36
  12.2 0.7 broadcast_in_dim.21
  12.9 1.1 pad_maximum_fusion.fields_ref
  14.0 0.0 copy-start.6
  14.0 0.8 copy.15.mask_ref
  14.8 0.0 collective-permute-done.left_ref.rest_6_
  14.8 0.0 collective-permute-done.1.right_ref.rest_9_
  14.8 0.0 copy-start
  14.8 2.8 %copy-done = f32[32,3,128,128]{3,2,1,0:T(8,128)S(1)} copy-done((f32[32,3,128,128]{3,2,1,0:T(8,128)S(1)}, f32[32,3,128,128]{3,2,1,0:T(8,128)}, u32[]{:S(2)}) %copy-start) | copy-done | bytes 6291480
  17.6 0.0 copy-start.2
  17.6 0.0 copy-start.3
  17.6 2.9 %start_kernel.1 = (f32[16,4096]{1,0:T(8,128)S(1)}, f32[32,4096]{1,0:T(8,128)S(1)}, f32[16,128]{1,0:T(8,128)S(1)}, f32[16,128]{1,0:T(8,128)S(1)}) custom-call(s32[32,2]{1,0:T(8,128)S(1)} %copy.15.mask_ref, f32[32,3,128,128]{3,2,1,0:T(8,128)S(1)} %copy-done, f32[40,4096]{1,0:T(8,128)S(1)} %pad_maximum_fusion.fields_ref, ...), custom_call_target="tpu_custom_call" | custom-call | tf_op jit(solution)/shard_map/start_kernel/pallas_call | solution.py:467
  20.5 1.9 %collective-permute-start.2 = (f32[16,128]{1,0:T(8,128)S(1)}, f32[16,128]{1,0:T(8,128)S(1)}, u32[]{:S(2)}, u32[]{:S(2)}) collective-permute-start(f32[16,128]{1,0:T(8,128)S(1)} %get-tuple-element.20), channel_id=1, source_target_pairs={{0,4},{4,8},{8,12},{12,16},{16,20},{20,24},{24,28},{28,32},{32,36}... | collective-permute-start | bytes 24584 | tf_op jit(solution)/shard_map/ppermute | solution.py:31
  22.4 2.4 %collective-permute-start.3 = (f32[16,128]{1,0:T(8,128)S(1)}, f32[16,128]{1,0:T(8,128)S(1)}, u32[]{:S(2)}, u32[]{:S(2)}) collective-permute-start(f32[16,128]{1,0:T(8,128)S(1)} %get-tuple-element.21), channel_id=1, source_target_pairs={{4,0},{8,4},{12,8},{16,12},{20,16},{24,20},{28,24},{32,28},{36,32}... | collective-permute-start | bytes 24584 | tf_op jit(solution)/shard_map/ppermute | solution.py:36
  24.8 0.0 collective-permute-done.2.rest_0_.rest_7_
  24.8 2.5 %collective-permute-done.3.rest_1_.rest_10_ = f32[16,128]{1,0:T(8,128)S(1)} collective-permute-done((f32[16,128]{1,0:T(8,128)S(1)}, f32[16,128]{1,0:T(8,128)S(1)}, u32[]{:S(2)}, u32[]{:S(2)}) %collective-permute-start.3) | collective-permute-done | bytes 8224 | tf_op jit(solution)/shard_map/ppermute | solution.py:36
  27.4 3.6 %gram_kernel.1 = (f32[16,4096]{1,0:T(8,128)S(1)}, f32[64,128]{1,0:T(8,128)S(1)}, f32[48,128]{1,0:T(8,128)S(1)}, f32[48,128]{1,0:T(8,128)S(1)}) custom-call(s32[32,2]{1,0:T(8,128)S(1)} %copy.15.mask_ref, f32[32,3,128,128]{3,2,1,0:T(8,128)S(1)} %copy-done, f32[40,4096]{1,0:T(8,128)S(1)} %pad_maximum_fusion.fields_ref, ...), custom_call_target="tpu_custom_call" | custom-call | tf_op jit(solution)/shard_map/gram_kernel/pallas_call | solution.py:467
  31.0 0.0 copy-start.4
  31.0 0.7 copy-done.4
  31.7 11.3 %all_to_all.30 = f32[8,8,128]{2,1,0:T(8,128)S(1)} all-to-all(f32[8,8,128]{2,1,0:T(8,128)S(1)} %bitcast.15), channel_id=1, replica_groups=mesh['z'=16,'y'=4,'core'=2,'x'=4] {'y','core'}, dimensions={0} | all-to-all | bytes 65536 | tf_op jit(solution)/shard_map/all_to_all | solution.py:22
  43.0 27.3 %all_to_all.31 = f32[16,8,128]{2,1,0:T(8,128)S(1)} all-to-all(f32[16,8,128]{2,1,0:T(8,128)S(1)} %broadcast_in_dim.52), channel_id=1, replica_groups=mesh['z'=16,'y'=4,'core'=2,'x'=4] {'z'}, dimensions={0} | all-to-all | bytes 131072 | tf_op jit(solution)/shard_map/all_to_all | solution.py:24
  70.4 0.6 broadcast_in_dim.53
  71.0 5.4 %all-to-all-start.2 = ((f32[8,8,128]{2,1,0:T(8,128)}), f32[8,8,128]{2,1,0:T(8,128)S(1)}, u32[]{:S(2)}, u32[]{:S(2)}) async-start(f32[8,8,128]{2,1,0:T(8,128)} %broadcast_in_dim.53), calls=%async_computation.2 | async-start | bytes 65536 | tf_op jit(solution)/shard_map/all_to_all | solution.py:26
  76.4 3.5 %collective-permute-start.4 = (f32[48,128]{1,0:T(8,128)S(1)}, f32[48,128]{1,0:T(8,128)S(1)}, u32[]{:S(2)}, u32[]{:S(2)}) collective-permute-start(f32[48,128]{1,0:T(8,128)S(1)} %get-tuple-element.26), channel_id=1, source_target_pairs={{0,4},{4,8},{8,12},{12,16},{16,20},{20,24},{24,28},{28,32},{32,36}... | collective-permute-start | bytes 73736 | tf_op jit(solution)/shard_map/ppermute | solution.py:31
  80.0 1.9 %collective-permute-start.5 = (f32[48,128]{1,0:T(8,128)S(1)}, f32[48,128]{1,0:T(8,128)S(1)}, u32[]{:S(2)}, u32[]{:S(2)}) collective-permute-start(f32[48,128]{1,0:T(8,128)S(1)} %get-tuple-element.27), channel_id=1, source_target_pairs={{4,0},{8,4},{12,8},{16,12},{20,16},{24,20},{28,24},{32,28},{36,32}... | collective-permute-start | bytes 73736 | tf_op jit(solution)/shard_map/ppermute | solution.py:36
  81.9 0.0 all-to-all-done.2
  81.9 4.8 %first_kernel.1 = (f32[32,128]{1,0:T(8,128)S(1)}, f32[16,16]{1,0:T(8,128)S(1)}) custom-call(f32[64,128]{1,0:T(8,128)S(1)} %bitcast.14), custom_call_target="tpu_custom_call" | custom-call | tf_op jit(solution)/shard_map/first_kernel/pallas_call | solution.py:514
  86.7 0.0 collective-permute-done.4.rest_8_
  86.7 0.0 collective-permute-done.5.rest_11_
  86.7 0.0 copy-done.6
  86.7 0.0 copy-done.2
  86.7 0.0 copy-done.3
  86.8 0.0 copy-start.1
  86.8 2.8 %copy-done.1 = f32[32,3,128,128]{3,2,1,0:T(8,128)S(1)} copy-done((f32[32,3,128,128]{3,2,1,0:T(8,128)S(1)}, f32[32,3,128,128]{3,2,1,0:T(8,128)}, u32[]{:S(2)}) %copy-start.1) | copy-done | bytes 6291480
  89.5 0.0 copy-start.5
  89.5 0.9 copy-done.5
  90.5 4.1 %middle_kernel.1 = (f32[112,4096]{1,0:T(8,128)S(1)}, f32[16,4096]{1,0:T(8,128)S(1)}, f32[16,4096]{1,0:T(8,128)S(1)}, f32[64,4096]{1,0:T(8,128)S(1)}, f32[16,128]{1,0:T(8,128)S(1)}) custom-call(s32[32,2]{1,0:T(8,128)S(1)} %copy.15.mask_ref, f32[32,3,128,128]{3,2,1,0:T(8,128)S(1)} %copy-done.1, f32[32,128]{1,0:T(8,128)S(1)} %get-tuple-element.23.coeffs_ref, ...), custom_call_target="tpu_custom_call" | custom-call | tf_op jit(solution)/shard_map/middle_kernel/pallas_call | solution.py:467
  94.6 2.1 %collective-permute-start.6 = (f32[16,128]{1,0:T(8,128)S(1)}, f32[16,128]{1,0:T(8,128)S(1)}, u32[]{:S(2)}, u32[]{:S(2)}) collective-permute-start(f32[16,128]{1,0:T(8,128)S(1)} %get-tuple-element.32), channel_id=1, source_target_pairs={{4,0},{8,4},{12,8},{16,12},{20,16},{24,20},{28,24},{32,28},{36,32}... | collective-permute-start | bytes 24584 | tf_op jit(solution)/shard_map/ppermute | solution.py:36
  96.7 2.9 %collective-permute-done.6.right_ref = f32[16,128]{1,0:T(8,128)S(1)} collective-permute-done((f32[16,128]{1,0:T(8,128)S(1)}, f32[16,128]{1,0:T(8,128)S(1)}, u32[]{:S(2)}, u32[]{:S(2)}) %collective-permute-start.6) | collective-permute-done | bytes 8224 | tf_op jit(solution)/shard_map/ppermute | solution.py:36
  99.6 3.6 %pack_kernel.1 = f32[128,128]{1,0:T(8,128)S(1)} custom-call(s32[32,2]{1,0:T(8,128)S(1)} %copy.15.mask_ref, f32[32,3,128,128]{3,2,1,0:T(8,128)S(1)} %copy-done.1, f32[1,4096]{1,0:T(1,128)S(1)} %bitcast.13, f32[112,4096]{1,0:T(8,128)S(1)} %get-tuple-element.28.own_ref, f32[16,4096]{1,0:T(8,128)S(1)} %get-tuple-element.29.ar_ref, ...), custom_call_target="tpu_custom_call" | custom-call | tf_op jit(solution)/shard_map/pack_kernel/pallas_call | solution.py:467
  103.2 10.2 %all_to_all.32 = f32[8,16,128]{2,1,0:T(8,128)S(1)} all-to-all(f32[8,16,128]{2,1,0:T(8,128)S(1)} %bitcast.9), channel_id=1, replica_groups=mesh['z'=16,'y'=4,'core'=2,'x'=4] {'y','core'}, dimensions={0} | all-to-all | bytes 131072 | tf_op jit(solution)/shard_map/all_to_all | solution.py:22
  113.4 18.6 %all_to_all.33 = f32[16,16,128]{2,1,0:T(8,128)S(1)} all-to-all(f32[16,16,128]{2,1,0:T(8,128)S(1)} %broadcast_in_dim.54), channel_id=1, replica_groups=mesh['z'=16,'y'=4,'core'=2,'x'=4] {'z'}, dimensions={0} | all-to-all | bytes 262144 | tf_op jit(solution)/shard_map/all_to_all | solution.py:24
  132.0 11.0 %all_to_all.34 = f32[8,16,128]{2,1,0:T(8,128)S(1)} all-to-all(f32[8,16,128]{2,1,0:T(8,128)S(1)} %broadcast_in_dim.55), channel_id=1, replica_groups=mesh['z'=16,'y'=4,'core'=2,'x'=4] {'y','core'}, dimensions={0} | all-to-all | bytes 131072 | tf_op jit(solution)/shard_map/all_to_all | solution.py:26
  143.0 9.5 %last_kernel.1 = (f32[16,4096]{1,0:T(8,128)}, f32[16,4096]{1,0:T(8,128)}, f32[16,16]{1,0:T(8,128)}) custom-call(f32[128,128]{1,0:T(8,128)S(1)} %bitcast.10, f32[16,16]{1,0:T(8,128)S(1)} %get-tuple-element.24.ritz_ref, f32[112,4096]{1,0:T(8,128)S(1)} %get-tuple-element.28.own_ref, f32[16,4096]{1,0:T(8,128)S(1)} %get-tuple-element.29.ar_ref), custom_call_target="tpu_custom_call" | custom-call | tf_op jit(solution)/shard_map/last_kernel/pallas_call | solution.py:531
  (11 shorter events, 0.1 us)
Async XLA Ops:
  2.1 12.7 %collective-permute-start = (f32[40,128]{1,0:T(8,128)S(1)}, f32[40,128]{1,0:T(8,128)S(1)}, u32[]{:S(2)}, u32[]{:S(2)}) collective-permute-start(f32[40,128]{1,0:T(8,128)S(1)} %pad_maximum_fusion.1), channel_id=1, source_target_pairs={{0,4},{4,8},{8,12},{12,16},{16,20},{20,24},{24,28},{28,32},{32,36}... | collective-permute-start | bytes 61448 | tf_op jit(solution)/shard_map/ppermute | solution.py:31
  6.7 8.1 %collective-permute-start.1 = (f32[40,128]{1,0:T(8,128)S(1)}, f32[40,128]{1,0:T(8,128)S(1)}, u32[]{:S(2)}, u32[]{:S(2)}) collective-permute-start(f32[40,128]{1,0:T(8,128)S(1)} %pad_maximum_fusion.2), channel_id=1, source_target_pairs={{4,0},{8,4},{12,8},{16,12},{20,16},{24,20},{28,24},{32,28},{36,32}... | collective-permute-start | bytes 61448 | tf_op jit(solution)/shard_map/ppermute | solution.py:36
  14.0 72.7 %copy-start.6 = (f32[4096]{0:T(1024)S(1)}, f32[4096]{0:T(1024)}, u32[]{:S(2)}) copy-start(f32[4096]{0:T(1024)} %param.7) | copy-start | bytes 49156
  14.8 2.8 %copy-start = (f32[32,3,128,128]{3,2,1,0:T(8,128)S(1)}, f32[32,3,128,128]{3,2,1,0:T(8,128)}, u32[]{:S(2)}) copy-start(f32[32,3,128,128]{3,2,1,0:T(8,128)} %tiles_ref.7) | copy-start | bytes 18874372
  17.6 69.2 %copy-start.2 = (f32[16,4096]{1,0:T(8,128)S(1)}, f32[16,4096]{1,0:T(8,128)}, u32[]{:S(2)}) copy-start(f32[16,4096]{1,0:T(8,128)} %rest_1_.1) | copy-start | bytes 786436
  17.6 69.2 %copy-start.3 = (f32[16,4096]{1,0:T(8,128)S(1)}, f32[16,4096]{1,0:T(8,128)}, u32[]{:S(2)}) copy-start(f32[16,4096]{1,0:T(8,128)} %rest_0_.1) | copy-start | bytes 786436
  20.5 4.3 %collective-permute-start.2 = (f32[16,128]{1,0:T(8,128)S(1)}, f32[16,128]{1,0:T(8,128)S(1)}, u32[]{:S(2)}, u32[]{:S(2)}) collective-permute-start(f32[16,128]{1,0:T(8,128)S(1)} %get-tuple-element.20), channel_id=1, source_target_pairs={{0,4},{4,8},{8,12},{12,16},{16,20},{20,24},{24,28},{28,32},{32,36}... | collective-permute-start | bytes 24584 | tf_op jit(solution)/shard_map/ppermute | solution.py:31
  22.4 5.0 %collective-permute-start.3 = (f32[16,128]{1,0:T(8,128)S(1)}, f32[16,128]{1,0:T(8,128)S(1)}, u32[]{:S(2)}, u32[]{:S(2)}) collective-permute-start(f32[16,128]{1,0:T(8,128)S(1)} %get-tuple-element.21), channel_id=1, source_target_pairs={{4,0},{8,4},{12,8},{16,12},{20,16},{24,20},{28,24},{32,28},{36,32}... | collective-permute-start | bytes 24584 | tf_op jit(solution)/shard_map/ppermute | solution.py:36
  31.0 0.7 copy-start.4
  71.0 10.9 %all-to-all-start.2 = ((f32[8,8,128]{2,1,0:T(8,128)}), f32[8,8,128]{2,1,0:T(8,128)S(1)}, u32[]{:S(2)}, u32[]{:S(2)}) async-start(f32[8,8,128]{2,1,0:T(8,128)} %broadcast_in_dim.53), calls=%async_computation.2 | async-start | bytes 65536 | tf_op jit(solution)/shard_map/all_to_all | solution.py:26
  76.4 10.3 %collective-permute-start.4 = (f32[48,128]{1,0:T(8,128)S(1)}, f32[48,128]{1,0:T(8,128)S(1)}, u32[]{:S(2)}, u32[]{:S(2)}) collective-permute-start(f32[48,128]{1,0:T(8,128)S(1)} %get-tuple-element.26), channel_id=1, source_target_pairs={{0,4},{4,8},{8,12},{12,16},{16,20},{20,24},{24,28},{28,32},{32,36}... | collective-permute-start | bytes 73736 | tf_op jit(solution)/shard_map/ppermute | solution.py:31
  80.0 6.8 %collective-permute-start.5 = (f32[48,128]{1,0:T(8,128)S(1)}, f32[48,128]{1,0:T(8,128)S(1)}, u32[]{:S(2)}, u32[]{:S(2)}) collective-permute-start(f32[48,128]{1,0:T(8,128)S(1)} %get-tuple-element.27), channel_id=1, source_target_pairs={{4,0},{8,4},{12,8},{16,12},{20,16},{24,20},{28,24},{32,28},{36,32}... | collective-permute-start | bytes 73736 | tf_op jit(solution)/shard_map/ppermute | solution.py:36
  86.8 2.8 %copy-start.1 = (f32[32,3,128,128]{3,2,1,0:T(8,128)S(1)}, f32[32,3,128,128]{3,2,1,0:T(8,128)}, u32[]{:S(2)}) copy-start(f32[32,3,128,128]{3,2,1,0:T(8,128)} %tiles_ref.7) | copy-start | bytes 18874372
  89.5 0.9 copy-start.5
  94.6 5.0 %collective-permute-start.6 = (f32[16,128]{1,0:T(8,128)S(1)}, f32[16,128]{1,0:T(8,128)S(1)}, u32[]{:S(2)}, u32[]{:S(2)}) collective-permute-start(f32[16,128]{1,0:T(8,128)S(1)} %get-tuple-element.32), channel_id=1, source_target_pairs={{4,0},{8,4},{12,8},{16,12},{20,16},{24,20},{28,24},{32,28},{36,32}... | collective-permute-start | bytes 24584 | tf_op jit(solution)/shard_map/ppermute | solution.py:36
